TPU v7x, 256 devices: a whole 4x4x8 slice. The times are simulated.
256 devices in a mesh: ctx: 64 (over y, z, core), fsdp: 4 (over x).
Axes of the slice: x: 4, y: 4, z: 8, core: 2. Of those that a mesh axis runs over, the one named last changes fastest.
Arguments:
- hidden_rows: bfloat16 [8192, 2048], P('ctx', 'fsdp'), may hold values from -18 to 18
- w_qkv: bfloat16 [2048, 3072], P(None, 'fsdp'), may hold values from -4 to 4
- doc_lengths: int32 [8], replicated, may hold values from 1 to 4096, 8192 in all
- owners: int32 [8192], replicated, may hold values from 0 to 63, as said below
- context_grad: bfloat16 [8192, 2048], P('ctx', 'fsdp'), may hold values from -6 to 6
Outputs:
- context: bfloat16 [8192, 2048], P('ctx', 'fsdp')
- input_grad: float32 [8192, 2048], P('ctx', 'fsdp')
- weight_grad: float32 [2048, 3072], P('ctx', 'fsdp')
Inputs may be any that keep to these rules, and one draw needn't show every extreme that they name: `owners`: each index of ctx owns exactly 128 rows. Of the 128 rows of one index of ctx, at most 4 go to any one owner, and in every draw some index sends exactly 4 rows to one owner. `doc_lengths`: 8 documents fill the 8192 rows; the longest has exactly 4096 tokens.
All inputs are finite; a program needn't handle non-finite values.
Results may differ from a plain program's by a relative error of at most 0.02.
Values may be sent and summed in bfloat16 or wider, within the bound.
No kernel may reach another device: no remote copies, remote signals or barrier semaphores. Data moves between devices by JAX's collectives and lax.ppermute only.
A program may use at most 128 MiB of HBM per device.

v0:
```python
import functools

import jax
import jax.numpy as jnp
from jax import lax
from jax.experimental import pallas as pl
from jax.experimental.pallas import tpu as pltpu
from jax.sharding import PartitionSpec as P

HD = 128
GROUP = 4
TOK = 128
NY, NZ, NC = 4, 8, 2
N_CTX = NY * NZ * NC
NX = 4
CAP = 4
SLOTS = N_CTX * CAP
VISITS = 3
KEPT = (0, 3, 5)
FROM_BELOW = (1, 4, 6)
FROM_ABOVE = (7, 2)
QW = GROUP * TOK
epsilon = 1e-05
rope_base = 500000.0
scale = HD ** (-0.5)
log2e = 1.4426950408889634
masked = -1e30

f32, bf16, i32 = jnp.float32, jnp.bfloat16, jnp.int32

NT = (((1,), (1,)), ((), ()))
NN = (((1,), (0,)), ((), ()))
TN = (((0,), (0,)), ((), ()))


def dot(a, b, dims=NN):
    return lax.dot_general(a, b, dims, preferred_element_type=f32)


def call(kernel, outs, in_kinds, args, scratch=(), flops=10**8, moved=2 * 10**6, name=None):
    vm = pl.BlockSpec(memory_space=pltpu.VMEM)
    sm = pl.BlockSpec(memory_space=pltpu.SMEM)
    return pl.pallas_call(
        kernel,
        out_shape=[jax.ShapeDtypeStruct(s, d) for s, d in outs],
        in_specs=[sm if k == "s" else vm for k in in_kinds],
        out_specs=[vm] * len(outs),
        scratch_shapes=list(scratch),
        compiler_params=pltpu.CompilerParams(vmem_limit_bytes=48 * 1024 * 1024),
        cost_estimate=pl.CostEstimate(flops=flops, bytes_accessed=moved, transcendentals=0),
        name=name,
    )(*args)


def route_kernel(sc, owners, cg, mo_ref, mh_ref, send_ref):
    me = sc[0]
    mine = (owners[...] == me).astype(f32).astype(bf16)
    count = dot(mine, jnp.ones((TOK, TOK), bf16)).astype(bf16)
    slot_src = lax.broadcasted_iota(i32, (SLOTS, N_CTX), 0) // CAP
    source = lax.broadcasted_iota(i32, (SLOTS, N_CTX), 1)
    base = dot((source < slot_src).astype(f32).astype(bf16), count)
    here = dot((source == slot_src).astype(f32).astype(bf16), count)
    slot = lax.broadcasted_iota(i32, (SLOTS, TOK), 0)
    place = lax.broadcasted_iota(i32, (SLOTS, TOK), 1)
    rank = (slot % CAP).astype(f32)
    mo = jnp.where((base + rank == place.astype(f32)) & (rank < here), 1.0, 0.0).astype(bf16)
    mo_ref[...] = mo
    send_ref[...] = dot(mo, cg[...]).astype(bf16)
    own = jnp.broadcast_to(owners[pl.ds(me, 1), :].astype(f32), (TOK, TOK))
    earlier = lax.broadcasted_iota(i32, (TOK, TOK), 0) < lax.broadcasted_iota(i32, (TOK, TOK), 1)
    same = jnp.where((own == own.T) & earlier, 1.0, 0.0)
    home_slot = own[0:1, :] * CAP + jnp.sum(same, axis=0, keepdims=True)
    mh_ref[...] = jnp.where(slot.astype(f32) == home_slot, 1.0, 0.0).astype(bf16)


def grad_home_kernel(mh, arrived, out_ref):
    rows = dot(mh[...], arrived[...], TN).astype(bf16)
    for h in range(GROUP):
        out_ref[h * TOK : (h + 1) * TOK, :] = rows[:, h * HD : (h + 1) * HD]


def place_kernel(mo, arrived, out_ref):
    out_ref[...] = dot(mo[...], arrived[...], TN).astype(bf16)


def turn(t, c, s):
    return t * c + pltpu.roll(t, HD // 2, 1) * s


def turn_back(t, c, s):
    return t * c - pltpu.roll(t, HD // 2, 1) * s


def project_kernel(sc, h0, h1, h2, h3, w, cos, sin, q_ref, kv_ref, n0, n1, n2, n3, inv_ref, held):
    y, x = sc[1], sc[4]
    blocks = [h[...].astype(f32) for h in (h0, h1, h2, h3)]
    square = sum(jnp.sum(b * b, axis=1, keepdims=True) for b in blocks)
    inv = lax.rsqrt(square * (1.0 / (NX * 512)) + epsilon)
    inv_ref[...] = jnp.broadcast_to(inv, (TOK, HD))
    total = jnp.zeros((TOK, 768), f32)
    for s in range(NX):
        chunk = (x + NX - s) % NX
        normed = (blocks[s] * inv).astype(bf16)
        held[chunk] = normed
        total = total + dot(normed, w[pl.ds(pl.multiple_of(chunk * 512, 512), 512), :])
    for t, out in enumerate((n0, n1, n2, n3)):
        out[...] = held[(y + t) % NX]
    c, s = cos[...], sin[...]
    for h in range(GROUP):
        q_ref[h * TOK : (h + 1) * TOK, :] = turn(total[:, h * HD : (h + 1) * HD], c, s).astype(bf16)
    kv_ref[0:TOK, :] = turn(total[:, 512:640], c, s).astype(bf16)
    kv_ref[TOK:, :] = total[:, 640:768].astype(bf16)


def block_start(sc, row):
    start, begin = 0, sc[8]
    for d in range(1, 8):
        start = jnp.where(begin <= row, begin, start)
        begin = begin + sc[8 + d]
    return start


def query_rows(sc, visit):
    first = ((sc[1] + visit) * NZ * NC + sc[2] * NC + sc[3]) * TOK
    rows = first + lax.broadcasted_iota(i32, (1, QW), 1) % TOK
    starts, begin = jnp.zeros((1, QW), i32), sc[8]
    for d in range(1, 8):
        starts = jnp.where(rows >= begin, begin, starts)
        begin = begin + sc[8 + d]
    return first, rows, starts


def key_tile(sc, s):
    return sc[1] * NZ + (sc[2] + NZ - s) % NZ


def tile_needed(sc, visit, s):
    pair = key_tile(sc, s)
    first = ((sc[1] + visit) * NZ * NC + sc[2] * NC + sc[3]) * TOK
    live = (sc[1] + visit < NY) & (pair <= (sc[1] + visit) * NZ + sc[2])
    return live & (pair * 256 + 255 >= block_start(sc, first))


def load_keys(kvs, keys, values):
    for e in range(NC):
        for stack, steps in zip(kvs[3 * e : 3 * e + 3], (KEPT, FROM_BELOW, FROM_ABOVE)):
            for i, s in enumerate(steps):
                keys[s, e * TOK : (e + 1) * TOK, :] = stack[i, 0:TOK, :]
                values[s, e * TOK : (e + 1) * TOK, :] = stack[i, TOK:, :]


def pack_kernel(b0, b3, b5, three_ref, two_ref):
    for i, b in enumerate((b0, b3, b5)):
        three_ref[i] = b[...]
        if i < 2:
            two_ref[i] = b[...]


def tile_mask(sc, s, rows, starts):
    offset = lax.broadcasted_iota(i32, (2 * TOK, QW), 0) ^ (sc[3] * TOK)
    key_rows = key_tile(sc, s) * 256 + offset
    return (key_rows >= starts) & (key_rows <= rows)


def forward_kernel(sc, *refs):
    qs, dos, kvs = refs[0:3], refs[3:6], refs[6:12]
    outs, stats = refs[12:15], refs[15]
    keys, values, acc, top, total = refs[16:]
    load_keys(kvs, keys, values)
    stats[...] = jnp.zeros_like(stats)
    for visit in range(VISITS):
        q_ref = qs[visit]
        _, rows, starts = query_rows(sc, visit)
        acc[...] = jnp.zeros_like(acc)
        total[...] = jnp.zeros_like(total)
        top[...] = jnp.full_like(top, masked)

        @pl.loop(0, NZ)
        def _(s):
            @pl.when(tile_needed(sc, visit, s))
            def _():
                scores = dot(keys[s], q_ref[...], NT) * (scale * log2e)
                scores = jnp.where(tile_mask(sc, s, rows, starts), scores, masked)
                old = top[...]
                new = jnp.maximum(old, jnp.max(scores, axis=0, keepdims=True))
                base = jnp.maximum(new, 0.1 * masked)
                p = jnp.exp2(scores - base)
                fade = jnp.exp2(old - base)
                top[...] = new
                total[...] = total[...] * fade + jnp.sum(p, axis=0, keepdims=True)
                acc[...] = acc[...] * fade + dot(values[s], p.astype(bf16), TN)

        mass = total[...]
        some = mass > 0.0
        mass = jnp.where(some, mass, 1.0)
        out = acc[...] * (1.0 / mass)
        outs[visit][...] = out.astype(bf16)
        stats[visit : visit + 1, :] = jnp.where(some, top[...] + jnp.log2(mass), masked)
        delta = jnp.sum(dos[visit][...].astype(f32).T * out, axis=0, keepdims=True)
        stats[4 + visit : 5 + visit, :] = delta


def combine_stats(sc, visit, held):
    logs, deltas = [], []
    for j in range(VISITS):
        t = visit - j
        logs.append(jnp.where(sc[1] + t >= 0, held[t % NY][j : j + 1, :], masked))
        deltas.append(held[t % NY][4 + j : 5 + j, :])
    top = functools.reduce(jnp.maximum, logs)
    weights = [jnp.exp2(v - top) for v in logs]
    mass = sum(weights)
    weights = [v / mass for v in weights]
    return top + jnp.log2(mass), sum(a * b for a, b in zip(weights, deltas)), weights


def backward_kernel(sc, *refs):
    qs, dos, kvs, held = refs[0:3], refs[3:6], refs[6:12], refs[12:16]
    dqs, own_ref, other_ref = refs[16:19], refs[19], refs[20]
    keys, values, q_all, do_all, dq_acc, logs, deltas, dk, dv = refs[21:]
    load_keys(kvs, keys, values)
    dq_acc[...] = jnp.zeros_like(dq_acc)
    for visit in range(VISITS):
        q_all[visit] = qs[visit][...]
        do_all[visit] = dos[visit][...]
        log_total, delta, _ = combine_stats(sc, visit, held)
        logs[visit] = log_total
        deltas[visit] = delta

    @pl.loop(0, NZ)
    def _(s):
        dk[...] = jnp.zeros_like(dk)
        dv[...] = jnp.zeros_like(dv)

        @pl.loop(0, VISITS)
        def _(visit):
            @pl.when(tile_needed(sc, visit, s))
            def _():
                _, rows, starts = query_rows(sc, visit)
                q, do = q_all[visit], do_all[visit]
                scores = dot(keys[s], q, NT) * (scale * log2e) - logs[visit]
                p = jnp.exp2(jnp.where(tile_mask(sc, s, rows, starts), scores, masked))
                dp = dot(values[s], do, NT)
                ds = (p * (dp - deltas[visit])).astype(bf16)
                dv[...] += dot(p.astype(bf16), do)
                dk[...] += dot(ds, q)
                dq_acc[visit] += dot(keys[s], ds, TN)

        for e, out in enumerate((own_ref, other_ref)):
            half = slice(e * TOK, (e + 1) * TOK)
            out[s, 0:TOK, :] = (dk[half, :] * scale).astype(bf16)
            out[s, TOK:, :] = dv[half, :].astype(bf16)

    for visit in range(VISITS):
        dqs[visit][...] = (dq_acc[visit] * scale).astype(bf16)


def context_kernel(sc, o0, o1, o2, s0, s1, s2, s3, mh, send_ref, rows):
    _, _, weights = combine_stats(sc, 0, (s0, s1, s2, s3))
    out = o0[...].astype(f32) * weights[0]
    for j, o in ((1, o1), (2, o2)):
        out = out + jnp.where(sc[1] >= j, o[...].astype(f32), 0.0) * weights[j]
    for h in range(GROUP):
        rows[:, h * HD : (h + 1) * HD] = out[:, h * TOK : (h + 1) * TOK].T.astype(bf16)
    send_ref[...] = dot(mh[...], rows[...]).astype(bf16)


def add_cores_kernel(own, came, kept, below, above):
    for out, steps in ((kept, KEPT), (below, FROM_BELOW), (above, FROM_ABOVE)):
        for i, s in enumerate(steps):
            out[i] = (own[s].astype(f32) + came[s].astype(f32)).astype(out.dtype)


def add_near_kernel(kept, below, above, o0, o3, o5):
    o0[...] = kept[0] + below[0].astype(f32) + above[0].astype(f32)
    o3[...] = (kept[1] + below[1].astype(f32) + above[1].astype(f32)).astype(bf16)
    o5[...] = (kept[2] + below[2].astype(f32)).astype(bf16)


def rows_kernel(sc, *refs):
    parts, dqs, (cos, sin, w), hids = refs[0:3], refs[3:6], refs[6:9], refs[9:13]
    rg_ref, keep_ref, inner_ref = refs[13], refs[14], refs[15]
    sends = refs[16:19]
    x = sc[4]
    c, s = cos[...], sin[...]
    dq = dqs[0][...].astype(f32)
    for j in (1, 2):
        dq = dq + jnp.where(sc[1] >= j, dqs[j][...].astype(f32), 0.0)
    for h in range(GROUP):
        rg_ref[:, h * HD : (h + 1) * HD] = turn_back(dq[:, h * TOK : (h + 1) * TOK].T, c, s).astype(bf16)
    dkv = sum(p[...].astype(f32) for p in parts)
    rg_ref[:, 512:640] = turn_back(dkv[0:TOK], c, s).astype(bf16)
    rg_ref[:, 640:768] = dkv[TOK:].astype(bf16)
    rg = rg_ref[...]
    inner = jnp.zeros((TOK, 1), f32)
    for t in range(NX):
        chunk = (x + t) % NX
        part = dot(rg, w[pl.ds(pl.multiple_of(chunk * 512, 512), 512), :], NT)
        inner = inner + jnp.sum(part * hids[-t % NX][...].astype(f32), axis=1, keepdims=True)
        if t == 0:
            keep_ref[...] = part
        else:
            sends[t - 1][0:TOK, :] = part.astype(bf16)
    row = jnp.broadcast_to(inner, (TOK, TOK)).T[0:16, :]
    inner_ref[...] = row[0:8, :]
    high = row.astype(bf16).astype(f32)
    line = lax.broadcasted_iota(i32, (16, TOK), 0)
    both = jnp.where(line == 0, high, jnp.where(line == 1, row - high, 0.0)).astype(bf16)
    for out in sends:
        out[TOK:, :] = jnp.concatenate([both, jnp.zeros((16, 384), bf16)], axis=1)


def input_kernel(keep, inner, r1, r2, r3, inv_ref, hid, out_ref):
    total = keep[...]
    row = inner[0:1, :]
    for r in (r1, r2, r3):
        total = total + r[0:TOK, :].astype(f32)
        tail = r[TOK:, 0:TOK].astype(f32)
        row = row + tail[0:1, :] + tail[1:2, :]
    column = jnp.broadcast_to(row, (TOK, TOK)).T[:, 0:1]
    inv = inv_ref[:, 0:1]
    out_ref[...] = inv * total - hid[...].astype(f32) * (inv * inv * inv * column * (1.0 / (NX * 512)))


def weight_kernel(sc, *refs):
    ns, rgs, own_ref, other_ref = refs[0:4], refs[4:8], refs[8], refs[9]
    n_all, rg_all, product = refs[10:]
    for t in range(NY):
        n_all[t * TOK : (t + 1) * TOK, :] = ns[t][...]
        rg_all[t * TOK : (t + 1) * TOK, :] = rgs[t][...]
    product[...] = dot(n_all[...], rg_all[...], TN)
    z, core = sc[2], sc[3]
    for s in range(NZ):
        first = ((z + NZ - s) % NZ) * 64
        own_ref[s] = product[pl.ds(pl.multiple_of(first + core * 32, 32), 32), :].astype(bf16)
        other_ref[s] = product[pl.ds(pl.multiple_of(first + (1 - core) * 32, 32), 32), :].astype(bf16)


def sum_kernel(*refs):
    refs[-1][...] = sum(r[...].astype(f32) for r in refs[:-1])


def index_of(y, z, c):
    return (y * NZ + z) * NC + c


def over_y(a, shift, wrap=True):
    pairs = [
        (index_of(y, z, c), index_of((y + shift) % NY, z, c))
        for y in range(NY)
        for z in range(NZ)
        for c in range(NC)
        if wrap or 0 <= y + shift < NY
    ]
    return lax.ppermute(a, "ctx", pairs)


def over_z(a, shift):
    pairs = [
        (index_of(y, z, c), index_of(y, (z + shift) % NZ, c))
        for y in range(NY)
        for z in range(NZ)
        for c in range(NC)
    ]
    return lax.ppermute(a, "ctx", pairs)


def over_c(a):
    pairs = [(index_of(y, z, c), index_of(y, z, 1 - c)) for y in range(NY) for z in range(NZ) for c in range(NC)]
    return lax.ppermute(a, "ctx", pairs)


def over_x(a, shift):
    return lax.ppermute(a, "fsdp", [(x, (x + shift) % NX) for x in range(NX)])


def exchange_slots(send):
    width = send.shape[1]
    came = lax.all_to_all(send.reshape(N_CTX, CAP, width), "ctx", split_axis=0, concat_axis=0, tiled=True)
    return came.reshape(SLOTS, width)


def reduce_cores_and_z(own, other, name):
    shape = own.shape[1:]
    came = over_c(other)
    kept, below, above = call(
        add_cores_kernel,
        [((3,) + shape, f32), ((3,) + shape, bf16), ((2,) + shape, bf16)],
        "vv",
        (own, came),
        name="add_cores_" + name,
    )
    below, above = over_z(below, -1), over_z(above, 1)
    o0, o3, o5 = call(
        add_near_kernel,
        [(shape, f32), (shape, bf16), (shape, bf16)],
        "vvv",
        (kept, below, above),
        name="add_near_" + name,
    )
    return o0, over_z(o3, -3), over_z(o5, 3)


def shards(hidden, w, doc_lengths, owners, context_grad):
    me = lax.axis_index("ctx").astype(i32)
    x = lax.axis_index("fsdp").astype(i32)
    zero = jnp.zeros((), i32)
    sc = jnp.concatenate(
        [jnp.stack([me, me // (NZ * NC), me // NC % NZ, me % NC, x, zero, zero, zero]), doc_lengths.astype(i32)]
    )
    hids = [hidden] + [over_x(hidden, s) for s in range(1, NX)]

    mo, mh, send = call(
        route_kernel,
        [((SLOTS, TOK), bf16), ((SLOTS, TOK), bf16), ((SLOTS, QW), bf16)],
        "svv",
        (sc, owners.reshape(N_CTX, TOK), context_grad),
        name="route",
    )
    arrived = exchange_slots(send)

    home = me * TOK + jnp.arange(TOK, dtype=i32)
    docs = jnp.arange(8, dtype=i32)
    doc_starts = jnp.sum(jnp.where(docs[:, None] > docs[None, :], doc_lengths[None, :], 0), axis=1)
    start = jnp.max(jnp.where(home[:, None] >= doc_starts[None, :], doc_starts[None, :], 0), axis=1)
    frequency = rope_base ** (-(2.0 * jnp.arange(HD // 2, dtype=f32)) / HD)
    angles = (home - start).astype(f32)[:, None] * frequency[None, :]
    cos, sin = jnp.cos(angles), jnp.sin(angles)
    cos, sin = jnp.concatenate([cos, cos], axis=1), jnp.concatenate([-sin, sin], axis=1)

    q, kv, n0, n1, n2, n3, inv = call(
        project_kernel,
        [((QW, HD), bf16), ((2 * TOK, HD), bf16)] + [((TOK, 512), bf16)] * 4 + [((TOK, HD), f32)],
        "svvvvvvv",
        (sc, *hids, w, cos, sin),
        scratch=[pltpu.VMEM((NX, TOK, 512), bf16)],
        flops=4 * 10**8,
        moved=4 * 10**6,
        name="project",
    )
    three, two = call(
        pack_kernel,
        [((3, 2 * TOK, HD), bf16), ((2, 2 * TOK, HD), bf16)],
        "vvv",
        (kv, over_z(kv, 3), over_z(kv, -3)),
        name="pack",
    )
    kv_own = [three, over_z(three, 1), over_z(two, -1)]
    qs = [q, over_y(q, -1, False), over_y(q, -2, False)]
    kvs = kv_own + [over_c(a) for a in kv_own]
    ns = [n0] + [over_y(n, t) for t, n in ((1, n1), (2, n2), (3, n3))]

    (do,) = call(grad_home_kernel, [((QW, HD), bf16)], "vv", (mh, arrived), name="grad_home")
    dos = [do, over_y(do, -1, False), over_y(do, -2, False)]

    *outs, stats = call(
        forward_kernel,
        [((HD, QW), bf16)] * 3 + [((8, QW), f32)],
        "s" + "v" * 12,
        (sc, *qs, *dos, *kvs),
        scratch=[
            pltpu.VMEM((NZ, 2 * TOK, HD), bf16),
            pltpu.VMEM((NZ, 2 * TOK, HD), bf16),
            pltpu.VMEM((HD, QW), f32),
            pltpu.VMEM((1, QW), f32),
            pltpu.VMEM((1, QW), f32),
        ],
        flops=3 * 10**9,
        name="forward",
    )
    held = [stats] + [over_y(stats, -t) for t in (1, 2, 3)]
    o_came = [outs[0], over_y(outs[1], 1, False), over_y(outs[2], 2, False)]

    *dqs, dkv_own, dkv_other = call(
        backward_kernel,
        [((HD, QW), bf16)] * 3 + [((NZ, 2 * TOK, HD), bf16)] * 2,
        "s" + "v" * 16,
        (sc, *qs, *dos, *kvs, *held),
        scratch=[
            pltpu.VMEM((NZ, 2 * TOK, HD), bf16),
            pltpu.VMEM((NZ, 2 * TOK, HD), bf16),
            pltpu.VMEM((VISITS, QW, HD), bf16),
            pltpu.VMEM((VISITS, QW, HD), bf16),
            pltpu.VMEM((VISITS, HD, QW), f32),
            pltpu.VMEM((VISITS, 1, QW), f32),
            pltpu.VMEM((VISITS, 1, QW), f32),
            pltpu.VMEM((2 * TOK, HD), f32),
            pltpu.VMEM((2 * TOK, HD), f32),
        ],
        flops=5 * 10**9,
        name="backward",
    )
    dkv_home = reduce_cores_and_z(dkv_own, dkv_other, "dkv")
    dq_came = [dqs[0], over_y(dqs[1], 1, False), over_y(dqs[2], 2, False)]

    (context_send,) = call(
        context_kernel,
        [((SLOTS, QW), bf16)],
        "s" + "v" * 8,
        (sc, *o_came, *held, mh),
        scratch=[pltpu.VMEM((TOK, QW), bf16)],
        name="context",
    )
    context_came = exchange_slots(context_send)

    rg, keep, inner, *sends = call(
        rows_kernel,
        [((TOK, 768), bf16), ((TOK, 512), f32), ((8, TOK), f32)] + [((TOK + 16, 512), bf16)] * 3,
        "s" + "v" * 13,
        (sc, *dkv_home, *dq_came, cos, sin, w, *hids),
        flops=4 * 10**8,
        moved=4 * 10**6,
        name="rows",
    )
    rgs = [rg] + [over_y(rg, t) for t in (1, 2, 3)]
    totals = [over_x(a, t) for t, a in zip((1, 2, 3), sends)]
    w_own, w_other = call(
        weight_kernel,
        [((NZ, 32, 768), bf16)] * 2,
        "s" + "v" * 8,
        (sc, *ns, *rgs),
        scratch=[
            pltpu.VMEM((NY * TOK, 512), bf16),
            pltpu.VMEM((NY * TOK, 768), bf16),
            pltpu.VMEM((512, 768), f32),
        ],
        flops=4 * 10**8,
        name="weight",
    )
    w_home = reduce_cores_and_z(w_own, w_other, "weight")
    (input_grad,) = call(
        input_kernel,
        [((TOK, 512), f32)],
        "v" * 7,
        (keep, inner, *totals, inv, hidden),
        name="input",
    )
    (context,) = call(place_kernel, [((TOK, QW), bf16)], "vv", (mo, context_came), name="place")
    (weight_grad,) = call(sum_kernel, [((32, 768), f32)], "vvv", w_home, name="sum_weight")
    return context, input_grad, weight_grad


def solution(mesh):
    placed = (P("ctx", "fsdp"), P(None, "fsdp"), P(), P(), P("ctx", "fsdp"))
    return jax.shard_map(
        shards,
        mesh=mesh,
        in_specs=placed,
        out_specs=(P("ctx", "fsdp"), P("ctx", "fsdp"), P("ctx", "fsdp")),
        check_vma=False,
    )
```

profile of v0, /device:TPU:2, one launch (start us, length us, event | category | flops | bytes accessed | tf_op | source)
XLA Modules:
  0.0 169.5 jit_solution(15681779722560359569)
XLA Ops:
  0.6 1.6 collective-permute-start
  2.2 2.8 %collective-permute-start.1 = (bf16[128,512]{1,0:T(8,128)(2,1)}, bf16[128,512]{1,0:T(8,128)(2,1)S(1)}, u32[]{:S(2)}, u32[]{:S(2)}) collective-permute-start(bf16[128,512]{1,0:T(8,128)(2,1)} %hid.1), channel_id=1, source_target_pairs={{0,2},{1,3},{2,0},{3,1},{4,6},{5,7},{6,4},{7,5},{8,10},{9,11},{10,... | collective-permute-start | bytes 393224 | tf_op jit(solution)/shard_map/ppermute | solution.py:373
  7.9 1.0 route.1
  9.7 12.1 %all-to-all-start = ((bf16[64,4,512]{2,1,0:T(4,128)(2,1)}), bf16[64,4,512]{2,1,0:T(4,128)(2,1)S(1)}, u32[]{:S(2)}, u32[]{:S(2)}) async-start(bf16[64,4,512]{2,1,0:T(4,128)(2,1)} %reshape.41), calls=%async_computation | async-start | bytes 524288 | tf_op jit(solution)/shard_map/all_to_all | solution.py:378
  23.1 1.9 %copy-done = bf16[2048,768]{1,0:T(8,128)(2,1)S(1)} copy-done((bf16[2048,768]{1,0:T(8,128)(2,1)S(1)}, bf16[2048,768]{1,0:T(8,128)(2,1)}, u32[]{:S(2)}) %copy-start) | copy-done | bytes 3145752
  25.9 1.4 project.1
  27.3 3.4 %collective-permute-start.7 = (bf16[256,128]{1,0:T(8,128)(2,1)S(1)}, bf16[256,128]{1,0:T(8,128)(2,1)S(1)}, u32[]{:S(2)}, u32[]{:S(2)}) collective-permute-start(bf16[256,128]{1,0:T(8,128)(2,1)S(1)} %get-tuple-element.48.b0), channel_id=1, source_target_pairs={{0,24},{4,28},{8,32},{12,36},{16,40},{20,44},{24,48},{28,52},{32,5... | collective-permute-start | bytes 196616 | tf_op jit(solution)/shard_map/ppermute | solution.py:364
  30.8 1.7 collective-permute-start.8
  32.4 3.8 %collective-permute-done.7.b3 = bf16[256,128]{1,0:T(8,128)(2,1)S(1)} collective-permute-done((bf16[256,128]{1,0:T(8,128)(2,1)S(1)}, bf16[256,128]{1,0:T(8,128)(2,1)S(1)}, u32[]{:S(2)}, u32[]{:S(2)}) %collective-permute-start.7) | collective-permute-done | bytes 65568 | tf_op jit(solution)/shard_map/ppermute | solution.py:364
  36.9 6.3 %collective-permute-start.9 = (bf16[3,256,128]{2,1,0:T(8,128)(2,1)S(1)}, bf16[3,256,128]{2,1,0:T(8,128)(2,1)S(1)}, u32[]{:S(2)}, u32[]{:S(2)}) collective-permute-start(bf16[3,256,128]{2,1,0:T(8,128)(2,1)S(1)} %get-tuple-element.49.refs_6_), channel_id=1, source_target_pairs={{0,8},{4,12},{8,16},{12,20},{16,24},{20,28},{24,32},{28,36},{32,40... | collective-permute-start | bytes 589832 | tf_op jit(solution)/shard_map/ppermute | solution.py:364
  43.3 1.3 collective-permute-start.3
  44.5 1.3 collective-permute-start.4
  45.9 1.3 collective-permute-done.9.refs_7_
  48.5 1.6 collective-permute-done.3.refs_1_
  50.1 1.3 collective-permute-start.5
  51.4 1.6 collective-permute-done.4.refs_2_
  53.0 1.3 collective-permute-start.6
  54.4 2.6 %collective-permute-done.5.refs_4_ = bf16[512,128]{1,0:T(8,128)(2,1)S(1)} collective-permute-done((bf16[512,128]{1,0:T(8,128)(2,1)S(1)}, bf16[512,128]{1,0:T(8,128)(2,1)S(1)}, u32[]{:S(2)}, u32[]{:S(2)}) %collective-permute-start.5) | collective-permute-done | bytes 131104 | tf_op jit(solution)/shard_map/ppermute | solution.py:354
  57.0 4.4 %collective-permute-done.6.refs_5_ = bf16[512,128]{1,0:T(8,128)(2,1)S(1)} collective-permute-done((bf16[512,128]{1,0:T(8,128)(2,1)S(1)}, bf16[512,128]{1,0:T(8,128)(2,1)S(1)}, u32[]{:S(2)}, u32[]{:S(2)}) %collective-permute-start.6) | collective-permute-done | bytes 131104 | tf_op jit(solution)/shard_map/ppermute | solution.py:354
  61.4 3.1 %forward.1 = (bf16[128,512]{1,0:T(8,128)(2,1)S(1)}, bf16[128,512]{1,0:T(8,128)(2,1)S(1)}, bf16[128,512]{1,0:T(8,128)(2,1)S(1)}, f32[8,512]{1,0:T(8,128)S(1)}) custom-call(s32[16]{0:T(128)S(1)} %concatenate.9.sc, bf16[512,128]{1,0:T(8,128)(2,1)S(1)} %get-tuple-element.45.refs_0_, bf16[512,128]{1,0:T(8,128)(2,1)S(1)} %collective-permute-done.3.refs_1_, ...), custom_call_target="tpu_custom_call" | custom-call | flops 3000000000 | bytes 2000000 | tf_op jit(solution)/shard_map/forward/pallas_call | solution.py:43
  64.9 7.4 %collective-permute-start.17 = (f32[8,512]{1,0:T(8,128)S(1)}, f32[8,512]{1,0:T(8,128)S(1)}, u32[]{:S(2)}, u32[]{:S(2)}) collective-permute-start(f32[8,512]{1,0:T(8,128)S(1)} %get-tuple-element.54.s0.refs_12_), channel_id=1, source_target_pairs={{0,128},{4,132},{8,136},{12,140},{16,144},{20,148},{24,152},{28,15... | collective-permute-start | bytes 49160 | tf_op jit(solution)/shard_map/ppermute | solution.py:354
  72.3 1.7 %collective-permute-done.17.s2.refs_14_ = f32[8,512]{1,0:T(8,128)S(1)} collective-permute-done((f32[8,512]{1,0:T(8,128)S(1)}, f32[8,512]{1,0:T(8,128)S(1)}, u32[]{:S(2)}, u32[]{:S(2)}) %collective-permute-start.17) | collective-permute-done | bytes 16416 | tf_op jit(solution)/shard_map/ppermute | solution.py:354
  74.1 3.2 %collective-permute-done.18.s3.refs_15_ = f32[8,512]{1,0:T(8,128)S(1)} collective-permute-done((f32[8,512]{1,0:T(8,128)S(1)}, f32[8,512]{1,0:T(8,128)S(1)}, u32[]{:S(2)}, u32[]{:S(2)}) %collective-permute-start.18) | collective-permute-done | bytes 16416 | tf_op jit(solution)/shard_map/ppermute | solution.py:354
  78.2 3.3 %backward.1 = (bf16[128,512]{1,0:T(8,128)(2,1)S(1)}, bf16[128,512]{1,0:T(8,128)(2,1)S(1)}, bf16[128,512]{1,0:T(8,128)(2,1)S(1)}, bf16[8,256,128]{2,1,0:T(8,128)(2,1)S(1)}, bf16[8,256,128]{2,1,0:T(8,128)(2,1)S(1)}) custom-call(s32[16]{0:T(128)S(1)} %concatenate.9.sc, bf16[512,128]{1,0:T(8,128)(2,1)S(1)} %get-tuple-element.45.refs_0_, ...), custom_call_target="tpu_custom_call" | custom-call | flops 5000000000 | bytes 2000000 | tf_op jit(solution)/shard_map/backward/pallas_call | solution.py:43
  81.6 1.9 %collective-permute-done.19.came = bf16[8,256,128]{2,1,0:T(8,128)(2,1)S(1)} collective-permute-done((bf16[8,256,128]{2,1,0:T(8,128)(2,1)S(1)}, bf16[8,256,128]{2,1,0:T(8,128)(2,1)S(1)}, u32[]{:S(2)}, u32[]{:S(2)}) %collective-permute-start.19) | collective-permute-done | bytes 524320 | tf_op jit(solution)/shard_map/ppermute | solution.py:369
  83.7 3.9 %collective-permute-start.20 = (bf16[3,256,128]{2,1,0:T(8,128)(2,1)S(1)}, bf16[3,256,128]{2,1,0:T(8,128)(2,1)S(1)}, u32[]{:S(2)}, u32[]{:S(2)}) collective-permute-start(bf16[3,256,128]{2,1,0:T(8,128)(2,1)S(1)} %get-tuple-element.58), channel_id=1, source_target_pairs={{0,56},{4,60},{8,0},{12,4},{16,8},{20,12},{24,16},{28,20},{32,24},... | collective-permute-start | bytes 589832 | tf_op jit(solution)/shard_map/ppermute | solution.py:364
  87.5 7.4 %collective-permute-start.24 = (bf16[128,512]{1,0:T(8,128)(2,1)S(1)}, bf16[128,512]{1,0:T(8,128)(2,1)S(1)}, u32[]{:S(2)}, u32[]{:S(2)}) collective-permute-start(bf16[128,512]{1,0:T(8,128)(2,1)S(1)} %get-tuple-element.64), channel_id=1, source_target_pairs={{0,64},{4,68},{8,72},{12,76},{16,80},{20,84},{24,88},{28,92},{32,9... | collective-permute-start | bytes 393224 | tf_op jit(solution)/shard_map/ppermute | solution.py:354
  94.9 1.3 collective-permute-start.25
  96.3 2.0 %collective-permute-start.22 = (bf16[256,128]{1,0:T(8,128)(2,1)S(1)}, bf16[256,128]{1,0:T(8,128)(2,1)S(1)}, u32[]{:S(2)}, u32[]{:S(2)}) collective-permute-start(bf16[256,128]{1,0:T(8,128)(2,1)S(1)} %get-tuple-element.61), channel_id=1, source_target_pairs={{0,40},{4,44},{8,48},{12,52},{16,56},{20,60},{24,0},{28,4},{32,8},... | collective-permute-start | bytes 196616 | tf_op jit(solution)/shard_map/ppermute | solution.py:364
  98.4 1.9 %collective-permute-start.23 = (bf16[256,128]{1,0:T(8,128)(2,1)S(1)}, bf16[256,128]{1,0:T(8,128)(2,1)S(1)}, u32[]{:S(2)}, u32[]{:S(2)}) collective-permute-start(bf16[256,128]{1,0:T(8,128)(2,1)S(1)} %get-tuple-element.62), channel_id=1, source_target_pairs={{0,24},{4,28},{8,32},{12,36},{16,40},{20,44},{24,48},{28,52},{32,5... | collective-permute-start | bytes 196616 | tf_op jit(solution)/shard_map/ppermute | solution.py:364
  100.2 3.2 %collective-permute-start.29 = (bf16[128,512]{1,0:T(8,128)(2,1)S(1)}, bf16[128,512]{1,0:T(8,128)(2,1)S(1)}, u32[]{:S(2)}, u32[]{:S(2)}) collective-permute-start(bf16[128,512]{1,0:T(8,128)(2,1)S(1)} %get-tuple-element.73), channel_id=1, source_target_pairs={{0,64},{4,68},{8,72},{12,76},{16,80},{20,84},{24,88},{28,92},{32,9... | collective-permute-start | bytes 393224 | tf_op jit(solution)/shard_map/ppermute | solution.py:354
  103.5 3.6 %collective-permute-done.23.refs_2_ = bf16[256,128]{1,0:T(8,128)(2,1)S(1)} collective-permute-done((bf16[256,128]{1,0:T(8,128)(2,1)S(1)}, bf16[256,128]{1,0:T(8,128)(2,1)S(1)}, u32[]{:S(2)}, u32[]{:S(2)}) %collective-permute-start.23) | collective-permute-done | bytes 65568 | tf_op jit(solution)/shard_map/ppermute | solution.py:364
  107.0 2.0 %rows.1 = (bf16[128,768]{1,0:T(8,128)(2,1)S(1)}, f32[128,512]{1,0:T(8,128)S(1)}, f32[8,128]{1,0:T(8,128)S(1)}, bf16[144,512]{1,0:T(8,128)(2,1)S(1)}, bf16[144,51...) custom-call(s32[16]{0:T(128)S(1)} %concatenate.9.sc, f32[256,128]{1,0:T(8,128)S(1)} %get-tuple-element.60.refs_0_, ...), custom_call_target="tpu_custom_call" | custom-call | flops 400000000 | bytes 4000000 | tf_op jit(solution)/shard_map/rows/pallas_call | solution.py:43
  109.0 1.8 %collective-permute-start.32 = (bf16[128,768]{1,0:T(8,128)(2,1)S(1)}, bf16[128,768]{1,0:T(8,128)(2,1)S(1)}, u32[]{:S(2)}, u32[]{:S(2)}) collective-permute-start(bf16[128,768]{1,0:T(8,128)(2,1)S(1)} %get-tuple-element.76.refs_4_), channel_id=1, source_target_pairs={{0,64},{4,68},{8,72},{12,76},{16,80},{20,84},{24,88},{28,92},{32,9... | collective-permute-start | bytes 589832 | tf_op jit(solution)/shard_map/ppermute | solution.py:354
  110.8 2.8 %collective-permute-start.34 = (bf16[128,768]{1,0:T(8,128)(2,1)S(1)}, bf16[128,768]{1,0:T(8,128)(2,1)S(1)}, u32[]{:S(2)}, u32[]{:S(2)}) collective-permute-start(bf16[128,768]{1,0:T(8,128)(2,1)S(1)} %get-tuple-element.76.refs_4_), channel_id=1, source_target_pairs={{0,192},{4,196},{8,200},{12,204},{16,208},{20,212},{24,216},{28,22... | collective-permute-start | bytes 589832 | tf_op jit(solution)/shard_map/ppermute | solution.py:354
  113.5 1.7 collective-permute-start.30
  115.8 5.0 %collective-permute-done.30.refs_2_ = bf16[128,512]{1,0:T(8,128)(2,1)S(1)} collective-permute-done((bf16[128,512]{1,0:T(8,128)(2,1)S(1)}, bf16[128,512]{1,0:T(8,128)(2,1)S(1)}, u32[]{:S(2)}, u32[]{:S(2)}) %collective-permute-start.30) | collective-permute-done | bytes 131104 | tf_op jit(solution)/shard_map/ppermute | solution.py:354
  120.8 7.5 %collective-permute-start.14 = (bf16[128,512]{1,0:T(8,128)(2,1)S(1)}, bf16[128,512]{1,0:T(8,128)(2,1)S(1)}, u32[]{:S(2)}, u32[]{:S(2)}) collective-permute-start(bf16[128,512]{1,0:T(8,128)(2,1)S(1)} %get-tuple-element.52), channel_id=1, source_target_pairs={{0,64},{4,68},{8,72},{12,76},{16,80},{20,84},{24,88},{28,92},{32,9... | collective-permute-start | bytes 393224 | tf_op jit(solution)/shard_map/ppermute | solution.py:354
  128.4 4.4 %collective-permute-start.15 = (bf16[128,512]{1,0:T(8,128)(2,1)S(1)}, bf16[128,512]{1,0:T(8,128)(2,1)S(1)}, u32[]{:S(2)}, u32[]{:S(2)}) collective-permute-start(bf16[128,512]{1,0:T(8,128)(2,1)S(1)} %get-tuple-element.53), channel_id=1, source_target_pairs={{0,128},{4,132},{8,136},{12,140},{16,144},{20,148},{24,152},{28,15... | collective-permute-start | bytes 393224 | tf_op jit(solution)/shard_map/ppermute | solution.py:354
  132.8 1.2 weight.1
  135.3 0.9 context.1
  137.0 9.7 %all-to-all-start.1 = ((bf16[64,4,512]{2,1,0:T(4,128)(2,1)}), bf16[64,4,512]{2,1,0:T(4,128)(2,1)S(1)}, u32[]{:S(2)}, u32[]{:S(2)}) async-start(bf16[64,4,512]{2,1,0:T(4,128)(2,1)} %reshape.43), calls=%async_computation.1 | async-start | bytes 524288 | tf_op jit(solution)/shard_map/all_to_all | solution.py:378
  146.8 2.9 %collective-permute-start.36 = (bf16[3,32,768]{2,1,0:T(8,128)(2,1)S(1)}, bf16[3,32,768]{2,1,0:T(8,128)(2,1)S(1)}, u32[]{:S(2)}, u32[]{:S(2)}) collective-permute-start(bf16[3,32,768]{2,1,0:T(8,128)(2,1)S(1)} %get-tuple-element.80), channel_id=1, source_target_pairs={{0,56},{4,60},{8,0},{12,4},{16,8},{20,12},{24,16},{28,20},{32,24},... | collective-permute-start | bytes 442376 | tf_op jit(solution)/shard_map/ppermute | solution.py:364
  149.6 3.5 %collective-permute-start.27 = (bf16[144,512]{1,0:T(8,128)(2,1)S(1)}, bf16[144,512]{1,0:T(8,128)(2,1)S(1)}, u32[]{:S(2)}, u32[]{:S(2)}) collective-permute-start(bf16[144,512]{1,0:T(8,128)(2,1)S(1)} %get-tuple-element.69), channel_id=1, source_target_pairs={{0,2},{1,3},{2,0},{3,1},{4,6},{5,7},{6,4},{7,5},{8,10},{9,11},{10,... | collective-permute-start | bytes 442376 | tf_op jit(solution)/shard_map/ppermute | solution.py:373
  153.1 5.9 %collective-permute-done.37.above = bf16[2,32,768]{2,1,0:T(8,128)(2,1)S(1)} collective-permute-done((bf16[2,32,768]{2,1,0:T(8,128)(2,1)S(1)}, bf16[2,32,768]{2,1,0:T(8,128)(2,1)S(1)}, u32[]{:S(2)}, u32[]{:S(2)}) %collective-permute-start.37) | collective-permute-done | bytes 98336 | tf_op jit(solution)/shard_map/ppermute | solution.py:364
  159.1 2.4 %collective-permute-start.38 = (bf16[32,768]{1,0:T(8,128)(2,1)S(1)}, bf16[32,768]{1,0:T(8,128)(2,1)S(1)}, u32[]{:S(2)}, u32[]{:S(2)}) collective-permute-start(bf16[32,768]{1,0:T(8,128)(2,1)S(1)} %get-tuple-element.83), channel_id=1, source_target_pairs={{0,40},{4,44},{8,48},{12,52},{16,56},{20,60},{24,0},{28,4},{32,8},... | collective-permute-start | bytes 147464 | tf_op jit(solution)/shard_map/ppermute | solution.py:364
  161.5 1.5 collective-permute-start.39
  165.1 3.7 %collective-permute-done.39.refs_2_ = bf16[32,768]{1,0:T(8,128)(2,1)S(1)} collective-permute-done((bf16[32,768]{1,0:T(8,128)(2,1)S(1)}, bf16[32,768]{1,0:T(8,128)(2,1)S(1)}, u32[]{:S(2)}, u32[]{:S(2)}) %collective-permute-start.39) | collective-permute-done | bytes 49184 | tf_op jit(solution)/shard_map/ppermute | solution.py:364
  (81 shorter events, 14.8 us)
Async XLA Ops:
  0.6 22.5 %collective-permute-start = (bf16[128,512]{1,0:T(8,128)(2,1)}, bf16[128,512]{1,0:T(8,128)(2,1)S(1)}, u32[]{:S(2)}, u32[]{:S(2)}) collective-permute-start(bf16[128,512]{1,0:T(8,128)(2,1)} %hid.1), channel_id=1, source_target_pairs={{0,1},{1,2},{2,3},{3,0},{4,5},{5,6},{6,7},{7,4},{8,9},{9,10},{10,1... | collective-permute-start | bytes 393224 | tf_op jit(solution)/shard_map/ppermute | solution.py:373
  2.2 20.9 %collective-permute-start.1 = (bf16[128,512]{1,0:T(8,128)(2,1)}, bf16[128,512]{1,0:T(8,128)(2,1)S(1)}, u32[]{:S(2)}, u32[]{:S(2)}) collective-permute-start(bf16[128,512]{1,0:T(8,128)(2,1)} %hid.1), channel_id=1, source_target_pairs={{0,2},{1,3},{2,0},{3,1},{4,6},{5,7},{6,4},{7,5},{8,10},{9,11},{10,... | collective-permute-start | bytes 393224 | tf_op jit(solution)/shard_map/ppermute | solution.py:373
  5.0 18.1 %collective-permute-start.2 = (bf16[128,512]{1,0:T(8,128)(2,1)}, bf16[128,512]{1,0:T(8,128)(2,1)S(1)}, u32[]{:S(2)}, u32[]{:S(2)}) collective-permute-start(bf16[128,512]{1,0:T(8,128)(2,1)} %hid.1), channel_id=1, source_target_pairs={{0,3},{1,0},{2,1},{3,2},{4,7},{5,4},{6,5},{7,6},{8,11},{9,8},{10,9... | collective-permute-start | bytes 393224 | tf_op jit(solution)/shard_map/ppermute | solution.py:373
  6.2 0.9 copy-start.4
  9.7 38.6 %all-to-all-start = ((bf16[64,4,512]{2,1,0:T(4,128)(2,1)}), bf16[64,4,512]{2,1,0:T(4,128)(2,1)S(1)}, u32[]{:S(2)}, u32[]{:S(2)}) async-start(bf16[64,4,512]{2,1,0:T(4,128)(2,1)} %reshape.41), calls=%async_computation | async-start | bytes 524288 | tf_op jit(solution)/shard_map/all_to_all | solution.py:378
  23.1 1.9 %copy-start = (bf16[2048,768]{1,0:T(8,128)(2,1)S(1)}, bf16[2048,768]{1,0:T(8,128)(2,1)}, u32[]{:S(2)}) copy-start(bf16[2048,768]{1,0:T(8,128)(2,1)} %refs_8_.1) | copy-start | bytes 9437188
  27.3 8.9 %collective-permute-start.7 = (bf16[256,128]{1,0:T(8,128)(2,1)S(1)}, bf16[256,128]{1,0:T(8,128)(2,1)S(1)}, u32[]{:S(2)}, u32[]{:S(2)}) collective-permute-start(bf16[256,128]{1,0:T(8,128)(2,1)S(1)} %get-tuple-element.48.b0), channel_id=1, source_target_pairs={{0,24},{4,28},{8,32},{12,36},{16,40},{20,44},{24,48},{28,52},{32,5... | collective-permute-start | bytes 196616 | tf_op jit(solution)/shard_map/ppermute | solution.py:364
  30.8 6.1 %collective-permute-start.8 = (bf16[256,128]{1,0:T(8,128)(2,1)S(1)}, bf16[256,128]{1,0:T(8,128)(2,1)S(1)}, u32[]{:S(2)}, u32[]{:S(2)}) collective-permute-start(bf16[256,128]{1,0:T(8,128)(2,1)S(1)} %get-tuple-element.48.b0), channel_id=1, source_target_pairs={{0,40},{4,44},{8,48},{12,52},{16,56},{20,60},{24,0},{28,4},{32,8},... | collective-permute-start | bytes 196616 | tf_op jit(solution)/shard_map/ppermute | solution.py:364
  36.9 10.4 %collective-permute-start.9 = (bf16[3,256,128]{2,1,0:T(8,128)(2,1)S(1)}, bf16[3,256,128]{2,1,0:T(8,128)(2,1)S(1)}, u32[]{:S(2)}, u32[]{:S(2)}) collective-permute-start(bf16[3,256,128]{2,1,0:T(8,128)(2,1)S(1)} %get-tuple-element.49.refs_6_), channel_id=1, source_target_pairs={{0,8},{4,12},{8,16},{12,20},{16,24},{20,28},{24,32},{28,36},{32,40... | collective-permute-start | bytes 589832 | tf_op jit(solution)/shard_map/ppermute | solution.py:364
  43.3 5.0 %collective-permute-start.10 = (bf16[2,256,128]{2,1,0:T(8,128)(2,1)S(1)}, bf16[2,256,128]{2,1,0:T(8,128)(2,1)S(1)}, u32[]{:S(2)}, u32[]{:S(2)}) collective-permute-start(bf16[2,256,128]{2,1,0:T(8,128)(2,1)S(1)} %get-tuple-element.50), channel_id=1, source_target_pairs={{0,56},{4,60},{8,0},{12,4},{16,8},{20,12},{24,16},{28,20},{32,24},... | collective-permute-start | bytes 393224 | tf_op jit(solution)/shard_map/ppermute | solution.py:364
  43.3 6.8 %collective-permute-start.3 = (bf16[512,128]{1,0:T(8,128)(2,1)S(1)}, bf16[512,128]{1,0:T(8,128)(2,1)S(1)}, u32[]{:S(2)}, u32[]{:S(2)}) collective-permute-start(bf16[512,128]{1,0:T(8,128)(2,1)S(1)} %get-tuple-element.45.refs_0_), channel_id=1, source_target_pairs={{64,0},{68,4},{72,8},{76,12},{80,16},{84,20},{88,24},{92,28},{96,3... | collective-permute-start | bytes 393224 | tf_op jit(solution)/shard_map/ppermute | solution.py:354
  44.5 8.5 %collective-permute-start.4 = (bf16[512,128]{1,0:T(8,128)(2,1)S(1)}, bf16[512,128]{1,0:T(8,128)(2,1)S(1)}, u32[]{:S(2)}, u32[]{:S(2)}) collective-permute-start(bf16[512,128]{1,0:T(8,128)(2,1)S(1)} %get-tuple-element.45.refs_0_), channel_id=1, source_target_pairs={{128,0},{132,4},{136,8},{140,12},{144,16},{148,20},{152,24},{156,2... | collective-permute-start | bytes 393224 | tf_op jit(solution)/shard_map/ppermute | solution.py:354
  45.8 8.5 %collective-permute-start.11 = (bf16[3,256,128]{2,1,0:T(8,128)(2,1)S(1)}, bf16[3,256,128]{2,1,0:T(8,128)(2,1)S(1)}, u32[]{:S(2)}, u32[]{:S(2)}) collective-permute-start(bf16[3,256,128]{2,1,0:T(8,128)(2,1)S(1)} %get-tuple-element.49.refs_6_), channel_id=1, source_target_pairs={{0,4},{4,0},{8,12},{12,8},{16,20},{20,16},{24,28},{28,24},{32,36},... | collective-permute-start | bytes 589832 | tf_op jit(solution)/shard_map/ppermute | solution.py:369
  47.3 7.1 %collective-permute-start.12 = (bf16[3,256,128]{2,1,0:T(8,128)(2,1)S(1)}, bf16[3,256,128]{2,1,0:T(8,128)(2,1)S(1)}, u32[]{:S(2)}, u32[]{:S(2)}) collective-permute-start(bf16[3,256,128]{2,1,0:T(8,128)(2,1)S(1)} %collective-permute-done.9.refs_7_), channel_id=1, source_target_pairs={{0,4},{4,0},{8,12},{12,8},{16,20},{20,16},{24,28},{28,24},{32,36},... | collective-permute-start | bytes 589832 | tf_op jit(solution)/shard_map/ppermute | solution.py:369
  48.2 6.1 %collective-permute-start.13 = (bf16[2,256,128]{2,1,0:T(8,128)(2,1)S(1)}, bf16[2,256,128]{2,1,0:T(8,128)(2,1)S(1)}, u32[]{:S(2)}, u32[]{:S(2)}) collective-permute-start(bf16[2,256,128]{2,1,0:T(8,128)(2,1)S(1)} %collective-permute-done.10.refs_8_), channel_id=1, source_target_pairs={{0,4},{4,0},{8,12},{12,8},{16,20},{20,16},{24,28},{28,24},{32,36},... | collective-permute-start | bytes 393224 | tf_op jit(solution)/shard_map/ppermute | solution.py:369
  50.1 6.8 %collective-permute-start.5 = (bf16[512,128]{1,0:T(8,128)(2,1)S(1)}, bf16[512,128]{1,0:T(8,128)(2,1)S(1)}, u32[]{:S(2)}, u32[]{:S(2)}) collective-permute-start(bf16[512,128]{1,0:T(8,128)(2,1)S(1)} %grad_home.1.refs_3_), channel_id=1, source_target_pairs={{64,0},{68,4},{72,8},{76,12},{80,16},{84,20},{88,24},{92,28},{96,3... | collective-permute-start | bytes 393224 | tf_op jit(solution)/shard_map/ppermute | solution.py:354
  53.0 8.4 %collective-permute-start.6 = (bf16[512,128]{1,0:T(8,128)(2,1)S(1)}, bf16[512,128]{1,0:T(8,128)(2,1)S(1)}, u32[]{:S(2)}, u32[]{:S(2)}) collective-permute-start(bf16[512,128]{1,0:T(8,128)(2,1)S(1)} %grad_home.1.refs_3_), channel_id=1, source_target_pairs={{128,0},{132,4},{136,8},{140,12},{144,16},{148,20},{152,24},{156,2... | collective-permute-start | bytes 393224 | tf_op jit(solution)/shard_map/ppermute | solution.py:354
  54.4 10.2 %copy-start.5 = (bf16[2,256,128]{2,1,0:T(8,128)(2,1)}, bf16[2,256,128]{2,1,0:T(8,128)(2,1)S(1)}, u32[]{:S(2)}) copy-start(bf16[2,256,128]{2,1,0:T(8,128)(2,1)S(1)} %collective-permute-done.13.refs_11_) | copy-start | bytes 393220
  64.6 42.5 %copy-start.3 = (bf16[128,512]{1,0:T(8,128)(2,1)S(1)}, bf16[128,512]{1,0:T(8,128)(2,1)}, u32[]{:S(2)}) copy-start(bf16[128,512]{1,0:T(8,128)(2,1)} %hid.1) | copy-start | bytes 393220
  64.6 7.8 %collective-permute-start.16 = (f32[8,512]{1,0:T(8,128)S(1)}, f32[8,512]{1,0:T(8,128)S(1)}, u32[]{:S(2)}, u32[]{:S(2)}) collective-permute-start(f32[8,512]{1,0:T(8,128)S(1)} %get-tuple-element.54.s0.refs_12_), channel_id=1, source_target_pairs={{0,192},{4,196},{8,200},{12,204},{16,208},{20,212},{24,216},{28,22... | collective-permute-start | bytes 49160 | tf_op jit(solution)/shard_map/ppermute | solution.py:354
  64.9 9.2 %collective-permute-start.17 = (f32[8,512]{1,0:T(8,128)S(1)}, f32[8,512]{1,0:T(8,128)S(1)}, u32[]{:S(2)}, u32[]{:S(2)}) collective-permute-start(f32[8,512]{1,0:T(8,128)S(1)} %get-tuple-element.54.s0.refs_12_), channel_id=1, source_target_pairs={{0,128},{4,132},{8,136},{12,140},{16,144},{20,148},{24,152},{28,15... | collective-permute-start | bytes 49160 | tf_op jit(solution)/shard_map/ppermute | solution.py:354
  72.3 4.9 %collective-permute-start.18 = (f32[8,512]{1,0:T(8,128)S(1)}, f32[8,512]{1,0:T(8,128)S(1)}, u32[]{:S(2)}, u32[]{:S(2)}) collective-permute-start(f32[8,512]{1,0:T(8,128)S(1)} %get-tuple-element.54.s0.refs_12_), channel_id=1, source_target_pairs={{0,64},{4,68},{8,72},{12,76},{16,80},{20,84},{24,88},{28,92},{32,9... | collective-permute-start | bytes 49160 | tf_op jit(solution)/shard_map/ppermute | solution.py:354
  77.3 0.9 copy-start.6
  78.2 28.8 %copy-start.1 = (bf16[2048,768]{1,0:T(8,128)(2,1)S(1)}, bf16[2048,768]{1,0:T(8,128)(2,1)}, u32[]{:S(2)}) copy-start(bf16[2048,768]{1,0:T(8,128)(2,1)} %refs_8_.1) | copy-start | bytes 9437188
  81.5 2.0 %collective-permute-start.19 = (bf16[8,256,128]{2,1,0:T(8,128)(2,1)S(1)}, bf16[8,256,128]{2,1,0:T(8,128)(2,1)S(1)}, u32[]{:S(2)}, u32[]{:S(2)}) collective-permute-start(bf16[8,256,128]{2,1,0:T(8,128)(2,1)S(1)} %get-tuple-element.56), channel_id=1, source_target_pairs={{0,4},{4,0},{8,12},{12,8},{16,20},{20,16},{24,28},{28,24},{32,36},... | collective-permute-start | bytes 1572872 | tf_op jit(solution)/shard_map/ppermute | solution.py:369
  83.7 12.6 %collective-permute-start.20 = (bf16[3,256,128]{2,1,0:T(8,128)(2,1)S(1)}, bf16[3,256,128]{2,1,0:T(8,128)(2,1)S(1)}, u32[]{:S(2)}, u32[]{:S(2)}) collective-permute-start(bf16[3,256,128]{2,1,0:T(8,128)(2,1)S(1)} %get-tuple-element.58), channel_id=1, source_target_pairs={{0,56},{4,60},{8,0},{12,4},{16,8},{20,12},{24,16},{28,20},{32,24},... | collective-permute-start | bytes 589832 | tf_op jit(solution)/shard_map/ppermute | solution.py:364
  87.5 8.7 %collective-permute-start.21 = (bf16[2,256,128]{2,1,0:T(8,128)(2,1)S(1)}, bf16[2,256,128]{2,1,0:T(8,128)(2,1)S(1)}, u32[]{:S(2)}, u32[]{:S(2)}) collective-permute-start(bf16[2,256,128]{2,1,0:T(8,128)(2,1)S(1)} %get-tuple-element.59), channel_id=1, source_target_pairs={{0,8},{4,12},{8,16},{12,20},{16,24},{20,28},{24,32},{28,36},{32,40... | collective-permute-start | bytes 393224 | tf_op jit(solution)/shard_map/ppermute | solution.py:364
  87.5 15.9 %collective-permute-start.24 = (bf16[128,512]{1,0:T(8,128)(2,1)S(1)}, bf16[128,512]{1,0:T(8,128)(2,1)S(1)}, u32[]{:S(2)}, u32[]{:S(2)}) collective-permute-start(bf16[128,512]{1,0:T(8,128)(2,1)S(1)} %get-tuple-element.64), channel_id=1, source_target_pairs={{0,64},{4,68},{8,72},{12,76},{16,80},{20,84},{24,88},{28,92},{32,9... | collective-permute-start | bytes 393224 | tf_op jit(solution)/shard_map/ppermute | solution.py:354
  94.9 8.5 %collective-permute-start.25 = (bf16[128,512]{1,0:T(8,128)(2,1)S(1)}, bf16[128,512]{1,0:T(8,128)(2,1)S(1)}, u32[]{:S(2)}, u32[]{:S(2)}) collective-permute-start(bf16[128,512]{1,0:T(8,128)(2,1)S(1)} %get-tuple-element.65), channel_id=1, source_target_pairs={{0,128},{4,132},{8,136},{12,140},{16,144},{20,148},{24,152},{28,15... | collective-permute-start | bytes 393224 | tf_op jit(solution)/shard_map/ppermute | solution.py:354
  96.3 7.1 %collective-permute-start.22 = (bf16[256,128]{1,0:T(8,128)(2,1)S(1)}, bf16[256,128]{1,0:T(8,128)(2,1)S(1)}, u32[]{:S(2)}, u32[]{:S(2)}) collective-permute-start(bf16[256,128]{1,0:T(8,128)(2,1)S(1)} %get-tuple-element.61), channel_id=1, source_target_pairs={{0,40},{4,44},{8,48},{12,52},{16,56},{20,60},{24,0},{28,4},{32,8},... | collective-permute-start | bytes 196616 | tf_op jit(solution)/shard_map/ppermute | solution.py:364
  98.4 8.7 %collective-permute-start.23 = (bf16[256,128]{1,0:T(8,128)(2,1)S(1)}, bf16[256,128]{1,0:T(8,128)(2,1)S(1)}, u32[]{:S(2)}, u32[]{:S(2)}) collective-permute-start(bf16[256,128]{1,0:T(8,128)(2,1)S(1)} %get-tuple-element.62), channel_id=1, source_target_pairs={{0,24},{4,28},{8,32},{12,36},{16,40},{20,44},{24,48},{28,52},{32,5... | collective-permute-start | bytes 196616 | tf_op jit(solution)/shard_map/ppermute | solution.py:364
  100.2 15.0 %collective-permute-start.29 = (bf16[128,512]{1,0:T(8,128)(2,1)S(1)}, bf16[128,512]{1,0:T(8,128)(2,1)S(1)}, u32[]{:S(2)}, u32[]{:S(2)}) collective-permute-start(bf16[128,512]{1,0:T(8,128)(2,1)S(1)} %get-tuple-element.73), channel_id=1, source_target_pairs={{0,64},{4,68},{8,72},{12,76},{16,80},{20,84},{24,88},{28,92},{32,9... | collective-permute-start | bytes 393224 | tf_op jit(solution)/shard_map/ppermute | solution.py:354
  109.0 23.8 %collective-permute-start.32 = (bf16[128,768]{1,0:T(8,128)(2,1)S(1)}, bf16[128,768]{1,0:T(8,128)(2,1)S(1)}, u32[]{:S(2)}, u32[]{:S(2)}) collective-permute-start(bf16[128,768]{1,0:T(8,128)(2,1)S(1)} %get-tuple-element.76.refs_4_), channel_id=1, source_target_pairs={{0,64},{4,68},{8,72},{12,76},{16,80},{20,84},{24,88},{28,92},{32,9... | collective-permute-start | bytes 589832 | tf_op jit(solution)/shard_map/ppermute | solution.py:354
  110.8 22.0 %collective-permute-start.33 = (bf16[128,768]{1,0:T(8,128)(2,1)S(1)}, bf16[128,768]{1,0:T(8,128)(2,1)S(1)}, u32[]{:S(2)}, u32[]{:S(2)}) collective-permute-start(bf16[128,768]{1,0:T(8,128)(2,1)S(1)} %get-tuple-element.76.refs_4_), channel_id=1, source_target_pairs={{0,128},{4,132},{8,136},{12,140},{16,144},{20,148},{24,152},{28,15... | collective-permute-start | bytes 589832 | tf_op jit(solution)/shard_map/ppermute | solution.py:354
  110.8 22.0 %collective-permute-start.34 = (bf16[128,768]{1,0:T(8,128)(2,1)S(1)}, bf16[128,768]{1,0:T(8,128)(2,1)S(1)}, u32[]{:S(2)}, u32[]{:S(2)}) collective-permute-start(bf16[128,768]{1,0:T(8,128)(2,1)S(1)} %get-tuple-element.76.refs_4_), channel_id=1, source_target_pairs={{0,192},{4,196},{8,200},{12,204},{16,208},{20,212},{24,216},{28,22... | collective-permute-start | bytes 589832 | tf_op jit(solution)/shard_map/ppermute | solution.py:354
  113.5 7.3 %collective-permute-start.30 = (bf16[128,512]{1,0:T(8,128)(2,1)S(1)}, bf16[128,512]{1,0:T(8,128)(2,1)S(1)}, u32[]{:S(2)}, u32[]{:S(2)}) collective-permute-start(bf16[128,512]{1,0:T(8,128)(2,1)S(1)} %get-tuple-element.74), channel_id=1, source_target_pairs={{0,128},{4,132},{8,136},{12,140},{16,144},{20,148},{24,152},{28,15... | collective-permute-start | bytes 393224 | tf_op jit(solution)/shard_map/ppermute | solution.py:354
  115.2 13.1 %collective-permute-start.31 = (bf16[128,512]{1,0:T(8,128)(2,1)S(1)}, bf16[128,512]{1,0:T(8,128)(2,1)S(1)}, u32[]{:S(2)}, u32[]{:S(2)}) collective-permute-start(bf16[128,512]{1,0:T(8,128)(2,1)S(1)} %get-tuple-element.75), channel_id=1, source_target_pairs={{0,192},{4,196},{8,200},{12,204},{16,208},{20,212},{24,216},{28,22... | collective-permute-start | bytes 393224 | tf_op jit(solution)/shard_map/ppermute | solution.py:354
  120.8 13.6 %collective-permute-start.14 = (bf16[128,512]{1,0:T(8,128)(2,1)S(1)}, bf16[128,512]{1,0:T(8,128)(2,1)S(1)}, u32[]{:S(2)}, u32[]{:S(2)}) collective-permute-start(bf16[128,512]{1,0:T(8,128)(2,1)S(1)} %get-tuple-element.52), channel_id=1, source_target_pairs={{0,64},{4,68},{8,72},{12,76},{16,80},{20,84},{24,88},{28,92},{32,9... | collective-permute-start | bytes 393224 | tf_op jit(solution)/shard_map/ppermute | solution.py:354
  128.4 6.9 %collective-permute-start.15 = (bf16[128,512]{1,0:T(8,128)(2,1)S(1)}, bf16[128,512]{1,0:T(8,128)(2,1)S(1)}, u32[]{:S(2)}, u32[]{:S(2)}) collective-permute-start(bf16[128,512]{1,0:T(8,128)(2,1)S(1)} %get-tuple-element.53), channel_id=1, source_target_pairs={{0,128},{4,132},{8,136},{12,140},{16,144},{20,148},{24,152},{28,15... | collective-permute-start | bytes 393224 | tf_op jit(solution)/shard_map/ppermute | solution.py:354
  134.0 12.6 %collective-permute-start.35 = (bf16[8,32,768]{2,1,0:T(8,128)(2,1)S(1)}, bf16[8,32,768]{2,1,0:T(8,128)(2,1)S(1)}, u32[]{:S(2)}, u32[]{:S(2)}) collective-permute-start(bf16[8,32,768]{2,1,0:T(8,128)(2,1)S(1)} %get-tuple-element.78), channel_id=1, source_target_pairs={{0,4},{4,0},{8,12},{12,8},{16,20},{20,16},{24,28},{28,24},{32,36},... | collective-permute-start | bytes 1179656 | tf_op jit(solution)/shard_map/ppermute | solution.py:369
  137.0 26.0 %all-to-all-start.1 = ((bf16[64,4,512]{2,1,0:T(4,128)(2,1)}), bf16[64,4,512]{2,1,0:T(4,128)(2,1)S(1)}, u32[]{:S(2)}, u32[]{:S(2)}) async-start(bf16[64,4,512]{2,1,0:T(4,128)(2,1)} %reshape.43), calls=%async_computation.1 | async-start | bytes 524288 | tf_op jit(solution)/shard_map/all_to_all | solution.py:378
  146.8 12.3 %collective-permute-start.36 = (bf16[3,32,768]{2,1,0:T(8,128)(2,1)S(1)}, bf16[3,32,768]{2,1,0:T(8,128)(2,1)S(1)}, u32[]{:S(2)}, u32[]{:S(2)}) collective-permute-start(bf16[3,32,768]{2,1,0:T(8,128)(2,1)S(1)} %get-tuple-element.80), channel_id=1, source_target_pairs={{0,56},{4,60},{8,0},{12,4},{16,8},{20,12},{24,16},{28,20},{32,24},... | collective-permute-start | bytes 442376 | tf_op jit(solution)/shard_map/ppermute | solution.py:364
  149.6 14.3 %collective-permute-start.26 = (bf16[144,512]{1,0:T(8,128)(2,1)S(1)}, bf16[144,512]{1,0:T(8,128)(2,1)S(1)}, u32[]{:S(2)}, u32[]{:S(2)}) collective-permute-start(bf16[144,512]{1,0:T(8,128)(2,1)S(1)} %get-tuple-element.68), channel_id=1, source_target_pairs={{0,1},{1,2},{2,3},{3,0},{4,5},{5,6},{6,7},{7,4},{8,9},{9,10},{10,1... | collective-permute-start | bytes 442376 | tf_op jit(solution)/shard_map/ppermute | solution.py:373
  149.6 14.3 %collective-permute-start.27 = (bf16[144,512]{1,0:T(8,128)(2,1)S(1)}, bf16[144,512]{1,0:T(8,128)(2,1)S(1)}, u32[]{:S(2)}, u32[]{:S(2)}) collective-permute-start(bf16[144,512]{1,0:T(8,128)(2,1)S(1)} %get-tuple-element.69), channel_id=1, source_target_pairs={{0,2},{1,3},{2,0},{3,1},{4,6},{5,7},{6,4},{7,5},{8,10},{9,11},{10,... | collective-permute-start | bytes 442376 | tf_op jit(solution)/shard_map/ppermute | solution.py:373
  153.1 5.9 %collective-permute-start.37 = (bf16[2,32,768]{2,1,0:T(8,128)(2,1)S(1)}, bf16[2,32,768]{2,1,0:T(8,128)(2,1)S(1)}, u32[]{:S(2)}, u32[]{:S(2)}) collective-permute-start(bf16[2,32,768]{2,1,0:T(8,128)(2,1)S(1)} %get-tuple-element.81), channel_id=1, source_target_pairs={{0,8},{4,12},{8,16},{12,20},{16,24},{20,28},{24,32},{28,36},{32,40... | collective-permute-start | bytes 294920 | tf_op jit(solution)/shard_map/ppermute | solution.py:364
  153.1 10.8 %collective-permute-start.28 = (bf16[144,512]{1,0:T(8,128)(2,1)S(1)}, bf16[144,512]{1,0:T(8,128)(2,1)S(1)}, u32[]{:S(2)}, u32[]{:S(2)}) collective-permute-start(bf16[144,512]{1,0:T(8,128)(2,1)S(1)} %get-tuple-element.70), channel_id=1, source_target_pairs={{0,3},{1,0},{2,1},{3,2},{4,7},{5,4},{6,5},{7,6},{8,11},{9,8},{10,9... | collective-permute-start | bytes 442376 | tf_op jit(solution)/shard_map/ppermute | solution.py:373
  159.1 6.1 %collective-permute-start.38 = (bf16[32,768]{1,0:T(8,128)(2,1)S(1)}, bf16[32,768]{1,0:T(8,128)(2,1)S(1)}, u32[]{:S(2)}, u32[]{:S(2)}) collective-permute-start(bf16[32,768]{1,0:T(8,128)(2,1)S(1)} %get-tuple-element.83), channel_id=1, source_target_pairs={{0,40},{4,44},{8,48},{12,52},{16,56},{20,60},{24,0},{28,4},{32,8},... | collective-permute-start | bytes 147464 | tf_op jit(solution)/shard_map/ppermute | solution.py:364
  161.5 7.4 %collective-permute-start.39 = (bf16[32,768]{1,0:T(8,128)(2,1)S(1)}, bf16[32,768]{1,0:T(8,128)(2,1)S(1)}, u32[]{:S(2)}, u32[]{:S(2)}) collective-permute-start(bf16[32,768]{1,0:T(8,128)(2,1)S(1)} %get-tuple-element.84), channel_id=1, source_target_pairs={{0,24},{4,28},{8,32},{12,36},{16,40},{20,44},{24,48},{28,52},{32,5... | collective-permute-start | bytes 147464 | tf_op jit(solution)/shard_map/ppermute | solution.py:364
  (2 other events, 1.7 us)
where the time goes:
time: 170 us
  starting transfers between devices  100 us (59%)
  waiting for transfers between devices  43.3 us (25%)
  Pallas kernels  16 us (9%)
  local copies, waits for them, and re-layouts  7.78 us (5%)
    ppermute x17, starting transfers between devices, over_y(): return lax.ppermute(a, 'ctx', pairs)  43.6 us
    ppermute x12, starting transfers between devices, over_z(): return lax.ppermute(a, 'ctx', pairs)  26 us
    all_to_all x2, starting transfers between devices, exchange_slots(): lax.all_to_all(send.reshape(N_CTX, CAP, width), 'ctx', split_axis=0, conc...  21.8 us
    ppermute x17, waiting for transfers between devices, over_y(): return lax.ppermute(a, 'ctx', pairs)  21.1 us
    ppermute x12, waiting for transfers between devices, over_z(): return lax.ppermute(a, 'ctx', pairs)  20.2 us
    pallas_call x16, Pallas kernels, call(): pl.pallas_call(kernel, out_shape=[jax.ShapeDtypeStruct(s, d) for s, d in...  16 us
    ppermute x6, starting transfers between devices, over_x(): return lax.ppermute(a, 'fsdp', [(x, (x + shift) % NX) for x in range(NX)])  8.33 us
    unnamed x16, local copies, waits for them, and re-layouts  5.37 us
  transfers between devices with their start and end apart: 42, of which 17 were waited for; matrix products, arithmetic and copies ran while one was open for 2% of the time, Pallas kernels for 5%

commit v1 on v0

--- a/solution.py
+++ b/solution.py
@@ -37,50 +37,80 @@
     return lax.dot_general(a, b, dims, preferred_element_type=f32)
 
 
-def call(kernel, outs, in_kinds, args, scratch=(), flops=10**8, moved=2 * 10**6, name=None):
+def call(kernel, outs, in_kinds, args, scratch=(), flops=10**8, moved=2 * 10**6, name=None, out_kinds=None):
     vm = pl.BlockSpec(memory_space=pltpu.VMEM)
     sm = pl.BlockSpec(memory_space=pltpu.SMEM)
+    hbm = pl.BlockSpec(memory_space=pltpu.HBM)
+    anywhere = pl.BlockSpec(memory_space=pl.ANY)
     return pl.pallas_call(
         kernel,
         out_shape=[jax.ShapeDtypeStruct(s, d) for s, d in outs],
-        in_specs=[sm if k == "s" else vm for k in in_kinds],
-        out_specs=[vm] * len(outs),
+        in_specs=[{"s": sm, "v": vm, "h": hbm, "a": anywhere}[k] for k in in_kinds],
+        out_specs=[{"v": vm, "h": hbm}[k] for k in out_kinds or "v" * len(outs)],
         scratch_shapes=list(scratch),
-        compiler_params=pltpu.CompilerParams(vmem_limit_bytes=48 * 1024 * 1024),
-        cost_estimate=pl.CostEstimate(flops=flops, bytes_accessed=moved, transcendentals=0),
+        compiler_params=pltpu.CompilerParams(vmem_limit_bytes=16 * 1024 * 1024),
+        cost_estimate=pl.CostEstimate(flops=1000, bytes_accessed=1000, transcendentals=0),
         name=name,
     )(*args)
 
 
-def route_kernel(sc, owners, cg, mo_ref, mh_ref, send_ref):
-    me = sc[0]
-    mine = (owners[...] == me).astype(f32).astype(bf16)
+def scalars(lengths):
+    me = lax.axis_index("ctx").astype(i32)
+    x = lax.axis_index("fsdp").astype(i32)
+    return [me, me // (NZ * NC), me // NC % NZ, me % NC, x, None, None, None] + [lengths[d] for d in range(8)]
+
+
+def one_hot(condition):
+    return jnp.where(condition, 1.0, 0.0).astype(bf16)
+
+
+def route_kernel(lengths, owners, cg, send_ref, mh_ref, from_owners_ref, from_homes_ref):
+    sc = scalars(lengths)
+    me, core = sc[0], sc[3]
+    mine = one_hot(owners[...] == me)
     count = dot(mine, jnp.ones((TOK, TOK), bf16)).astype(bf16)
-    slot_src = lax.broadcasted_iota(i32, (SLOTS, N_CTX), 0) // CAP
+    slot = lax.broadcasted_iota(i32, (SLOTS, TOK), 0)
+    place = lax.broadcasted_iota(i32, (SLOTS, TOK), 1).astype(f32)
+    rank = (slot % CAP).astype(f32)
     source = lax.broadcasted_iota(i32, (SLOTS, N_CTX), 1)
-    base = dot((source < slot_src).astype(f32).astype(bf16), count)
-    here = dot((source == slot_src).astype(f32).astype(bf16), count)
-    slot = lax.broadcasted_iota(i32, (SLOTS, TOK), 0)
-    place = lax.broadcasted_iota(i32, (SLOTS, TOK), 1)
-    rank = (slot % CAP).astype(f32)
-    mo = jnp.where((base + rank == place.astype(f32)) & (rank < here), 1.0, 0.0).astype(bf16)
-    mo_ref[...] = mo
-    send_ref[...] = dot(mo, cg[...]).astype(bf16)
+    slot_row = lax.broadcasted_iota(i32, (SLOTS, N_CTX), 0)
+
+    def owned(home):
+        base = dot(one_hot(source < home), count)
+        here = dot(one_hot(source == home), count)
+        return (base + rank == place) & (rank < here)
+
+    send_ref[...] = dot(one_hot(owned(slot_row // CAP)), cg[...]).astype(bf16)
+    for_me = slot // CAP % NC == core
+    for e in range(NC):
+        sender = slot_row // (NC * CAP) * NC + (core ^ e)
+        from_homes_ref[e * SLOTS : (e + 1) * SLOTS, :] = one_hot(owned(sender) & for_me)
+
     own = jnp.broadcast_to(owners[pl.ds(me, 1), :].astype(f32), (TOK, TOK))
     earlier = lax.broadcasted_iota(i32, (TOK, TOK), 0) < lax.broadcasted_iota(i32, (TOK, TOK), 1)
     same = jnp.where((own == own.T) & earlier, 1.0, 0.0)
-    home_slot = own[0:1, :] * CAP + jnp.sum(same, axis=0, keepdims=True)
-    mh_ref[...] = jnp.where(slot.astype(f32) == home_slot, 1.0, 0.0).astype(bf16)
-
-
-def grad_home_kernel(mh, arrived, out_ref):
-    rows = dot(mh[...], arrived[...], TN).astype(bf16)
+    own_rank = jnp.sum(same, axis=0, keepdims=True).astype(i32)
+    owner = own[0:1, :].astype(i32)
+    mh_ref[...] = one_hot(slot == owner * CAP + own_rank)
+    came_slot = owner // NC * (NC * CAP) + core * CAP + own_rank
+    for e in range(NC):
+        here = (slot == came_slot) & (owner % NC == (core ^ e))
+        from_owners_ref[e * SLOTS : (e + 1) * SLOTS, :] = one_hot(here)
+
+
+def place_rows(matrix, same_core, other_core):
+    rows = dot(matrix[0:SLOTS, :], same_core[...], TN) + dot(matrix[SLOTS:, :], other_core[...], TN)
+    return rows.astype(bf16)
+
+
+def grad_home_kernel(matrix, same_core, other_core, out_ref):
+    rows = place_rows(matrix, same_core, other_core)
     for h in range(GROUP):
         out_ref[h * TOK : (h + 1) * TOK, :] = rows[:, h * HD : (h + 1) * HD]
 
 
-def place_kernel(mo, arrived, out_ref):
-    out_ref[...] = dot(mo[...], arrived[...], TN).astype(bf16)
+def place_kernel(matrix, same_core, other_core, out_ref):
+    out_ref[...] = place_rows(matrix, same_core, other_core)
 
 
 def turn(t, c, s):
@@ -91,25 +121,32 @@
     return t * c - pltpu.roll(t, HD // 2, 1) * s
 
 
-def project_kernel(sc, h0, h1, h2, h3, w, cos, sin, q_ref, kv_ref, n0, n1, n2, n3, inv_ref, held):
+def project_kernel(lengths, *refs):
+    sc = scalars(lengths)
+    hids, (w, cos, sin) = refs[0:4], refs[4:7]
+    q_ref, kv_ref, *ns, inv_ref, held, out_sems = refs[7:]
     y, x = sc[1], sc[4]
-    blocks = [h[...].astype(f32) for h in (h0, h1, h2, h3)]
+    blocks = [h[...].astype(f32) for h in hids]
     square = sum(jnp.sum(b * b, axis=1, keepdims=True) for b in blocks)
     inv = lax.rsqrt(square * (1.0 / (NX * 512)) + epsilon)
     inv_ref[...] = jnp.broadcast_to(inv, (TOK, HD))
+    for s in range(NX):
+        held[(x + NX - s) % NX] = (blocks[s] * inv).astype(bf16)
+    out_copies = [
+        pltpu.make_async_copy(held.at[(y + t) % NX], out, out_sems.at[t]) for t, out in enumerate(ns)
+    ]
+    for copy in out_copies:
+        copy.start()
     total = jnp.zeros((TOK, 768), f32)
-    for s in range(NX):
-        chunk = (x + NX - s) % NX
-        normed = (blocks[s] * inv).astype(bf16)
-        held[chunk] = normed
-        total = total + dot(normed, w[pl.ds(pl.multiple_of(chunk * 512, 512), 512), :])
-    for t, out in enumerate((n0, n1, n2, n3)):
-        out[...] = held[(y + t) % NX]
+    for k in range(NX):
+        total = total + dot(held[k], w[k * 512 : (k + 1) * 512, :])
     c, s = cos[...], sin[...]
     for h in range(GROUP):
         q_ref[h * TOK : (h + 1) * TOK, :] = turn(total[:, h * HD : (h + 1) * HD], c, s).astype(bf16)
     kv_ref[0:TOK, :] = turn(total[:, 512:640], c, s).astype(bf16)
     kv_ref[TOK:, :] = total[:, 640:768].astype(bf16)
+    for copy in out_copies:
+        copy.wait()
 
 
 def block_start(sc, row):
@@ -149,7 +186,7 @@
                 values[s, e * TOK : (e + 1) * TOK, :] = stack[i, TOK:, :]
 
 
-def pack_kernel(b0, b3, b5, three_ref, two_ref):
+def pack_kernel(b0, b3, b5, _, __, three_ref, two_ref):
     for i, b in enumerate((b0, b3, b5)):
         three_ref[i] = b[...]
         if i < 2:
@@ -162,10 +199,11 @@
     return (key_rows >= starts) & (key_rows <= rows)
 
 
-def forward_kernel(sc, *refs):
-    qs, dos, kvs = refs[0:3], refs[3:6], refs[6:12]
-    outs, stats = refs[12:15], refs[15]
-    keys, values, acc, top, total = refs[16:]
+def forward_kernel(lengths, *refs):
+    sc = scalars(lengths)
+    qs, kvs = refs[0:3], refs[3:9]
+    outs, stats = refs[9:12], refs[12]
+    keys, values, acc, top, total = refs[13:]
     load_keys(kvs, keys, values)
     stats[...] = jnp.zeros_like(stats)
     for visit in range(VISITS):
@@ -193,11 +231,16 @@
         mass = total[...]
         some = mass > 0.0
         mass = jnp.where(some, mass, 1.0)
-        out = acc[...] * (1.0 / mass)
-        outs[visit][...] = out.astype(bf16)
+        outs[visit][...] = (acc[...] * (1.0 / mass)).astype(bf16)
         stats[visit : visit + 1, :] = jnp.where(some, top[...] + jnp.log2(mass), masked)
-        delta = jnp.sum(dos[visit][...].astype(f32).T * out, axis=0, keepdims=True)
-        stats[4 + visit : 5 + visit, :] = delta
+
+
+def delta_kernel(stats, o0, o1, o2, d0, d1, d2, out_ref):
+    out_ref[0:4, :] = stats[0:4, :]
+    for visit, (o, d) in enumerate(((o0, d0), (o1, d1), (o2, d2))):
+        product = d[...].astype(f32).T * o[...].astype(f32)
+        out_ref[4 + visit : 5 + visit, :] = jnp.sum(product, axis=0, keepdims=True)
+    out_ref[7:8, :] = jnp.zeros((1, QW), f32)
 
 
 def combine_stats(sc, visit, held):
@@ -213,10 +256,11 @@
     return top + jnp.log2(mass), sum(a * b for a, b in zip(weights, deltas)), weights
 
 
-def backward_kernel(sc, *refs):
-    qs, dos, kvs, held = refs[0:3], refs[3:6], refs[6:12], refs[12:16]
-    dqs, own_ref, other_ref = refs[16:19], refs[19], refs[20]
-    keys, values, q_all, do_all, dq_acc, logs, deltas, dk, dv = refs[21:]
+def backward_kernel(lengths, *refs):
+    sc = scalars(lengths)
+    qs, dos, kvs, held, outs = refs[0:3], refs[3:6], refs[6:12], refs[12:16], refs[16:18]
+    dq_ref, returns, own_ref, other_ref = refs[18], refs[19:21], refs[21], refs[22]
+    keys, values, q_all, do_all, dq_acc, logs, deltas, dk, dv = refs[23:]
     load_keys(kvs, keys, values)
     dq_acc[...] = jnp.zeros_like(dq_acc)
     for visit in range(VISITS):
@@ -250,15 +294,18 @@
             out[s, 0:TOK, :] = (dk[half, :] * scale).astype(bf16)
             out[s, TOK:, :] = dv[half, :].astype(bf16)
 
-    for visit in range(VISITS):
-        dqs[visit][...] = (dq_acc[visit] * scale).astype(bf16)
-
-
-def context_kernel(sc, o0, o1, o2, s0, s1, s2, s3, mh, send_ref, rows):
+    dq_ref[...] = dq_acc[0] * scale
+    for visit in (1, 2):
+        returns[visit - 1][0:HD, :] = outs[visit - 1][...]
+        returns[visit - 1][HD:, :] = (dq_acc[visit] * scale).astype(bf16)
+
+
+def context_kernel(lengths, o0, o1, o2, s0, s1, s2, s3, mh, _, send_ref, rows):
+    sc = scalars(lengths)
     _, _, weights = combine_stats(sc, 0, (s0, s1, s2, s3))
     out = o0[...].astype(f32) * weights[0]
     for j, o in ((1, o1), (2, o2)):
-        out = out + jnp.where(sc[1] >= j, o[...].astype(f32), 0.0) * weights[j]
+        out = out + jnp.where(sc[1] >= j, o[0:HD, :].astype(f32), 0.0) * weights[j]
     for h in range(GROUP):
         rows[:, h * HD : (h + 1) * HD] = out[:, h * TOK : (h + 1) * TOK].T.astype(bf16)
     send_ref[...] = dot(mh[...], rows[...]).astype(bf16)
@@ -270,34 +317,43 @@
             out[i] = (own[s].astype(f32) + came[s].astype(f32)).astype(out.dtype)
 
 
-def add_near_kernel(kept, below, above, o0, o3, o5):
+def add_near_kernel(kept, below, above, *refs):
+    o0, o3, o5 = refs[-3:]
     o0[...] = kept[0] + below[0].astype(f32) + above[0].astype(f32)
     o3[...] = (kept[1] + below[1].astype(f32) + above[1].astype(f32)).astype(bf16)
     o5[...] = (kept[2] + below[2].astype(f32)).astype(bf16)
 
 
-def rows_kernel(sc, *refs):
-    parts, dqs, (cos, sin, w), hids = refs[0:3], refs[3:6], refs[6:9], refs[9:13]
-    rg_ref, keep_ref, inner_ref = refs[13], refs[14], refs[15]
-    sends = refs[16:19]
-    x = sc[4]
+def rows_kernel(lengths, *refs):
+    sc = scalars(lengths)
+    parts, dqs, (cos, sin, rg_ref) = refs[0:3], refs[3:6], refs[6:9]
     c, s = cos[...], sin[...]
-    dq = dqs[0][...].astype(f32)
+    dq = dqs[0][...]
     for j in (1, 2):
-        dq = dq + jnp.where(sc[1] >= j, dqs[j][...].astype(f32), 0.0)
+        dq = dq + jnp.where(sc[1] >= j, dqs[j][HD:, :].astype(f32), 0.0)
     for h in range(GROUP):
         rg_ref[:, h * HD : (h + 1) * HD] = turn_back(dq[:, h * TOK : (h + 1) * TOK].T, c, s).astype(bf16)
     dkv = sum(p[...].astype(f32) for p in parts)
     rg_ref[:, 512:640] = turn_back(dkv[0:TOK], c, s).astype(bf16)
     rg_ref[:, 640:768] = dkv[TOK:].astype(bf16)
+
+
+def spread_kernel(lengths, *refs):
+    sc = scalars(lengths)
+    rg_ref, w, hids = refs[0], refs[1], refs[2:6]
+    keep_ref, inner_ref, sends = refs[9], refs[10], refs[11:14]
+    kept, sem = refs[14:]
+    x = sc[4]
     rg = rg_ref[...]
     inner = jnp.zeros((TOK, 1), f32)
     for t in range(NX):
-        chunk = (x + t) % NX
-        part = dot(rg, w[pl.ds(pl.multiple_of(chunk * 512, 512), 512), :], NT)
+        first = pl.multiple_of((x + t) % NX * 512, 512)
+        part = dot(rg, w[pl.ds(first, 512), :], NT)
         inner = inner + jnp.sum(part * hids[-t % NX][...].astype(f32), axis=1, keepdims=True)
         if t == 0:
-            keep_ref[...] = part
+            kept[...] = part
+            keep_copy = pltpu.make_async_copy(kept, keep_ref, sem)
+            keep_copy.start()
         else:
             sends[t - 1][0:TOK, :] = part.astype(bf16)
     row = jnp.broadcast_to(inner, (TOK, TOK)).T[0:16, :]
@@ -307,6 +363,7 @@
     both = jnp.where(line == 0, high, jnp.where(line == 1, row - high, 0.0)).astype(bf16)
     for out in sends:
         out[TOK:, :] = jnp.concatenate([both, jnp.zeros((16, 384), bf16)], axis=1)
+    keep_copy.wait()
 
 
 def input_kernel(keep, inner, r1, r2, r3, inv_ref, hid, out_ref):
@@ -321,12 +378,17 @@
     out_ref[...] = inv * total - hid[...].astype(f32) * (inv * inv * inv * column * (1.0 / (NX * 512)))
 
 
-def weight_kernel(sc, *refs):
+def weight_kernel(lengths, *refs):
+    sc = scalars(lengths)
     ns, rgs, own_ref, other_ref = refs[0:4], refs[4:8], refs[8], refs[9]
-    n_all, rg_all, product = refs[10:]
+    n_all, rg_all, product, sems = refs[10:]
+    copies = [pltpu.make_async_copy(ns[t], n_all.at[pl.ds(t * TOK, TOK), :], sems.at[t]) for t in range(NY)]
+    for copy in copies:
+        copy.start()
     for t in range(NY):
-        n_all[t * TOK : (t + 1) * TOK, :] = ns[t][...]
         rg_all[t * TOK : (t + 1) * TOK, :] = rgs[t][...]
+    for copy in copies:
+        copy.wait()
     product[...] = dot(n_all[...], rg_all[...], TN)
     z, core = sc[2], sc[3]
     for s in range(NZ):
@@ -375,11 +437,14 @@
 
 def exchange_slots(send):
     width = send.shape[1]
-    came = lax.all_to_all(send.reshape(N_CTX, CAP, width), "ctx", split_axis=0, concat_axis=0, tiled=True)
+    groups = [[index_of(y, z, c) for y in range(NY) for z in range(NZ)] for c in range(NC)]
+    came = lax.all_to_all(
+        send.reshape(NY * NZ, NC * CAP, width), "ctx", split_axis=0, concat_axis=0, tiled=True, axis_index_groups=groups
+    )
     return came.reshape(SLOTS, width)
 
 
-def reduce_cores_and_z(own, other, name):
+def reduce_cores_and_z(own, other, name, after=()):
     shape = own.shape[1:]
     came = over_c(other)
     kept, below, above = call(
@@ -393,34 +458,29 @@
     o0, o3, o5 = call(
         add_near_kernel,
         [(shape, f32), (shape, bf16), (shape, bf16)],
-        "vvv",
-        (kept, below, above),
+        "vvv" + "a" * len(after),
+        (kept, below, above, *after),
         name="add_near_" + name,
     )
     return o0, over_z(o3, -3), over_z(o5, 3)
 
 
 def shards(hidden, w, doc_lengths, owners, context_grad):
-    me = lax.axis_index("ctx").astype(i32)
-    x = lax.axis_index("fsdp").astype(i32)
-    zero = jnp.zeros((), i32)
-    sc = jnp.concatenate(
-        [jnp.stack([me, me // (NZ * NC), me // NC % NZ, me % NC, x, zero, zero, zero]), doc_lengths.astype(i32)]
-    )
+    lengths = doc_lengths.astype(i32)
     hids = [hidden] + [over_x(hidden, s) for s in range(1, NX)]
 
-    mo, mh, send = call(
+    grad_send, mh, from_owners, from_homes = call(
         route_kernel,
-        [((SLOTS, TOK), bf16), ((SLOTS, TOK), bf16), ((SLOTS, QW), bf16)],
+        [((SLOTS, QW), bf16), ((SLOTS, TOK), bf16), ((NC * SLOTS, TOK), bf16), ((NC * SLOTS, TOK), bf16)],
         "svv",
-        (sc, owners.reshape(N_CTX, TOK), context_grad),
+        (lengths, owners.reshape(N_CTX, TOK), context_grad),
         name="route",
     )
-    arrived = exchange_slots(send)
-
-    home = me * TOK + jnp.arange(TOK, dtype=i32)
+    arrived = exchange_slots(grad_send)
+
+    home = lax.axis_index("ctx").astype(i32) * TOK + jnp.arange(TOK, dtype=i32)
     docs = jnp.arange(8, dtype=i32)
-    doc_starts = jnp.sum(jnp.where(docs[:, None] > docs[None, :], doc_lengths[None, :], 0), axis=1)
+    doc_starts = jnp.sum(jnp.where(docs[:, None] > docs[None, :], lengths[None, :], 0), axis=1)
     start = jnp.max(jnp.where(home[:, None] >= doc_starts[None, :], doc_starts[None, :], 0), axis=1)
     frequency = rope_base ** (-(2.0 * jnp.arange(HD // 2, dtype=f32)) / HD)
     angles = (home - start).astype(f32)[:, None] * frequency[None, :]
@@ -431,32 +491,35 @@
         project_kernel,
         [((QW, HD), bf16), ((2 * TOK, HD), bf16)] + [((TOK, 512), bf16)] * 4 + [((TOK, HD), f32)],
         "svvvvvvv",
-        (sc, *hids, w, cos, sin),
-        scratch=[pltpu.VMEM((NX, TOK, 512), bf16)],
+        (lengths, *hids, w, cos, sin),
+        scratch=[pltpu.VMEM((NX, TOK, 512), bf16), pltpu.SemaphoreType.DMA((NX,))],
+        out_kinds="vvhhhhv",
         flops=4 * 10**8,
         moved=4 * 10**6,
         name="project",
     )
+    qs = [q, over_y(q, -1, False), over_y(q, -2, False)]
     three, two = call(
         pack_kernel,
         [((3, 2 * TOK, HD), bf16), ((2, 2 * TOK, HD), bf16)],
-        "vvv",
-        (kv, over_z(kv, 3), over_z(kv, -3)),
+        "vvvaa",
+        (kv, over_z(kv, 3), over_z(kv, -3), qs[1], qs[2]),
         name="pack",
     )
     kv_own = [three, over_z(three, 1), over_z(two, -1)]
-    qs = [q, over_y(q, -1, False), over_y(q, -2, False)]
     kvs = kv_own + [over_c(a) for a in kv_own]
     ns = [n0] + [over_y(n, t) for t, n in ((1, n1), (2, n2), (3, n3))]
 
-    (do,) = call(grad_home_kernel, [((QW, HD), bf16)], "vv", (mh, arrived), name="grad_home")
+    (do,) = call(
+        grad_home_kernel, [((QW, HD), bf16)], "vvv", (from_owners, arrived, over_c(arrived)), name="grad_home"
+    )
     dos = [do, over_y(do, -1, False), over_y(do, -2, False)]
 
     *outs, stats = call(
         forward_kernel,
         [((HD, QW), bf16)] * 3 + [((8, QW), f32)],
-        "s" + "v" * 12,
-        (sc, *qs, *dos, *kvs),
+        "s" + "v" * 9,
+        (lengths, *qs, *kvs),
         scratch=[
             pltpu.VMEM((NZ, 2 * TOK, HD), bf16),
             pltpu.VMEM((NZ, 2 * TOK, HD), bf16),
@@ -467,14 +530,14 @@
         flops=3 * 10**9,
         name="forward",
     )
+    (stats,) = call(delta_kernel, [((8, QW), f32)], "v" * 7, (stats, *outs, *dos), name="delta")
     held = [stats] + [over_y(stats, -t) for t in (1, 2, 3)]
-    o_came = [outs[0], over_y(outs[1], 1, False), over_y(outs[2], 2, False)]
-
-    *dqs, dkv_own, dkv_other = call(
+
+    dq, back1, back2, dkv_own, dkv_other = call(
         backward_kernel,
-        [((HD, QW), bf16)] * 3 + [((NZ, 2 * TOK, HD), bf16)] * 2,
-        "s" + "v" * 16,
-        (sc, *qs, *dos, *kvs, *held),
+        [((HD, QW), f32)] + [((2 * HD, QW), bf16)] * 2 + [((NZ, 2 * TOK, HD), bf16)] * 2,
+        "s" + "v" * 18,
+        (lengths, *qs, *dos, *kvs, *held, outs[1], outs[2]),
         scratch=[
             pltpu.VMEM((NZ, 2 * TOK, HD), bf16),
             pltpu.VMEM((NZ, 2 * TOK, HD), bf16),
@@ -489,39 +552,47 @@
         flops=5 * 10**9,
         name="backward",
     )
+    back1, back2 = over_y(back1, 1, False), over_y(back2, 2, False)
+
     dkv_home = reduce_cores_and_z(dkv_own, dkv_other, "dkv")
-    dq_came = [dqs[0], over_y(dqs[1], 1, False), over_y(dqs[2], 2, False)]
-
+    (rg,) = call(
+        rows_kernel,
+        [((TOK, 768), bf16)],
+        "s" + "v" * 8,
+        (lengths, *dkv_home, dq, back1, back2, cos, sin),
+        name="rows",
+    )
+    rgs = [rg] + [over_y(rg, t) for t in (1, 2, 3)]
+    keep, inner, *sends = call(
+        spread_kernel,
+        [((TOK, 512), f32), ((8, TOK), f32)] + [((TOK + 16, 512), bf16)] * 3,
+        "svvvvvvaaa",
+        (lengths, rg, w, *hids, *ns[1:]),
+        scratch=[pltpu.VMEM((TOK, 512), f32), pltpu.SemaphoreType.DMA],
+        name="spread",
+        out_kinds="hvvvv",
+    )
     (context_send,) = call(
         context_kernel,
         [((SLOTS, QW), bf16)],
-        "s" + "v" * 8,
-        (sc, *o_came, *held, mh),
+        "s" + "v" * 8 + "a",
+        (lengths, outs[0], back1, back2, *held, mh, inner),
         scratch=[pltpu.VMEM((TOK, QW), bf16)],
         name="context",
     )
     context_came = exchange_slots(context_send)
 
-    rg, keep, inner, *sends = call(
-        rows_kernel,
-        [((TOK, 768), bf16), ((TOK, 512), f32), ((8, TOK), f32)] + [((TOK + 16, 512), bf16)] * 3,
-        "s" + "v" * 13,
-        (sc, *dkv_home, *dq_came, cos, sin, w, *hids),
-        flops=4 * 10**8,
-        moved=4 * 10**6,
-        name="rows",
-    )
-    rgs = [rg] + [over_y(rg, t) for t in (1, 2, 3)]
     totals = [over_x(a, t) for t, a in zip((1, 2, 3), sends)]
     w_own, w_other = call(
         weight_kernel,
         [((NZ, 32, 768), bf16)] * 2,
-        "s" + "v" * 8,
-        (sc, *ns, *rgs),
+        "s" + "h" * 4 + "v" * 4,
+        (lengths, *ns, *rgs),
         scratch=[
             pltpu.VMEM((NY * TOK, 512), bf16),
             pltpu.VMEM((NY * TOK, 768), bf16),
             pltpu.VMEM((512, 768), f32),
+            pltpu.SemaphoreType.DMA((NY,)),
         ],
         flops=4 * 10**8,
         name="weight",
@@ -534,7 +605,9 @@
         (keep, inner, *totals, inv, hidden),
         name="input",
     )
-    (context,) = call(place_kernel, [((TOK, QW), bf16)], "vv", (mo, context_came), name="place")
+    (context,) = call(
+        place_kernel, [((TOK, QW), bf16)], "vvv", (from_homes, context_came, over_c(context_came)), name="place"
+    )
     (weight_grad,) = call(sum_kernel, [((32, 768), f32)], "vvv", w_home, name="sum_weight")
     return context, input_grad, weight_grad
 

time: 170 us -> 151 us (0.89); the launches traced: 170 us -> 153 us
  starting transfers between devices: 100 us -> 83.9 us
  Pallas kernels: 16 us -> 18.8 us
  local copies, waits for them, and re-layouts: 7.78 us -> 5.78 us
    ppermute x17 -> x15, starting transfers between devices: 43.6 us -> 27.1 us  [over_y(): return lax.ppermute(a, 'ctx', pairs)]
    ppermute x17 -> x15, waiting for transfers between devices: 21.1 us -> 6.38 us  [over_y(): return lax.ppermute(a, 'ctx', pairs)]
    all_to_all x2, waiting for transfers between devices: 0.01 us -> 8.59 us  [exchange_slots(): lax.all_to_all(send.reshape(NY * NZ, NC * CAP, width), 'ctx', split_axis=...]
    ppermute x12, waiting for transfers between devices: 20.2 us -> 24.5 us  [over_z(): return lax.ppermute(a, 'ctx', pairs)]
    pallas_call x16 -> x18, Pallas kernels: 16 us -> 18.8 us  [call(): pl.pallas_call(kernel, out_shape=[jax.ShapeDtypeStruct(s, d) for s, d in...]
    ppermute x6, waiting for transfers between devices: 0.02 us -> 2.64 us  [over_x(): return lax.ppermute(a, 'fsdp', [(x, (x + shift) % NX) for x in range(NX)])]
    ppermute x5 -> x7, waiting for transfers between devices: 1.91 us -> 0.02 us  [over_c(): return lax.ppermute(a, 'ctx', pairs)]
    unnamed x16 -> x20, local copies, waits for them, and re-layouts: 5.37 us -> 5.78 us
  transfers between devices with their start and end apart: 42 -> 42, of which waited for: 17 -> 15; matrix products, arithmetic and copies ran while one was open for 2% -> 1% of each run, Pallas kernels for 5% -> 10%
where the time goes in v1:
time: 151 us; the launch traced here: 153 us
  starting transfers between devices  83.9 us (56%)
  waiting for transfers between devices  42.1 us (28%)
  Pallas kernels  18.8 us (12%)
  local copies, waits for them, and re-layouts  5.78 us (4%)
    ppermute x12, starting transfers between devices, over_z(): return lax.ppermute(a, 'ctx', pairs)  27.1 us
    ppermute x15, starting transfers between devices, over_y(): return lax.ppermute(a, 'ctx', pairs)  27.1 us
    ppermute x12, waiting for transfers between devices, over_z(): return lax.ppermute(a, 'ctx', pairs)  24.5 us
    all_to_all x2, starting transfers between devices, exchange_slots(): lax.all_to_all(send.reshape(NY * NZ, NC * CAP, width), 'ctx', split_axis=...  20.6 us
    pallas_call x18, Pallas kernels, call(): pl.pallas_call(kernel, out_shape=[jax.ShapeDtypeStruct(s, d) for s, d in...  18.8 us
    all_to_all x2, waiting for transfers between devices, exchange_slots(): lax.all_to_all(send.reshape(NY * NZ, NC * CAP, width), 'ctx', split_axis=...  8.59 us
    ppermute x6, starting transfers between devices, over_x(): return lax.ppermute(a, 'fsdp', [(x, (x + shift) % NX) for x in range(NX)])  8.05 us
    ppermute x15, waiting for transfers between devices, over_y(): return lax.ppermute(a, 'ctx', pairs)  6.38 us
  transfers between devices with their start and end apart: 42, of which 15 were waited for; matrix products, arithmetic and copies ran while one was open for 1% of the time, Pallas kernels for 10%

profile of v1, /device:TPU:2, one launch (start us, length us, event | category | flops | bytes accessed | tf_op | source)
XLA Modules:
  0.0 152.9 jit_solution(15611238948168292878)
XLA Ops:
  0.6 2.3 %collective-permute-start.2 = (bf16[128,512]{1,0:T(8,128)(2,1)}, bf16[128,512]{1,0:T(8,128)(2,1)S(1)}, u32[]{:S(2)}, u32[]{:S(2)}) collective-permute-start(bf16[128,512]{1,0:T(8,128)(2,1)} %hid.1), channel_id=1, source_target_pairs={{0,3},{1,0},{2,1},{3,2},{4,7},{5,4},{6,5},{7,6},{8,11},{9,8},{10,9... | collective-permute-start | bytes 393224 | tf_op jit(solution)/shard_map/ppermute | solution.py:435
  3.7 1.8 %collective-permute-start = (bf16[128,512]{1,0:T(8,128)(2,1)}, bf16[128,512]{1,0:T(8,128)(2,1)S(1)}, u32[]{:S(2)}, u32[]{:S(2)}) collective-permute-start(bf16[128,512]{1,0:T(8,128)(2,1)} %hid.1), channel_id=1, source_target_pairs={{0,1},{1,2},{2,3},{3,0},{4,5},{5,6},{6,7},{7,4},{8,9},{9,10},{10,1... | collective-permute-start | bytes 393224 | tf_op jit(solution)/shard_map/ppermute | solution.py:435
  5.5 0.9 copy-done.4
  7.8 1.7 %route.1 = (bf16[256,512]{1,0:T(8,128)(2,1)}, bf16[256,128]{1,0:T(8,128)(2,1)S(1)}, bf16[512,128]{1,0:T(8,128)(2,1)S(1)}, bf16[512,128]{1,0:T(8,128)(2,1)S(1)}) custom-call(s32[8]{0:T(128)S(1)} %copy-done.5, s32[64,128]{1,0:T(8,128)S(1)} %bitcast.9, bf16[128,512]{1,0:T(8,128)(2,1)S(1)} %copy-done.4), custom_call_target="tpu_custom_call" | custom-call | flops 1000 | bytes 1000 | tf_op jit(solution)/shard_map/route/pallas_call | solution.py:45
  9.5 11.5 %all-to-all-start = ((bf16[32,8,512]{2,1,0:T(8,128)(2,1)}), bf16[32,8,512]{2,1,0:T(8,128)(2,1)S(1)}, u32[]{:S(2)}, u32[]{:S(2)}) async-start(bf16[32,8,512]{2,1,0:T(8,128)(2,1)} %bitcast.1), calls=%async_computation | async-start | bytes 524288 | tf_op jit(solution)/shard_map/all_to_all | solution.py:441
  22.4 1.9 %copy-done = bf16[2048,768]{1,0:T(8,128)(2,1)S(1)} copy-done((bf16[2048,768]{1,0:T(8,128)(2,1)S(1)}, bf16[2048,768]{1,0:T(8,128)(2,1)}, u32[]{:S(2)}) %copy-start) | copy-done | bytes 3145752
  24.3 0.9 copy-done.2
  25.8 2.2 %project.1 = (bf16[512,128]{1,0:T(8,128)(2,1)S(1)}, bf16[256,128]{1,0:T(8,128)(2,1)S(1)}, bf16[128,512]{1,0:T(8,128)(2,1)S(1)}, bf16[128,512]{1,0:T(8,128)(2,1)S...) custom-call(s32[8]{0:T(128)S(1)} %copy-done.6, ...), custom_call_target="tpu_custom_call" | custom-call | flops 1000 | bytes 1000 | tf_op jit(solution)/shard_map/project/pallas_call | solution.py:45
  28.0 1.3 collective-permute-start.4
  29.3 1.3 collective-permute-start.3
  30.6 4.9 %collective-permute-start.6 = (bf16[256,128]{1,0:T(8,128)(2,1)S(1)}, bf16[256,128]{1,0:T(8,128)(2,1)S(1)}, u32[]{:S(2)}, u32[]{:S(2)}) collective-permute-start(bf16[256,128]{1,0:T(8,128)(2,1)S(1)} %get-tuple-element.46.b0), channel_id=1, source_target_pairs={{0,40},{4,44},{8,48},{12,52},{16,56},{20,60},{24,0},{28,4},{32,8},... | collective-permute-start | bytes 196616 | tf_op jit(solution)/shard_map/ppermute | solution.py:426
  35.5 3.2 %collective-permute-done.6.b5 = bf16[256,128]{1,0:T(8,128)(2,1)S(1)} collective-permute-done((bf16[256,128]{1,0:T(8,128)(2,1)S(1)}, bf16[256,128]{1,0:T(8,128)(2,1)S(1)}, u32[]{:S(2)}, u32[]{:S(2)}) %collective-permute-start.6) | collective-permute-done | bytes 65568 | tf_op jit(solution)/shard_map/ppermute | solution.py:426
  38.7 5.1 %collective-permute-done.5.b3 = bf16[256,128]{1,0:T(8,128)(2,1)S(1)} collective-permute-done((bf16[256,128]{1,0:T(8,128)(2,1)S(1)}, bf16[256,128]{1,0:T(8,128)(2,1)S(1)}, u32[]{:S(2)}, u32[]{:S(2)}) %collective-permute-start.5) | collective-permute-done | bytes 65568 | tf_op jit(solution)/shard_map/ppermute | solution.py:426
  44.0 3.1 %collective-permute-start.8 = (bf16[2,256,128]{2,1,0:T(8,128)(2,1)S(1)}, bf16[2,256,128]{2,1,0:T(8,128)(2,1)S(1)}, u32[]{:S(2)}, u32[]{:S(2)}) collective-permute-start(bf16[2,256,128]{2,1,0:T(8,128)(2,1)S(1)} %get-tuple-element.48), channel_id=1, source_target_pairs={{0,56},{4,60},{8,0},{12,4},{16,8},{20,12},{24,16},{28,20},{32,24},... | collective-permute-start | bytes 393224 | tf_op jit(solution)/shard_map/ppermute | solution.py:426
  47.4 3.4 %collective-permute-done.7.refs_4_.refs_7_ = bf16[3,256,128]{2,1,0:T(8,128)(2,1)S(1)} collective-permute-done((bf16[3,256,128]{2,1,0:T(8,128)(2,1)S(1)}, bf16[3,256,128]{2,1,0:T(8,128)(2,1)S(1)}, u32[]{:S(2)}, u32[]{:S(2)}) %collective-permute-start.7) | collective-permute-done | bytes 196640 | tf_op jit(solution)/shard_map/ppermute | solution.py:426
  51.6 1.3 collective-permute-start.14
  52.9 1.3 collective-permute-start.13
  54.2 2.3 %forward.1 = (bf16[128,512]{1,0:T(8,128)(2,1)S(1)}, bf16[128,512]{1,0:T(8,128)(2,1)S(1)}, bf16[128,512]{1,0:T(8,128)(2,1)S(1)}, f32[8,512]{1,0:T(8,128)S(1)}) custom-call(s32[8]{0:T(128)S(1)} %copy-done.7, bf16[512,128]{1,0:T(8,128)(2,1)S(1)} %get-tuple-element.45.refs_0_, bf16[512,128]{1,0:T(8,128)(2,1)S(1)} %collective-permute-done.3._.refs_1_, ...), custom_call_target="tpu_custom_call" | custom-call | flops 1000 | bytes 1000 | tf_op jit(solution)/shard_map/forward/pallas_call | solution.py:45
  56.5 4.4 %collective-permute-done.14.d2.refs_5_ = bf16[512,128]{1,0:T(8,128)(2,1)S(1)} collective-permute-done((bf16[512,128]{1,0:T(8,128)(2,1)S(1)}, bf16[512,128]{1,0:T(8,128)(2,1)S(1)}, u32[]{:S(2)}, u32[]{:S(2)}) %collective-permute-start.14) | collective-permute-done | bytes 131104 | tf_op jit(solution)/shard_map/ppermute | solution.py:416
  61.1 4.9 %collective-permute-start.17 = (f32[8,512]{1,0:T(8,128)S(1)}, f32[8,512]{1,0:T(8,128)S(1)}, u32[]{:S(2)}, u32[]{:S(2)}) collective-permute-start(f32[8,512]{1,0:T(8,128)S(1)} %delta.1.refs_12_.s0), channel_id=1, source_target_pairs={{0,64},{4,68},{8,72},{12,76},{16,80},{20,84},{24,88},{28,92},{32,9... | collective-permute-start | bytes 49160 | tf_op jit(solution)/shard_map/ppermute | solution.py:416
  66.8 2.5 %collective-permute-start.15 = (f32[8,512]{1,0:T(8,128)S(1)}, f32[8,512]{1,0:T(8,128)S(1)}, u32[]{:S(2)}, u32[]{:S(2)}) collective-permute-start(f32[8,512]{1,0:T(8,128)S(1)} %delta.1.refs_12_.s0), channel_id=1, source_target_pairs={{0,192},{4,196},{8,200},{12,204},{16,208},{20,212},{24,216},{28,22... | collective-permute-start | bytes 49160 | tf_op jit(solution)/shard_map/ppermute | solution.py:416
  69.3 2.0 %collective-permute-done.16.refs_14_.s2 = f32[8,512]{1,0:T(8,128)S(1)} collective-permute-done((f32[8,512]{1,0:T(8,128)S(1)}, f32[8,512]{1,0:T(8,128)S(1)}, u32[]{:S(2)}, u32[]{:S(2)}) %collective-permute-start.16) | collective-permute-done | bytes 16416 | tf_op jit(solution)/shard_map/ppermute | solution.py:416
  71.3 2.7 %backward.1 = (f32[128,512]{1,0:T(8,128)S(1)}, bf16[256,512]{1,0:T(8,128)(2,1)S(1)}, bf16[256,512]{1,0:T(8,128)(2,1)S(1)}, bf16[8,256,128]{2,1,0:T(8,128)(2,1)S(1)}, bf16[8,256,128]{2,1,0:T(8,128)(2,1)S(1)}) custom-call(s32[8]{0:T(128)S(1)} %copy-done.7, bf16[512,128]{1,0:T(8,128)(2,1)S(1)} %get-tuple-element.45.refs_0_, ...), custom_call_target="tpu_custom_call" | custom-call | flops 1000 | bytes 1000 | tf_op jit(solution)/shard_map/backward/pallas_call | solution.py:45
  74.1 2.0 %collective-permute-start.18 = (bf16[256,512]{1,0:T(8,128)(2,1)S(1)}, bf16[256,512]{1,0:T(8,128)(2,1)S(1)}, u32[]{:S(2)}, u32[]{:S(2)}) collective-permute-start(bf16[256,512]{1,0:T(8,128)(2,1)S(1)} %get-tuple-element.55), channel_id=1, source_target_pairs={{0,64},{4,68},{8,72},{12,76},{16,80},{20,84},{24,88},{28,92},{32,9... | collective-permute-start | bytes 786440 | tf_op jit(solution)/shard_map/ppermute | solution.py:416
  76.1 7.7 %collective-permute-start.19 = (bf16[256,512]{1,0:T(8,128)(2,1)S(1)}, bf16[256,512]{1,0:T(8,128)(2,1)S(1)}, u32[]{:S(2)}, u32[]{:S(2)}) collective-permute-start(bf16[256,512]{1,0:T(8,128)(2,1)S(1)} %get-tuple-element.56), channel_id=1, source_target_pairs={{0,128},{4,132},{8,136},{12,140},{16,144},{20,148},{24,152},{28,15... | collective-permute-start | bytes 786440 | tf_op jit(solution)/shard_map/ppermute | solution.py:416
  83.9 8.7 %collective-permute-start.21 = (bf16[3,256,128]{2,1,0:T(8,128)(2,1)S(1)}, bf16[3,256,128]{2,1,0:T(8,128)(2,1)S(1)}, u32[]{:S(2)}, u32[]{:S(2)}) collective-permute-start(bf16[3,256,128]{2,1,0:T(8,128)(2,1)S(1)} %get-tuple-element.61), channel_id=1, source_target_pairs={{0,56},{4,60},{8,0},{12,4},{16,8},{20,12},{24,16},{28,20},{32,24},... | collective-permute-start | bytes 589832 | tf_op jit(solution)/shard_map/ppermute | solution.py:426
  92.6 6.5 %collective-permute-done.22.above = bf16[2,256,128]{2,1,0:T(8,128)(2,1)S(1)} collective-permute-done((bf16[2,256,128]{2,1,0:T(8,128)(2,1)S(1)}, bf16[2,256,128]{2,1,0:T(8,128)(2,1)S(1)}, u32[]{:S(2)}, u32[]{:S(2)}) %collective-permute-start.22) | collective-permute-done | bytes 131104 | tf_op jit(solution)/shard_map/ppermute | solution.py:426
  99.3 3.8 %collective-permute-start.24 = (bf16[256,128]{1,0:T(8,128)(2,1)S(1)}, bf16[256,128]{1,0:T(8,128)(2,1)S(1)}, u32[]{:S(2)}, u32[]{:S(2)}) collective-permute-start(bf16[256,128]{1,0:T(8,128)(2,1)S(1)} %get-tuple-element.65), channel_id=1, source_target_pairs={{0,24},{4,28},{8,32},{12,36},{16,40},{20,44},{24,48},{28,52},{32,5... | collective-permute-start | bytes 196616 | tf_op jit(solution)/shard_map/ppermute | solution.py:426
  103.1 2.0 %collective-permute-start.27 = (bf16[128,512]{1,0:T(8,128)(2,1)S(1)}, bf16[128,512]{1,0:T(8,128)(2,1)S(1)}, u32[]{:S(2)}, u32[]{:S(2)}) collective-permute-start(bf16[128,512]{1,0:T(8,128)(2,1)S(1)} %get-tuple-element.69), channel_id=1, source_target_pairs={{0,192},{4,196},{8,200},{12,204},{16,208},{20,212},{24,216},{28,22... | collective-permute-start | bytes 393224 | tf_op jit(solution)/shard_map/ppermute | solution.py:416
  105.7 1.9 %collective-permute-done.24.refs_2_ = bf16[256,128]{1,0:T(8,128)(2,1)S(1)} collective-permute-done((bf16[256,128]{1,0:T(8,128)(2,1)S(1)}, bf16[256,128]{1,0:T(8,128)(2,1)S(1)}, u32[]{:S(2)}, u32[]{:S(2)}) %collective-permute-start.24) | collective-permute-done | bytes 65568 | tf_op jit(solution)/shard_map/ppermute | solution.py:426
  107.6 0.9 rows.1.refs_0_.refs_4_
  108.6 1.4 collective-permute-start.33
  110.7 2.1 %spread.1 = (f32[128,512]{1,0:T(8,128)S(1)}, f32[8,128]{1,0:T(8,128)S(1)}, bf16[144,512]{1,0:T(8,128)(2,1)S(1)}, bf16[144,512]{1,0:T(8,128)(2,1)S(1)}, bf16[144,512]{1,0:T(8,128)(2,1)S(1)}) custom-call(s32[8]{0:T(128)S(1)} %copy-done.7, bf16[128,768]{1,0:T(8,128)(2,1)S(1)} %rows.1.refs_0_.refs_4_, bf16[2048,768]{1,0:T(8,128)(2,1)S(1)} %copy-done.1, ...), custom_call_target="tpu_custom_call" | custom-call | flops 1000 | bytes 1000 | tf_op jit(solution)/shard_map/spread/pallas_call | solution.py:45
  112.8 1.7 %context.1 = bf16[256,512]{1,0:T(8,128)(2,1)} custom-call(s32[8]{0:T(128)S(1)} %copy-done.7, bf16[128,512]{1,0:T(8,128)(2,1)S(1)} %get-tuple-element.49.o0, bf16[256,512]{1,0:T(8,128)(2,1)S(1)} %collective-permute-done.18.refs_4_.o1, bf16[256,512]{1,0:T(8,128)(2,1)S(1)} %collective-permute-done.19.refs_5_.o2, f32[8,512]{1,0:T(8,128)S(1)} %delta.1.refs_12_.s0, ...), custom_call_target="tpu_custom_call" | custom-call | flops 1000 | bytes 1000 | tf_op jit(solution)/shard_map/context/pallas_call | solution.py:45
  114.4 9.1 %all-to-all-start.1 = ((bf16[32,8,512]{2,1,0:T(8,128)(2,1)}), bf16[32,8,512]{2,1,0:T(8,128)(2,1)S(1)}, u32[]{:S(2)}, u32[]{:S(2)}) async-start(bf16[32,8,512]{2,1,0:T(8,128)(2,1)} %bitcast.3), calls=%async_computation.1 | async-start | bytes 524288 | tf_op jit(solution)/shard_map/all_to_all | solution.py:441
  123.6 2.0 %weight.1 = (bf16[8,32,768]{2,1,0:T(8,128)(2,1)S(1)}, bf16[8,32,768]{2,1,0:T(8,128)(2,1)S(1)}) custom-call(s32[8]{0:T(128)S(1)} %copy-done.7, bf16[128,512]{1,0:T(8,128)(2,1)S(1)} %get-tuple-element.76.refs_0_, bf16[128,512]{1,0:T(8,128)(2,1)S(1)} %collective-permute-done.25.refs_6_.refs_1_, bf16[128,512]{1,0:T(8,128)(2,1)S(1)} %collective-permute-done.26.refs_7_.refs_2_, ...), custom_call_target="tpu_custom_call" | custom-call | flops 1000 | bytes 1000 | tf_op jit(solution)/shard_map/weight/pallas_call | solution.py:45
  125.7 8.6 %all-to-all-done.1 = bf16[32,8,512]{2,1,0:T(8,128)(2,1)S(1)} async-done(((bf16[32,8,512]{2,1,0:T(8,128)(2,1)}), bf16[32,8,512]{2,1,0:T(8,128)(2,1)S(1)}, u32[]{:S(2)}, u32[]{:S(2)}) %all-to-all-start.1) | async-done | bytes 262176 | tf_op jit(solution)/shard_map/all_to_all | solution.py:441
  134.4 1.9 %collective-permute-start.37 = (bf16[2,32,768]{2,1,0:T(8,128)(2,1)S(1)}, bf16[2,32,768]{2,1,0:T(8,128)(2,1)S(1)}, u32[]{:S(2)}, u32[]{:S(2)}) collective-permute-start(bf16[2,32,768]{2,1,0:T(8,128)(2,1)S(1)} %get-tuple-element.81), channel_id=1, source_target_pairs={{0,8},{4,12},{8,16},{12,20},{16,24},{20,28},{24,32},{28,36},{32,40... | collective-permute-start | bytes 294920 | tf_op jit(solution)/shard_map/ppermute | solution.py:426
  136.3 1.4 collective-permute-start.36
  138.1 1.9 %collective-permute-start.30 = (bf16[144,512]{1,0:T(8,128)(2,1)S(1)}, bf16[144,512]{1,0:T(8,128)(2,1)S(1)}, u32[]{:S(2)}, u32[]{:S(2)}) collective-permute-start(bf16[144,512]{1,0:T(8,128)(2,1)S(1)} %get-tuple-element.73), channel_id=1, source_target_pairs={{0,2},{1,3},{2,0},{3,1},{4,6},{5,7},{6,4},{7,5},{8,10},{9,11},{10,... | collective-permute-start | bytes 442376 | tf_op jit(solution)/shard_map/ppermute | solution.py:435
  140.0 0.9 collective-permute-done.37.above
  140.9 0.9 collective-permute-start.31
  142.4 1.5 %collective-permute-start.38 = (bf16[32,768]{1,0:T(8,128)(2,1)S(1)}, bf16[32,768]{1,0:T(8,128)(2,1)S(1)}, u32[]{:S(2)}, u32[]{:S(2)}) collective-permute-start(bf16[32,768]{1,0:T(8,128)(2,1)S(1)} %get-tuple-element.83), channel_id=1, source_target_pairs={{0,40},{4,44},{8,48},{12,52},{16,56},{20,60},{24,0},{28,4},{32,8},... | collective-permute-start | bytes 147464 | tf_op jit(solution)/shard_map/ppermute | solution.py:426
  144.6 1.6 %collective-permute-start.39 = (bf16[32,768]{1,0:T(8,128)(2,1)S(1)}, bf16[32,768]{1,0:T(8,128)(2,1)S(1)}, u32[]{:S(2)}, u32[]{:S(2)}) collective-permute-start(bf16[32,768]{1,0:T(8,128)(2,1)S(1)} %get-tuple-element.84), channel_id=1, source_target_pairs={{0,24},{4,28},{8,32},{12,36},{16,40},{20,44},{24,48},{28,52},{32,5... | collective-permute-start | bytes 147464 | tf_op jit(solution)/shard_map/ppermute | solution.py:426
  146.4 1.8 %collective-permute-done.31.r3 = bf16[144,512]{1,0:T(8,128)(2,1)S(1)} collective-permute-done((bf16[144,512]{1,0:T(8,128)(2,1)S(1)}, bf16[144,512]{1,0:T(8,128)(2,1)S(1)}, u32[]{:S(2)}, u32[]{:S(2)}) %collective-permute-start.31) | collective-permute-done | bytes 147488 | tf_op jit(solution)/shard_map/ppermute | solution.py:435
  148.2 0.9 input.1
  149.1 0.9 place.1
  150.0 2.3 %collective-permute-done.39.refs_2_ = bf16[32,768]{1,0:T(8,128)(2,1)S(1)} collective-permute-done((bf16[32,768]{1,0:T(8,128)(2,1)S(1)}, bf16[32,768]{1,0:T(8,128)(2,1)S(1)}, u32[]{:S(2)}, u32[]{:S(2)}) %collective-permute-start.39) | collective-permute-done | bytes 49184 | tf_op jit(solution)/shard_map/ppermute | solution.py:426
  (81 shorter events, 10.6 us)
Async XLA Ops:
  0.6 21.7 %collective-permute-start.2 = (bf16[128,512]{1,0:T(8,128)(2,1)}, bf16[128,512]{1,0:T(8,128)(2,1)S(1)}, u32[]{:S(2)}, u32[]{:S(2)}) collective-permute-start(bf16[128,512]{1,0:T(8,128)(2,1)} %hid.1), channel_id=1, source_target_pairs={{0,3},{1,0},{2,1},{3,2},{4,7},{5,4},{6,5},{7,6},{8,11},{9,8},{10,9... | collective-permute-start | bytes 393224 | tf_op jit(solution)/shard_map/ppermute | solution.py:435
  3.0 19.4 %collective-permute-start.1 = (bf16[128,512]{1,0:T(8,128)(2,1)}, bf16[128,512]{1,0:T(8,128)(2,1)S(1)}, u32[]{:S(2)}, u32[]{:S(2)}) collective-permute-start(bf16[128,512]{1,0:T(8,128)(2,1)} %hid.1), channel_id=1, source_target_pairs={{0,2},{1,3},{2,0},{3,1},{4,6},{5,7},{6,4},{7,5},{8,10},{9,11},{10,... | collective-permute-start | bytes 393224 | tf_op jit(solution)/shard_map/ppermute | solution.py:435
  3.7 18.7 %collective-permute-start = (bf16[128,512]{1,0:T(8,128)(2,1)}, bf16[128,512]{1,0:T(8,128)(2,1)S(1)}, u32[]{:S(2)}, u32[]{:S(2)}) collective-permute-start(bf16[128,512]{1,0:T(8,128)(2,1)} %hid.1), channel_id=1, source_target_pairs={{0,1},{1,2},{2,3},{3,0},{4,5},{5,6},{6,7},{7,4},{8,9},{9,10},{10,1... | collective-permute-start | bytes 393224 | tf_op jit(solution)/shard_map/ppermute | solution.py:435
  7.8 46.4 %copy-start.7 = (s32[8]{0:T(128)S(1)}, s32[8]{0:T(128)}, u32[]{:S(2)}) copy-start(s32[8]{0:T(128)} %lengths.15) | copy-start | bytes 100
  9.5 34.4 %all-to-all-start = ((bf16[32,8,512]{2,1,0:T(8,128)(2,1)}), bf16[32,8,512]{2,1,0:T(8,128)(2,1)S(1)}, u32[]{:S(2)}, u32[]{:S(2)}) async-start(bf16[32,8,512]{2,1,0:T(8,128)(2,1)} %bitcast.1), calls=%async_computation | async-start | bytes 524288 | tf_op jit(solution)/shard_map/all_to_all | solution.py:441
  22.4 1.9 %copy-start = (bf16[2048,768]{1,0:T(8,128)(2,1)S(1)}, bf16[2048,768]{1,0:T(8,128)(2,1)}, u32[]{:S(2)}) copy-start(bf16[2048,768]{1,0:T(8,128)(2,1)} %refs_1_.1) | copy-start | bytes 9437188
  24.3 0.9 copy-start.2
  28.0 15.8 %collective-permute-start.4 = (bf16[512,128]{1,0:T(8,128)(2,1)S(1)}, bf16[512,128]{1,0:T(8,128)(2,1)S(1)}, u32[]{:S(2)}, u32[]{:S(2)}) collective-permute-start(bf16[512,128]{1,0:T(8,128)(2,1)S(1)} %get-tuple-element.45.refs_0_), channel_id=1, source_target_pairs={{128,0},{132,4},{136,8},{140,12},{144,16},{148,20},{152,24},{156,2... | collective-permute-start | bytes 393224 | tf_op jit(solution)/shard_map/ppermute | solution.py:416
  29.3 14.5 %collective-permute-start.3 = (bf16[512,128]{1,0:T(8,128)(2,1)S(1)}, bf16[512,128]{1,0:T(8,128)(2,1)S(1)}, u32[]{:S(2)}, u32[]{:S(2)}) collective-permute-start(bf16[512,128]{1,0:T(8,128)(2,1)S(1)} %get-tuple-element.45.refs_0_), channel_id=1, source_target_pairs={{64,0},{68,4},{72,8},{76,12},{80,16},{84,20},{88,24},{92,28},{96,3... | collective-permute-start | bytes 393224 | tf_op jit(solution)/shard_map/ppermute | solution.py:416
  30.6 8.1 %collective-permute-start.6 = (bf16[256,128]{1,0:T(8,128)(2,1)S(1)}, bf16[256,128]{1,0:T(8,128)(2,1)S(1)}, u32[]{:S(2)}, u32[]{:S(2)}) collective-permute-start(bf16[256,128]{1,0:T(8,128)(2,1)S(1)} %get-tuple-element.46.b0), channel_id=1, source_target_pairs={{0,40},{4,44},{8,48},{12,52},{16,56},{20,60},{24,0},{28,4},{32,8},... | collective-permute-start | bytes 196616 | tf_op jit(solution)/shard_map/ppermute | solution.py:426
  35.5 8.3 %collective-permute-start.5 = (bf16[256,128]{1,0:T(8,128)(2,1)S(1)}, bf16[256,128]{1,0:T(8,128)(2,1)S(1)}, u32[]{:S(2)}, u32[]{:S(2)}) collective-permute-start(bf16[256,128]{1,0:T(8,128)(2,1)S(1)} %get-tuple-element.46.b0), channel_id=1, source_target_pairs={{0,24},{4,28},{8,32},{12,36},{16,40},{20,44},{24,48},{28,52},{32,5... | collective-permute-start | bytes 196616 | tf_op jit(solution)/shard_map/ppermute | solution.py:426
  43.8 7.0 %collective-permute-start.7 = (bf16[3,256,128]{2,1,0:T(8,128)(2,1)S(1)}, bf16[3,256,128]{2,1,0:T(8,128)(2,1)S(1)}, u32[]{:S(2)}, u32[]{:S(2)}) collective-permute-start(bf16[3,256,128]{2,1,0:T(8,128)(2,1)S(1)} %get-tuple-element.47.refs_3_.refs_6_), channel_id=1, source_target_pairs={{0,8},{4,12},{8,16},{12,20},{16,24},{20,28},{24,32},{28,36},{32,40... | collective-permute-start | bytes 589832 | tf_op jit(solution)/shard_map/ppermute | solution.py:426
  43.9 7.4 %collective-permute-start.12 = (bf16[256,512]{1,0:T(8,128)(2,1)S(1)}, bf16[256,512]{1,0:T(8,128)(2,1)S(1)}, u32[]{:S(2)}, u32[]{:S(2)}) collective-permute-start(bf16[256,512]{1,0:T(8,128)(2,1)S(1)} %bitcast.5), channel_id=1, source_target_pairs={{0,4},{4,0},{8,12},{12,8},{16,20},{20,16},{24,28},{28,24},{32,36},... | collective-permute-start | bytes 786440 | tf_op jit(solution)/shard_map/ppermute | solution.py:431
  44.0 6.8 %collective-permute-start.8 = (bf16[2,256,128]{2,1,0:T(8,128)(2,1)S(1)}, bf16[2,256,128]{2,1,0:T(8,128)(2,1)S(1)}, u32[]{:S(2)}, u32[]{:S(2)}) collective-permute-start(bf16[2,256,128]{2,1,0:T(8,128)(2,1)S(1)} %get-tuple-element.48), channel_id=1, source_target_pairs={{0,56},{4,60},{8,0},{12,4},{16,8},{20,12},{24,16},{28,20},{32,24},... | collective-permute-start | bytes 393224 | tf_op jit(solution)/shard_map/ppermute | solution.py:426
  47.2 7.0 %collective-permute-start.9 = (bf16[3,256,128]{2,1,0:T(8,128)(2,1)S(1)}, bf16[3,256,128]{2,1,0:T(8,128)(2,1)S(1)}, u32[]{:S(2)}, u32[]{:S(2)}) collective-permute-start(bf16[3,256,128]{2,1,0:T(8,128)(2,1)S(1)} %get-tuple-element.47.refs_3_.refs_6_), channel_id=1, source_target_pairs={{0,4},{4,0},{8,12},{12,8},{16,20},{20,16},{24,28},{28,24},{32,36},... | collective-permute-start | bytes 589832 | tf_op jit(solution)/shard_map/ppermute | solution.py:431
  50.8 3.4 %collective-permute-start.10 = (bf16[3,256,128]{2,1,0:T(8,128)(2,1)S(1)}, bf16[3,256,128]{2,1,0:T(8,128)(2,1)S(1)}, u32[]{:S(2)}, u32[]{:S(2)}) collective-permute-start(bf16[3,256,128]{2,1,0:T(8,128)(2,1)S(1)} %collective-permute-done.7.refs_4_.refs_7_), channel_id=1, source_target_pairs={{0,4},{4,0},{8,12},{12,8},{16,20},{20,16},{24,28},{28,24},{32,36},... | collective-permute-start | bytes 589832 | tf_op jit(solution)/shard_map/ppermute | solution.py:431
  50.8 3.4 %collective-permute-start.11 = (bf16[2,256,128]{2,1,0:T(8,128)(2,1)S(1)}, bf16[2,256,128]{2,1,0:T(8,128)(2,1)S(1)}, u32[]{:S(2)}, u32[]{:S(2)}) collective-permute-start(bf16[2,256,128]{2,1,0:T(8,128)(2,1)S(1)} %collective-permute-done.8.refs_5_.refs_8_), channel_id=1, source_target_pairs={{0,4},{4,0},{8,12},{12,8},{16,20},{20,16},{24,28},{28,24},{32,36},... | collective-permute-start | bytes 393224 | tf_op jit(solution)/shard_map/ppermute | solution.py:431
  51.6 9.3 %collective-permute-start.14 = (bf16[512,128]{1,0:T(8,128)(2,1)S(1)}, bf16[512,128]{1,0:T(8,128)(2,1)S(1)}, u32[]{:S(2)}, u32[]{:S(2)}) collective-permute-start(bf16[512,128]{1,0:T(8,128)(2,1)S(1)} %grad_home.1.d0.refs_3_), channel_id=1, source_target_pairs={{128,0},{132,4},{136,8},{140,12},{144,16},{148,20},{152,24},{156,2... | collective-permute-start | bytes 393224 | tf_op jit(solution)/shard_map/ppermute | solution.py:416
  52.9 8.0 %collective-permute-start.13 = (bf16[512,128]{1,0:T(8,128)(2,1)S(1)}, bf16[512,128]{1,0:T(8,128)(2,1)S(1)}, u32[]{:S(2)}, u32[]{:S(2)}) collective-permute-start(bf16[512,128]{1,0:T(8,128)(2,1)S(1)} %grad_home.1.d0.refs_3_), channel_id=1, source_target_pairs={{64,0},{68,4},{72,8},{76,12},{80,16},{84,20},{88,24},{92,28},{96,3... | collective-permute-start | bytes 393224 | tf_op jit(solution)/shard_map/ppermute | solution.py:416
  56.5 54.1 %copy-start.1 = (bf16[2048,768]{1,0:T(8,128)(2,1)S(1)}, bf16[2048,768]{1,0:T(8,128)(2,1)}, u32[]{:S(2)}) copy-start(bf16[2048,768]{1,0:T(8,128)(2,1)} %refs_1_.1) | copy-start | bytes 9437188
  56.5 54.1 %copy-start.3 = (bf16[128,512]{1,0:T(8,128)(2,1)S(1)}, bf16[128,512]{1,0:T(8,128)(2,1)}, u32[]{:S(2)}) copy-start(bf16[128,512]{1,0:T(8,128)(2,1)} %hid.1) | copy-start | bytes 393220
  61.1 8.2 %collective-permute-start.17 = (f32[8,512]{1,0:T(8,128)S(1)}, f32[8,512]{1,0:T(8,128)S(1)}, u32[]{:S(2)}, u32[]{:S(2)}) collective-permute-start(f32[8,512]{1,0:T(8,128)S(1)} %delta.1.refs_12_.s0), channel_id=1, source_target_pairs={{0,64},{4,68},{8,72},{12,76},{16,80},{20,84},{24,88},{28,92},{32,9... | collective-permute-start | bytes 49160 | tf_op jit(solution)/shard_map/ppermute | solution.py:416
  66.0 5.2 %collective-permute-start.16 = (f32[8,512]{1,0:T(8,128)S(1)}, f32[8,512]{1,0:T(8,128)S(1)}, u32[]{:S(2)}, u32[]{:S(2)}) collective-permute-start(f32[8,512]{1,0:T(8,128)S(1)} %delta.1.refs_12_.s0), channel_id=1, source_target_pairs={{0,128},{4,132},{8,136},{12,140},{16,144},{20,148},{24,152},{28,15... | collective-permute-start | bytes 49160 | tf_op jit(solution)/shard_map/ppermute | solution.py:416
  66.8 4.5 %collective-permute-start.15 = (f32[8,512]{1,0:T(8,128)S(1)}, f32[8,512]{1,0:T(8,128)S(1)}, u32[]{:S(2)}, u32[]{:S(2)}) collective-permute-start(f32[8,512]{1,0:T(8,128)S(1)} %delta.1.refs_12_.s0), channel_id=1, source_target_pairs={{0,192},{4,196},{8,200},{12,204},{16,208},{20,212},{24,216},{28,22... | collective-permute-start | bytes 49160 | tf_op jit(solution)/shard_map/ppermute | solution.py:416
  74.0 9.8 %collective-permute-start.20 = (bf16[8,256,128]{2,1,0:T(8,128)(2,1)S(1)}, bf16[8,256,128]{2,1,0:T(8,128)(2,1)S(1)}, u32[]{:S(2)}, u32[]{:S(2)}) collective-permute-start(bf16[8,256,128]{2,1,0:T(8,128)(2,1)S(1)} %get-tuple-element.59), channel_id=1, source_target_pairs={{0,4},{4,0},{8,12},{12,8},{16,20},{20,16},{24,28},{28,24},{32,36},... | collective-permute-start | bytes 1572872 | tf_op jit(solution)/shard_map/ppermute | solution.py:431
  74.1 29.0 %collective-permute-start.18 = (bf16[256,512]{1,0:T(8,128)(2,1)S(1)}, bf16[256,512]{1,0:T(8,128)(2,1)S(1)}, u32[]{:S(2)}, u32[]{:S(2)}) collective-permute-start(bf16[256,512]{1,0:T(8,128)(2,1)S(1)} %get-tuple-element.55), channel_id=1, source_target_pairs={{0,64},{4,68},{8,72},{12,76},{16,80},{20,84},{24,88},{28,92},{32,9... | collective-permute-start | bytes 786440 | tf_op jit(solution)/shard_map/ppermute | solution.py:416
  76.1 27.0 %collective-permute-start.19 = (bf16[256,512]{1,0:T(8,128)(2,1)S(1)}, bf16[256,512]{1,0:T(8,128)(2,1)S(1)}, u32[]{:S(2)}, u32[]{:S(2)}) collective-permute-start(bf16[256,512]{1,0:T(8,128)(2,1)S(1)} %get-tuple-element.56), channel_id=1, source_target_pairs={{0,128},{4,132},{8,136},{12,140},{16,144},{20,148},{24,152},{28,15... | collective-permute-start | bytes 786440 | tf_op jit(solution)/shard_map/ppermute | solution.py:416
  83.9 15.2 %collective-permute-start.21 = (bf16[3,256,128]{2,1,0:T(8,128)(2,1)S(1)}, bf16[3,256,128]{2,1,0:T(8,128)(2,1)S(1)}, u32[]{:S(2)}, u32[]{:S(2)}) collective-permute-start(bf16[3,256,128]{2,1,0:T(8,128)(2,1)S(1)} %get-tuple-element.61), channel_id=1, source_target_pairs={{0,56},{4,60},{8,0},{12,4},{16,8},{20,12},{24,16},{28,20},{32,24},... | collective-permute-start | bytes 589832 | tf_op jit(solution)/shard_map/ppermute | solution.py:426
  92.6 6.5 %collective-permute-start.22 = (bf16[2,256,128]{2,1,0:T(8,128)(2,1)S(1)}, bf16[2,256,128]{2,1,0:T(8,128)(2,1)S(1)}, u32[]{:S(2)}, u32[]{:S(2)}) collective-permute-start(bf16[2,256,128]{2,1,0:T(8,128)(2,1)S(1)} %get-tuple-element.62), channel_id=1, source_target_pairs={{0,8},{4,12},{8,16},{12,20},{16,24},{20,28},{24,32},{28,36},{32,40... | collective-permute-start | bytes 393224 | tf_op jit(solution)/shard_map/ppermute | solution.py:426
  92.6 17.4 %collective-permute-start.25 = (bf16[128,512]{1,0:T(8,128)(2,1)S(1)}, bf16[128,512]{1,0:T(8,128)(2,1)S(1)}, u32[]{:S(2)}, u32[]{:S(2)}) collective-permute-start(bf16[128,512]{1,0:T(8,128)(2,1)S(1)} %get-tuple-element.67), channel_id=1, source_target_pairs={{0,64},{4,68},{8,72},{12,76},{16,80},{20,84},{24,88},{28,92},{32,9... | collective-permute-start | bytes 393224 | tf_op jit(solution)/shard_map/ppermute | solution.py:416
  99.2 6.6 %collective-permute-start.23 = (bf16[256,128]{1,0:T(8,128)(2,1)S(1)}, bf16[256,128]{1,0:T(8,128)(2,1)S(1)}, u32[]{:S(2)}, u32[]{:S(2)}) collective-permute-start(bf16[256,128]{1,0:T(8,128)(2,1)S(1)} %get-tuple-element.64), channel_id=1, source_target_pairs={{0,40},{4,44},{8,48},{12,52},{16,56},{20,60},{24,0},{28,4},{32,8},... | collective-permute-start | bytes 196616 | tf_op jit(solution)/shard_map/ppermute | solution.py:426
  99.3 8.4 %collective-permute-start.24 = (bf16[256,128]{1,0:T(8,128)(2,1)S(1)}, bf16[256,128]{1,0:T(8,128)(2,1)S(1)}, u32[]{:S(2)}, u32[]{:S(2)}) collective-permute-start(bf16[256,128]{1,0:T(8,128)(2,1)S(1)} %get-tuple-element.65), channel_id=1, source_target_pairs={{0,24},{4,28},{8,32},{12,36},{16,40},{20,44},{24,48},{28,52},{32,5... | collective-permute-start | bytes 196616 | tf_op jit(solution)/shard_map/ppermute | solution.py:426
  103.1 7.6 %collective-permute-start.26 = (bf16[128,512]{1,0:T(8,128)(2,1)S(1)}, bf16[128,512]{1,0:T(8,128)(2,1)S(1)}, u32[]{:S(2)}, u32[]{:S(2)}) collective-permute-start(bf16[128,512]{1,0:T(8,128)(2,1)S(1)} %get-tuple-element.68), channel_id=1, source_target_pairs={{0,128},{4,132},{8,136},{12,140},{16,144},{20,148},{24,152},{28,15... | collective-permute-start | bytes 393224 | tf_op jit(solution)/shard_map/ppermute | solution.py:416
  103.1 7.5 %collective-permute-start.27 = (bf16[128,512]{1,0:T(8,128)(2,1)S(1)}, bf16[128,512]{1,0:T(8,128)(2,1)S(1)}, u32[]{:S(2)}, u32[]{:S(2)}) collective-permute-start(bf16[128,512]{1,0:T(8,128)(2,1)S(1)} %get-tuple-element.69), channel_id=1, source_target_pairs={{0,192},{4,196},{8,200},{12,204},{16,208},{20,212},{24,216},{28,22... | collective-permute-start | bytes 393224 | tf_op jit(solution)/shard_map/ppermute | solution.py:416
  108.5 15.0 %collective-permute-start.34 = (bf16[128,768]{1,0:T(8,128)(2,1)S(1)}, bf16[128,768]{1,0:T(8,128)(2,1)S(1)}, u32[]{:S(2)}, u32[]{:S(2)}) collective-permute-start(bf16[128,768]{1,0:T(8,128)(2,1)S(1)} %rows.1.refs_0_.refs_4_), channel_id=1, source_target_pairs={{0,192},{4,196},{8,200},{12,204},{16,208},{20,212},{24,216},{28,22... | collective-permute-start | bytes 589832 | tf_op jit(solution)/shard_map/ppermute | solution.py:416
  108.6 14.9 %collective-permute-start.33 = (bf16[128,768]{1,0:T(8,128)(2,1)S(1)}, bf16[128,768]{1,0:T(8,128)(2,1)S(1)}, u32[]{:S(2)}, u32[]{:S(2)}) collective-permute-start(bf16[128,768]{1,0:T(8,128)(2,1)S(1)} %rows.1.refs_0_.refs_4_), channel_id=1, source_target_pairs={{0,128},{4,132},{8,136},{12,140},{16,144},{20,148},{24,152},{28,15... | collective-permute-start | bytes 589832 | tf_op jit(solution)/shard_map/ppermute | solution.py:416
  110.0 13.6 %collective-permute-start.32 = (bf16[128,768]{1,0:T(8,128)(2,1)S(1)}, bf16[128,768]{1,0:T(8,128)(2,1)S(1)}, u32[]{:S(2)}, u32[]{:S(2)}) collective-permute-start(bf16[128,768]{1,0:T(8,128)(2,1)S(1)} %rows.1.refs_0_.refs_4_), channel_id=1, source_target_pairs={{0,64},{4,68},{8,72},{12,76},{16,80},{20,84},{24,88},{28,92},{32,9... | collective-permute-start | bytes 589832 | tf_op jit(solution)/shard_map/ppermute | solution.py:416
  112.7 1.7 %copy-start.9 = (bf16[144,512]{1,0:T(8,128)(2,1)}, bf16[144,512]{1,0:T(8,128)(2,1)S(1)}, u32[]{:S(2)}) copy-start(bf16[144,512]{1,0:T(8,128)(2,1)S(1)} %get-tuple-element.72) | copy-start | bytes 442372
  114.4 19.9 %all-to-all-start.1 = ((bf16[32,8,512]{2,1,0:T(8,128)(2,1)}), bf16[32,8,512]{2,1,0:T(8,128)(2,1)S(1)}, u32[]{:S(2)}, u32[]{:S(2)}) async-start(bf16[32,8,512]{2,1,0:T(8,128)(2,1)} %bitcast.3), calls=%async_computation.1 | async-start | bytes 524288 | tf_op jit(solution)/shard_map/all_to_all | solution.py:441
  125.6 8.7 %collective-permute-start.35 = (bf16[8,32,768]{2,1,0:T(8,128)(2,1)S(1)}, bf16[8,32,768]{2,1,0:T(8,128)(2,1)S(1)}, u32[]{:S(2)}, u32[]{:S(2)}) collective-permute-start(bf16[8,32,768]{2,1,0:T(8,128)(2,1)S(1)} %get-tuple-element.78), channel_id=1, source_target_pairs={{0,4},{4,0},{8,12},{12,8},{16,20},{20,16},{24,28},{28,24},{32,36},... | collective-permute-start | bytes 1179656 | tf_op jit(solution)/shard_map/ppermute | solution.py:431
  134.3 14.8 %collective-permute-start.28 = (bf16[256,512]{1,0:T(8,128)(2,1)S(1)}, bf16[256,512]{1,0:T(8,128)(2,1)S(1)}, u32[]{:S(2)}, u32[]{:S(2)}) collective-permute-start(bf16[256,512]{1,0:T(8,128)(2,1)S(1)} %bitcast.7), channel_id=1, source_target_pairs={{0,4},{4,0},{8,12},{12,8},{16,20},{20,16},{24,28},{28,24},{32,36},... | collective-permute-start | bytes 786440 | tf_op jit(solution)/shard_map/ppermute | solution.py:431
  134.4 6.5 %collective-permute-start.37 = (bf16[2,32,768]{2,1,0:T(8,128)(2,1)S(1)}, bf16[2,32,768]{2,1,0:T(8,128)(2,1)S(1)}, u32[]{:S(2)}, u32[]{:S(2)}) collective-permute-start(bf16[2,32,768]{2,1,0:T(8,128)(2,1)S(1)} %get-tuple-element.81), channel_id=1, source_target_pairs={{0,8},{4,12},{8,16},{12,20},{16,24},{20,28},{24,32},{28,36},{32,40... | collective-permute-start | bytes 294920 | tf_op jit(solution)/shard_map/ppermute | solution.py:426
  136.3 6.0 %collective-permute-start.36 = (bf16[3,32,768]{2,1,0:T(8,128)(2,1)S(1)}, bf16[3,32,768]{2,1,0:T(8,128)(2,1)S(1)}, u32[]{:S(2)}, u32[]{:S(2)}) collective-permute-start(bf16[3,32,768]{2,1,0:T(8,128)(2,1)S(1)} %get-tuple-element.80), channel_id=1, source_target_pairs={{0,56},{4,60},{8,0},{12,4},{16,8},{20,12},{24,16},{28,20},{32,24},... | collective-permute-start | bytes 442376 | tf_op jit(solution)/shard_map/ppermute | solution.py:426
  137.7 6.9 %collective-permute-start.29 = (bf16[144,512]{1,0:T(8,128)(2,1)}, bf16[144,512]{1,0:T(8,128)(2,1)S(1)}, u32[]{:S(2)}, u32[]{:S(2)}) collective-permute-start(bf16[144,512]{1,0:T(8,128)(2,1)} %copy-done.9), channel_id=1, source_target_pairs={{0,1},{1,2},{2,3},{3,0},{4,5},{5,6},{6,7},{7,4},{8,9},{9,10},{10,1... | collective-permute-start | bytes 442376 | tf_op jit(solution)/shard_map/ppermute | solution.py:435
  138.1 8.3 %collective-permute-start.30 = (bf16[144,512]{1,0:T(8,128)(2,1)S(1)}, bf16[144,512]{1,0:T(8,128)(2,1)S(1)}, u32[]{:S(2)}, u32[]{:S(2)}) collective-permute-start(bf16[144,512]{1,0:T(8,128)(2,1)S(1)} %get-tuple-element.73), channel_id=1, source_target_pairs={{0,2},{1,3},{2,0},{3,1},{4,6},{5,7},{6,4},{7,5},{8,10},{9,11},{10,... | collective-permute-start | bytes 442376 | tf_op jit(solution)/shard_map/ppermute | solution.py:435
  140.9 7.3 %collective-permute-start.31 = (bf16[144,512]{1,0:T(8,128)(2,1)S(1)}, bf16[144,512]{1,0:T(8,128)(2,1)S(1)}, u32[]{:S(2)}, u32[]{:S(2)}) collective-permute-start(bf16[144,512]{1,0:T(8,128)(2,1)S(1)} %get-tuple-element.74), channel_id=1, source_target_pairs={{0,3},{1,0},{2,1},{3,2},{4,7},{5,4},{6,5},{7,6},{8,11},{9,8},{10,9... | collective-permute-start | bytes 442376 | tf_op jit(solution)/shard_map/ppermute | solution.py:435
  142.4 7.6 %collective-permute-start.38 = (bf16[32,768]{1,0:T(8,128)(2,1)S(1)}, bf16[32,768]{1,0:T(8,128)(2,1)S(1)}, u32[]{:S(2)}, u32[]{:S(2)}) collective-permute-start(bf16[32,768]{1,0:T(8,128)(2,1)S(1)} %get-tuple-element.83), channel_id=1, source_target_pairs={{0,40},{4,44},{8,48},{12,52},{16,56},{20,60},{24,0},{28,4},{32,8},... | collective-permute-start | bytes 147464 | tf_op jit(solution)/shard_map/ppermute | solution.py:426
  144.6 7.6 %collective-permute-start.39 = (bf16[32,768]{1,0:T(8,128)(2,1)S(1)}, bf16[32,768]{1,0:T(8,128)(2,1)S(1)}, u32[]{:S(2)}, u32[]{:S(2)}) collective-permute-start(bf16[32,768]{1,0:T(8,128)(2,1)S(1)} %get-tuple-element.84), channel_id=1, source_target_pairs={{0,24},{4,28},{8,32},{12,36},{16,40},{20,44},{24,48},{28,52},{32,5... | collective-permute-start | bytes 147464 | tf_op jit(solution)/shard_map/ppermute | solution.py:426
  (4 other events, 3.0 us)

commit v2 on v1

--- a/solution.py
+++ b/solution.py
@@ -16,6 +16,7 @@
 CAP = 4
 SLOTS = N_CTX * CAP
 VISITS = 3
+TILE = 512
 KEPT = (0, 3, 5)
 FROM_BELOW = (1, 4, 6)
 FROM_ABOVE = (7, 2)
@@ -149,7 +150,13 @@
         copy.wait()
 
 
-def block_start(sc, row):
+def turn_heads(rows, out):
+    for h in range(GROUP):
+        part = slice(h * TOK, (h + 1) * TOK)
+        out[:, part] = rows[part, :].astype(f32).T.astype(bf16)
+
+
+def doc_start(sc, row):
     start, begin = 0, sc[8]
     for d in range(1, 8):
         start = jnp.where(begin <= row, begin, start)
@@ -157,33 +164,56 @@
     return start
 
 
-def query_rows(sc, visit):
-    first = ((sc[1] + visit) * NZ * NC + sc[2] * NC + sc[3]) * TOK
-    rows = first + lax.broadcasted_iota(i32, (1, QW), 1) % TOK
-    starts, begin = jnp.zeros((1, QW), i32), sc[8]
-    for d in range(1, 8):
-        starts = jnp.where(rows >= begin, begin, starts)
-        begin = begin + sc[8 + d]
-    return first, rows, starts
+def first_query(sc, visit):
+    return ((sc[1] + visit) * NZ * NC + sc[2] * NC + sc[3]) * TOK
 
 
 def key_tile(sc, s):
     return sc[1] * NZ + (sc[2] + NZ - s) % NZ
 
 
-def tile_needed(sc, visit, s):
-    pair = key_tile(sc, s)
-    first = ((sc[1] + visit) * NZ * NC + sc[2] * NC + sc[3]) * TOK
-    live = (sc[1] + visit < NY) & (pair <= (sc[1] + visit) * NZ + sc[2])
-    return live & (pair * 256 + 255 >= block_start(sc, first))
-
-
-def load_keys(kvs, keys, values):
+def tile_state(sc, visit, s):
+    first, low = first_query(sc, visit), key_tile(sc, s) * (NC * TOK)
+    high = low + NC * TOK - 1
+    some = (sc[1] + visit < NY) & (low <= first + TOK - 1) & (high >= doc_start(sc, first))
+    every = (high <= first) & (low >= doc_start(sc, first + TOK - 1))
+    return some, every
+
+
+def tile_mask(sc, visit, s):
+    rows = first_query(sc, visit) + lax.broadcasted_iota(i32, (1, TOK), 1)
+    starts = doc_start(sc, rows)
+    line = lax.broadcasted_iota(i32, (TILE, TOK), 0)
+    offset = (line % (NC * TOK)) ^ (sc[3] * TOK)
+    first, second = key_tile(sc, 2 * s) * (NC * TOK), key_tile(sc, 2 * s + 1) * (NC * TOK)
+    key_rows = jnp.where(line < NC * TOK, first, second) + offset
+    return (key_rows >= starts) & (key_rows <= rows)
+
+
+def on_tile(sc, visit, s, work):
+    some, every = tile_state(sc, visit, 2 * s)
+    some2, every2 = tile_state(sc, visit, 2 * s + 1)
+    some, every = some | some2, every & every2
+
+    @pl.when(some & every)
+    def _():
+        work(None)
+
+    @pl.when(some & jnp.logical_not(every))
+    def _():
+        work(tile_mask(sc, visit, s))
+
+
+def load_keys(kvs, keys, values, turned, which):
     for e in range(NC):
         for stack, steps in zip(kvs[3 * e : 3 * e + 3], (KEPT, FROM_BELOW, FROM_ABOVE)):
             for i, s in enumerate(steps):
-                keys[s, e * TOK : (e + 1) * TOK, :] = stack[i, 0:TOK, :]
-                values[s, e * TOK : (e + 1) * TOK, :] = stack[i, TOK:, :]
+                at = s // 2
+                half = slice((s % 2 * NC + e) * TOK, (s % 2 * NC + e + 1) * TOK)
+                keys[at, half, :] = stack[i, 0:TOK, :]
+                values[at, half, :] = stack[i, TOK:, :]
+                picked = stack[i, which * TOK : (which + 1) * TOK, :]
+                turned[at, :, half] = picked.astype(f32).T.astype(bf16)
 
 
 def pack_kernel(b0, b3, b5, _, __, three_ref, two_ref):
@@ -193,46 +223,46 @@
             two_ref[i] = b[...]
 
 
-def tile_mask(sc, s, rows, starts):
-    offset = lax.broadcasted_iota(i32, (2 * TOK, QW), 0) ^ (sc[3] * TOK)
-    key_rows = key_tile(sc, s) * 256 + offset
-    return (key_rows >= starts) & (key_rows <= rows)
-
-
 def forward_kernel(lengths, *refs):
     sc = scalars(lengths)
     qs, kvs = refs[0:3], refs[3:9]
     outs, stats = refs[9:12], refs[12]
-    keys, values, acc, top, total = refs[13:]
-    load_keys(kvs, keys, values)
+    keys, values, values_t, probs, acc, top, total, q_t = refs[13:]
+    load_keys(kvs, keys, values, values_t, 1)
     stats[...] = jnp.zeros_like(stats)
     for visit in range(VISITS):
-        q_ref = qs[visit]
-        _, rows, starts = query_rows(sc, visit)
+        turn_heads(qs[visit], q_t)
         acc[...] = jnp.zeros_like(acc)
         total[...] = jnp.zeros_like(total)
         top[...] = jnp.full_like(top, masked)
 
-        @pl.loop(0, NZ)
+        @pl.loop(0, NZ // 2)
         def _(s):
-            @pl.when(tile_needed(sc, visit, s))
-            def _():
-                scores = dot(keys[s], q_ref[...], NT) * (scale * log2e)
-                scores = jnp.where(tile_mask(sc, s, rows, starts), scores, masked)
-                old = top[...]
-                new = jnp.maximum(old, jnp.max(scores, axis=0, keepdims=True))
-                base = jnp.maximum(new, 0.1 * masked)
-                p = jnp.exp2(scores - base)
-                fade = jnp.exp2(old - base)
-                top[...] = new
-                total[...] = total[...] * fade + jnp.sum(p, axis=0, keepdims=True)
-                acc[...] = acc[...] * fade + dot(values[s], p.astype(bf16), TN)
+            def work(allowed):
+                for h in range(GROUP):
+                    cols = slice(h * TOK, (h + 1) * TOK)
+                    scores = dot(keys[s], q_t[:, cols])
+                    if allowed is not None:
+                        scores = jnp.where(allowed, scores, masked)
+                    old = top[:, cols]
+                    new = jnp.maximum(old, jnp.max(scores, axis=0, keepdims=True))
+                    base = jnp.maximum(new, 0.1 * masked) * (scale * log2e)
+                    p = jnp.exp2(scores * (scale * log2e) - base)
+                    fade = jnp.exp2(old * (scale * log2e) - base)
+                    top[:, cols] = new
+                    total[:, cols] = total[:, cols] * fade + jnp.sum(p, axis=0, keepdims=True)
+                    probs[:, cols] = p.astype(bf16)
+                    acc[:, cols] = acc[:, cols] * fade
+                acc[...] += dot(values_t[s], probs[...])
+
+            on_tile(sc, visit, s, work)
 
         mass = total[...]
         some = mass > 0.0
         mass = jnp.where(some, mass, 1.0)
         outs[visit][...] = (acc[...] * (1.0 / mass)).astype(bf16)
-        stats[visit : visit + 1, :] = jnp.where(some, top[...] + jnp.log2(mass), masked)
+        logs = top[...] * (scale * log2e) + jnp.log2(mass)
+        stats[visit : visit + 1, :] = jnp.where(some, logs, masked)
 
 
 def delta_kernel(stats, o0, o1, o2, d0, d1, d2, out_ref):
@@ -260,39 +290,46 @@
     sc = scalars(lengths)
     qs, dos, kvs, held, outs = refs[0:3], refs[3:6], refs[6:12], refs[12:16], refs[16:18]
     dq_ref, returns, own_ref, other_ref = refs[18], refs[19:21], refs[21], refs[22]
-    keys, values, q_all, do_all, dq_acc, logs, deltas, dk, dv = refs[23:]
-    load_keys(kvs, keys, values)
+    keys, values, keys_t, q_all, do_all, dq_acc, logs, deltas, probs, dscores, dk, dv, q_t, do_t = refs[23:]
+    load_keys(kvs, keys, values, keys_t, 0)
     dq_acc[...] = jnp.zeros_like(dq_acc)
     for visit in range(VISITS):
         q_all[visit] = qs[visit][...]
         do_all[visit] = dos[visit][...]
+        turn_heads(qs[visit], q_t.at[visit])
+        turn_heads(dos[visit], do_t.at[visit])
         log_total, delta, _ = combine_stats(sc, visit, held)
         logs[visit] = log_total
         deltas[visit] = delta
 
-    @pl.loop(0, NZ)
+    @pl.loop(0, NZ // 2)
     def _(s):
         dk[...] = jnp.zeros_like(dk)
         dv[...] = jnp.zeros_like(dv)
 
         @pl.loop(0, VISITS)
         def _(visit):
-            @pl.when(tile_needed(sc, visit, s))
-            def _():
-                _, rows, starts = query_rows(sc, visit)
-                q, do = q_all[visit], do_all[visit]
-                scores = dot(keys[s], q, NT) * (scale * log2e) - logs[visit]
-                p = jnp.exp2(jnp.where(tile_mask(sc, s, rows, starts), scores, masked))
-                dp = dot(values[s], do, NT)
-                ds = (p * (dp - deltas[visit])).astype(bf16)
-                dv[...] += dot(p.astype(bf16), do)
-                dk[...] += dot(ds, q)
-                dq_acc[visit] += dot(keys[s], ds, TN)
+            def work(allowed):
+                for h in range(GROUP):
+                    cols = slice(h * TOK, (h + 1) * TOK)
+                    scores = dot(keys[s], q_t[visit, :, cols]) * (scale * log2e) - logs[visit, :, cols]
+                    if allowed is not None:
+                        scores = jnp.where(allowed, scores, masked)
+                    p = jnp.exp2(scores)
+                    dp = dot(values[s], do_t[visit, :, cols])
+                    probs[:, cols] = p.astype(bf16)
+                    dscores[:, cols] = (p * (dp - deltas[visit, :, cols])).astype(bf16)
+                dv[...] += dot(probs[...], do_all[visit])
+                dk[...] += dot(dscores[...], q_all[visit])
+                dq_acc[visit] += dot(keys_t[s], dscores[...])
+
+            on_tile(sc, visit, s, work)
 
         for e, out in enumerate((own_ref, other_ref)):
-            half = slice(e * TOK, (e + 1) * TOK)
-            out[s, 0:TOK, :] = (dk[half, :] * scale).astype(bf16)
-            out[s, TOK:, :] = dv[half, :].astype(bf16)
+            for i in range(2):
+                half = slice((i * NC + e) * TOK, (i * NC + e + 1) * TOK)
+                out[2 * s + i, 0:TOK, :] = (dk[half, :] * scale).astype(bf16)
+                out[2 * s + i, TOK:, :] = dv[half, :].astype(bf16)
 
     dq_ref[...] = dq_acc[0] * scale
     for visit in (1, 2):
@@ -317,8 +354,7 @@
             out[i] = (own[s].astype(f32) + came[s].astype(f32)).astype(out.dtype)
 
 
-def add_near_kernel(kept, below, above, *refs):
-    o0, o3, o5 = refs[-3:]
+def add_near_kernel(kept, below, above, o0, o3, o5):
     o0[...] = kept[0] + below[0].astype(f32) + above[0].astype(f32)
     o3[...] = (kept[1] + below[1].astype(f32) + above[1].astype(f32)).astype(bf16)
     o5[...] = (kept[2] + below[2].astype(f32)).astype(bf16)
@@ -444,7 +480,7 @@
     return came.reshape(SLOTS, width)
 
 
-def reduce_cores_and_z(own, other, name, after=()):
+def reduce_cores_and_z(own, other, name):
     shape = own.shape[1:]
     came = over_c(other)
     kept, below, above = call(
@@ -458,8 +494,8 @@
     o0, o3, o5 = call(
         add_near_kernel,
         [(shape, f32), (shape, bf16), (shape, bf16)],
-        "vvv" + "a" * len(after),
-        (kept, below, above, *after),
+        "vvv",
+        (kept, below, above),
         name="add_near_" + name,
     )
     return o0, over_z(o3, -3), over_z(o5, 3)
@@ -521,11 +557,14 @@
         "s" + "v" * 9,
         (lengths, *qs, *kvs),
         scratch=[
-            pltpu.VMEM((NZ, 2 * TOK, HD), bf16),
-            pltpu.VMEM((NZ, 2 * TOK, HD), bf16),
+            pltpu.VMEM((NZ // 2, TILE, HD), bf16),
+            pltpu.VMEM((NZ // 2, TILE, HD), bf16),
+            pltpu.VMEM((NZ // 2, HD, TILE), bf16),
+            pltpu.VMEM((TILE, QW), bf16),
             pltpu.VMEM((HD, QW), f32),
             pltpu.VMEM((1, QW), f32),
             pltpu.VMEM((1, QW), f32),
+            pltpu.VMEM((HD, QW), bf16),
         ],
         flops=3 * 10**9,
         name="forward",
@@ -539,15 +578,20 @@
         "s" + "v" * 18,
         (lengths, *qs, *dos, *kvs, *held, outs[1], outs[2]),
         scratch=[
-            pltpu.VMEM((NZ, 2 * TOK, HD), bf16),
-            pltpu.VMEM((NZ, 2 * TOK, HD), bf16),
+            pltpu.VMEM((NZ // 2, TILE, HD), bf16),
+            pltpu.VMEM((NZ // 2, TILE, HD), bf16),
+            pltpu.VMEM((NZ // 2, HD, TILE), bf16),
             pltpu.VMEM((VISITS, QW, HD), bf16),
             pltpu.VMEM((VISITS, QW, HD), bf16),
             pltpu.VMEM((VISITS, HD, QW), f32),
             pltpu.VMEM((VISITS, 1, QW), f32),
             pltpu.VMEM((VISITS, 1, QW), f32),
-            pltpu.VMEM((2 * TOK, HD), f32),
-            pltpu.VMEM((2 * TOK, HD), f32),
+            pltpu.VMEM((TILE, QW), bf16),
+            pltpu.VMEM((TILE, QW), bf16),
+            pltpu.VMEM((TILE, HD), f32),
+            pltpu.VMEM((TILE, HD), f32),
+            pltpu.VMEM((VISITS, HD, QW), bf16),
+            pltpu.VMEM((VISITS, HD, QW), bf16),
         ],
         flops=5 * 10**9,
         name="backward",

time: 151 us -> 149 us (0.987); the launches traced: 153 us -> 147 us
  starting transfers between devices: 83.9 us -> 72.8 us
  Pallas kernels: 18.8 us -> 24.9 us
    pallas_call x18, Pallas kernels: 18.8 us -> 24.9 us  [call(): pl.pallas_call(kernel, out_shape=[jax.ShapeDtypeStruct(s, d) for s, d in...]
    ppermute x15, starting transfers between devices: 27.1 us -> 21.4 us  [over_y(): return lax.ppermute(a, 'ctx', pairs)]
    ppermute x12, starting transfers between devices: 27.1 us -> 22 us  [over_z(): return lax.ppermute(a, 'ctx', pairs)]
    ppermute x15, waiting for transfers between devices: 6.38 us -> 3.52 us  [over_y(): return lax.ppermute(a, 'ctx', pairs)]
  transfers between devices with their start and end apart: 42 -> 42, of which waited for: 15 -> 15; matrix products, arithmetic and copies ran while one was open for 1% -> 1% of each run, Pallas kernels for 10% -> 12%
where the time goes in v2:
time: 149 us; the launch traced here: 147 us
  starting transfers between devices  72.8 us (49%)
  waiting for transfers between devices  41.2 us (28%)
  Pallas kernels  24.9 us (17%)
  local copies, waits for them, and re-layouts  5.78 us (4%)
    ppermute x12, waiting for transfers between devices, over_z(): return lax.ppermute(a, 'ctx', pairs)  25.9 us
    pallas_call x18, Pallas kernels, call(): pl.pallas_call(kernel, out_shape=[jax.ShapeDtypeStruct(s, d) for s, d in...  24.9 us
    ppermute x12, starting transfers between devices, over_z(): return lax.ppermute(a, 'ctx', pairs)  22 us
    ppermute x15, starting transfers between devices, over_y(): return lax.ppermute(a, 'ctx', pairs)  21.4 us
    all_to_all x2, starting transfers between devices, exchange_slots(): lax.all_to_all(send.reshape(NY * NZ, NC * CAP, width), 'ctx', split_axis=...  20.3 us
    all_to_all x2, waiting for transfers between devices, exchange_slots(): lax.all_to_all(send.reshape(NY * NZ, NC * CAP, width), 'ctx', split_axis=...  8.83 us
    ppermute x6, starting transfers between devices, over_x(): return lax.ppermute(a, 'fsdp', [(x, (x + shift) % NX) for x in range(NX)])  8.07 us
    unnamed x20, local copies, waits for them, and re-layouts  5.78 us
  transfers between devices with their start and end apart: 42, of which 15 were waited for; matrix products, arithmetic and copies ran while one was open for 1% of the time, Pallas kernels for 12%

profile of v2, /device:TPU:2, one launch (start us, length us, event | category | flops | bytes accessed | tf_op | source)
XLA Modules:
  0.0 147.1 jit_solution(12378550364356699360)
XLA Ops:
  0.6 2.3 %collective-permute-start.2 = (bf16[128,512]{1,0:T(8,128)(2,1)}, bf16[128,512]{1,0:T(8,128)(2,1)S(1)}, u32[]{:S(2)}, u32[]{:S(2)}) collective-permute-start(bf16[128,512]{1,0:T(8,128)(2,1)} %hid.1), channel_id=1, source_target_pairs={{0,3},{1,0},{2,1},{3,2},{4,7},{5,4},{6,5},{7,6},{8,11},{9,8},{10,9... | collective-permute-start | bytes 393224 | tf_op jit(solution)/shard_map/ppermute | solution.py:471
  3.7 1.8 %collective-permute-start = (bf16[128,512]{1,0:T(8,128)(2,1)}, bf16[128,512]{1,0:T(8,128)(2,1)S(1)}, u32[]{:S(2)}, u32[]{:S(2)}) collective-permute-start(bf16[128,512]{1,0:T(8,128)(2,1)} %hid.1), channel_id=1, source_target_pairs={{0,1},{1,2},{2,3},{3,0},{4,5},{5,6},{6,7},{7,4},{8,9},{9,10},{10,1... | collective-permute-start | bytes 393224 | tf_op jit(solution)/shard_map/ppermute | solution.py:471
  5.5 0.9 copy-done.4
  7.8 1.7 %route.1 = (bf16[256,512]{1,0:T(8,128)(2,1)}, bf16[256,128]{1,0:T(8,128)(2,1)S(1)}, bf16[512,128]{1,0:T(8,128)(2,1)S(1)}, bf16[512,128]{1,0:T(8,128)(2,1)S(1)}) custom-call(s32[8]{0:T(128)S(1)} %copy-done.5, s32[64,128]{1,0:T(8,128)S(1)} %bitcast.9, bf16[128,512]{1,0:T(8,128)(2,1)S(1)} %copy-done.4), custom_call_target="tpu_custom_call" | custom-call | flops 1000 | bytes 1000 | tf_op jit(solution)/shard_map/route/pallas_call | solution.py:46
  9.5 11.5 %all-to-all-start = ((bf16[32,8,512]{2,1,0:T(8,128)(2,1)}), bf16[32,8,512]{2,1,0:T(8,128)(2,1)S(1)}, u32[]{:S(2)}, u32[]{:S(2)}) async-start(bf16[32,8,512]{2,1,0:T(8,128)(2,1)} %bitcast.1), calls=%async_computation | async-start | bytes 524288 | tf_op jit(solution)/shard_map/all_to_all | solution.py:477
  22.4 1.9 %copy-done = bf16[2048,768]{1,0:T(8,128)(2,1)S(1)} copy-done((bf16[2048,768]{1,0:T(8,128)(2,1)S(1)}, bf16[2048,768]{1,0:T(8,128)(2,1)}, u32[]{:S(2)}) %copy-start) | copy-done | bytes 3145752
  24.3 0.9 copy-done.2
  25.8 2.2 %project.1 = (bf16[512,128]{1,0:T(8,128)(2,1)S(1)}, bf16[256,128]{1,0:T(8,128)(2,1)S(1)}, bf16[128,512]{1,0:T(8,128)(2,1)S(1)}, bf16[128,512]{1,0:T(8,128)(2,1)S...) custom-call(s32[8]{0:T(128)S(1)} %copy-done.6, ...), custom_call_target="tpu_custom_call" | custom-call | flops 1000 | bytes 1000 | tf_op jit(solution)/shard_map/project/pallas_call | solution.py:46
  28.0 1.3 collective-permute-start.4
  29.3 1.3 collective-permute-start.3
  30.6 4.9 %collective-permute-start.6 = (bf16[256,128]{1,0:T(8,128)(2,1)S(1)}, bf16[256,128]{1,0:T(8,128)(2,1)S(1)}, u32[]{:S(2)}, u32[]{:S(2)}) collective-permute-start(bf16[256,128]{1,0:T(8,128)(2,1)S(1)} %get-tuple-element.46.b0), channel_id=1, source_target_pairs={{0,40},{4,44},{8,48},{12,52},{16,56},{20,60},{24,0},{28,4},{32,8},... | collective-permute-start | bytes 196616 | tf_op jit(solution)/shard_map/ppermute | solution.py:462
  35.5 3.2 %collective-permute-done.6.b5 = bf16[256,128]{1,0:T(8,128)(2,1)S(1)} collective-permute-done((bf16[256,128]{1,0:T(8,128)(2,1)S(1)}, bf16[256,128]{1,0:T(8,128)(2,1)S(1)}, u32[]{:S(2)}, u32[]{:S(2)}) %collective-permute-start.6) | collective-permute-done | bytes 65568 | tf_op jit(solution)/shard_map/ppermute | solution.py:462
  38.7 5.1 %collective-permute-done.5.b3 = bf16[256,128]{1,0:T(8,128)(2,1)S(1)} collective-permute-done((bf16[256,128]{1,0:T(8,128)(2,1)S(1)}, bf16[256,128]{1,0:T(8,128)(2,1)S(1)}, u32[]{:S(2)}, u32[]{:S(2)}) %collective-permute-start.5) | collective-permute-done | bytes 65568 | tf_op jit(solution)/shard_map/ppermute | solution.py:462
  44.0 3.1 %collective-permute-start.8 = (bf16[2,256,128]{2,1,0:T(8,128)(2,1)S(1)}, bf16[2,256,128]{2,1,0:T(8,128)(2,1)S(1)}, u32[]{:S(2)}, u32[]{:S(2)}) collective-permute-start(bf16[2,256,128]{2,1,0:T(8,128)(2,1)S(1)} %get-tuple-element.48), channel_id=1, source_target_pairs={{0,56},{4,60},{8,0},{12,4},{16,8},{20,12},{24,16},{28,20},{32,24},... | collective-permute-start | bytes 393224 | tf_op jit(solution)/shard_map/ppermute | solution.py:462
  47.4 3.4 %collective-permute-done.7.refs_4_.refs_7_ = bf16[3,256,128]{2,1,0:T(8,128)(2,1)S(1)} collective-permute-done((bf16[3,256,128]{2,1,0:T(8,128)(2,1)S(1)}, bf16[3,256,128]{2,1,0:T(8,128)(2,1)S(1)}, u32[]{:S(2)}, u32[]{:S(2)}) %collective-permute-start.7) | collective-permute-done | bytes 196640 | tf_op jit(solution)/shard_map/ppermute | solution.py:462
  51.6 1.3 collective-permute-start.14
  52.9 1.5 %collective-permute-start.13 = (bf16[512,128]{1,0:T(8,128)(2,1)S(1)}, bf16[512,128]{1,0:T(8,128)(2,1)S(1)}, u32[]{:S(2)}, u32[]{:S(2)}) collective-permute-start(bf16[512,128]{1,0:T(8,128)(2,1)S(1)} %grad_home.1.d0.refs_3_), channel_id=1, source_target_pairs={{64,0},{68,4},{72,8},{76,12},{80,16},{84,20},{88,24},{92,28},{96,3... | collective-permute-start | bytes 393224 | tf_op jit(solution)/shard_map/ppermute | solution.py:452
  54.4 5.0 %forward.1 = (bf16[128,512]{1,0:T(8,128)(2,1)S(1)}, bf16[128,512]{1,0:T(8,128)(2,1)S(1)}, bf16[128,512]{1,0:T(8,128)(2,1)S(1)}, f32[8,512]{1,0:T(8,128)S(1)}) custom-call(s32[8]{0:T(128)S(1)} %copy-done.7, bf16[512,128]{1,0:T(8,128)(2,1)S(1)} %get-tuple-element.45.refs_0_, bf16[512,128]{1,0:T(8,128)(2,1)S(1)} %collective-permute-done.3._.refs_1_, ...), custom_call_target="tpu_custom_call" | custom-call | flops 1000 | bytes 1000 | tf_op jit(solution)/shard_map/forward/pallas_call | solution.py:46
  59.4 1.5 %collective-permute-done.14.d2.refs_5_ = bf16[512,128]{1,0:T(8,128)(2,1)S(1)} collective-permute-done((bf16[512,128]{1,0:T(8,128)(2,1)S(1)}, bf16[512,128]{1,0:T(8,128)(2,1)S(1)}, u32[]{:S(2)}, u32[]{:S(2)}) %collective-permute-start.14) | collective-permute-done | bytes 131104 | tf_op jit(solution)/shard_map/ppermute | solution.py:452
  61.1 4.7 %collective-permute-start.17 = (f32[8,512]{1,0:T(8,128)S(1)}, f32[8,512]{1,0:T(8,128)S(1)}, u32[]{:S(2)}, u32[]{:S(2)}) collective-permute-start(f32[8,512]{1,0:T(8,128)S(1)} %delta.1.refs_12_.s0), channel_id=1, source_target_pairs={{0,64},{4,68},{8,72},{12,76},{16,80},{20,84},{24,88},{28,92},{32,9... | collective-permute-start | bytes 49160 | tf_op jit(solution)/shard_map/ppermute | solution.py:452
  66.6 2.5 %collective-permute-start.15 = (f32[8,512]{1,0:T(8,128)S(1)}, f32[8,512]{1,0:T(8,128)S(1)}, u32[]{:S(2)}, u32[]{:S(2)}) collective-permute-start(f32[8,512]{1,0:T(8,128)S(1)} %delta.1.refs_12_.s0), channel_id=1, source_target_pairs={{0,192},{4,196},{8,200},{12,204},{16,208},{20,212},{24,216},{28,22... | collective-permute-start | bytes 49160 | tf_op jit(solution)/shard_map/ppermute | solution.py:452
  69.1 2.0 %collective-permute-done.16.refs_14_.s2 = f32[8,512]{1,0:T(8,128)S(1)} collective-permute-done((f32[8,512]{1,0:T(8,128)S(1)}, f32[8,512]{1,0:T(8,128)S(1)}, u32[]{:S(2)}, u32[]{:S(2)}) %collective-permute-start.16) | collective-permute-done | bytes 16416 | tf_op jit(solution)/shard_map/ppermute | solution.py:452
  71.1 6.2 %backward.1 = (f32[128,512]{1,0:T(8,128)S(1)}, bf16[256,512]{1,0:T(8,128)(2,1)S(1)}, bf16[256,512]{1,0:T(8,128)(2,1)S(1)}, bf16[8,256,128]{2,1,0:T(8,128)(2,1)S(1)}, bf16[8,256,128]{2,1,0:T(8,128)(2,1)S(1)}) custom-call(s32[8]{0:T(128)S(1)} %copy-done.7, bf16[512,128]{1,0:T(8,128)(2,1)S(1)} %get-tuple-element.45.refs_0_, ...), custom_call_target="tpu_custom_call" | custom-call | flops 1000 | bytes 1000 | tf_op jit(solution)/shard_map/backward/pallas_call | solution.py:46
  77.4 1.3 collective-permute-start.18
  78.7 3.7 %collective-permute-start.19 = (bf16[256,512]{1,0:T(8,128)(2,1)S(1)}, bf16[256,512]{1,0:T(8,128)(2,1)S(1)}, u32[]{:S(2)}, u32[]{:S(2)}) collective-permute-start(bf16[256,512]{1,0:T(8,128)(2,1)S(1)} %get-tuple-element.56), channel_id=1, source_target_pairs={{0,128},{4,132},{8,136},{12,140},{16,144},{20,148},{24,152},{28,15... | collective-permute-start | bytes 786440 | tf_op jit(solution)/shard_map/ppermute | solution.py:452
  82.5 3.6 %collective-permute-start.21 = (bf16[3,256,128]{2,1,0:T(8,128)(2,1)S(1)}, bf16[3,256,128]{2,1,0:T(8,128)(2,1)S(1)}, u32[]{:S(2)}, u32[]{:S(2)}) collective-permute-start(bf16[3,256,128]{2,1,0:T(8,128)(2,1)S(1)} %get-tuple-element.61), channel_id=1, source_target_pairs={{0,56},{4,60},{8,0},{12,4},{16,8},{20,12},{24,16},{28,20},{32,24},... | collective-permute-start | bytes 589832 | tf_op jit(solution)/shard_map/ppermute | solution.py:462
  86.1 6.8 %collective-permute-done.22.above = bf16[2,256,128]{2,1,0:T(8,128)(2,1)S(1)} collective-permute-done((bf16[2,256,128]{2,1,0:T(8,128)(2,1)S(1)}, bf16[2,256,128]{2,1,0:T(8,128)(2,1)S(1)}, u32[]{:S(2)}, u32[]{:S(2)}) %collective-permute-start.22) | collective-permute-done | bytes 131104 | tf_op jit(solution)/shard_map/ppermute | solution.py:462
  93.2 3.8 %collective-permute-start.24 = (bf16[256,128]{1,0:T(8,128)(2,1)S(1)}, bf16[256,128]{1,0:T(8,128)(2,1)S(1)}, u32[]{:S(2)}, u32[]{:S(2)}) collective-permute-start(bf16[256,128]{1,0:T(8,128)(2,1)S(1)} %get-tuple-element.65), channel_id=1, source_target_pairs={{0,24},{4,28},{8,32},{12,36},{16,40},{20,44},{24,48},{28,52},{32,5... | collective-permute-start | bytes 196616 | tf_op jit(solution)/shard_map/ppermute | solution.py:462
  97.1 1.0 collective-permute-start.27
  98.1 2.0 %collective-permute-done.23.refs_1_ = bf16[256,128]{1,0:T(8,128)(2,1)S(1)} collective-permute-done((bf16[256,128]{1,0:T(8,128)(2,1)S(1)}, bf16[256,128]{1,0:T(8,128)(2,1)S(1)}, u32[]{:S(2)}, u32[]{:S(2)}) %collective-permute-start.23) | collective-permute-done | bytes 65568 | tf_op jit(solution)/shard_map/ppermute | solution.py:462
  100.1 1.8 %collective-permute-done.24.refs_2_ = bf16[256,128]{1,0:T(8,128)(2,1)S(1)} collective-permute-done((bf16[256,128]{1,0:T(8,128)(2,1)S(1)}, bf16[256,128]{1,0:T(8,128)(2,1)S(1)}, u32[]{:S(2)}, u32[]{:S(2)}) %collective-permute-start.24) | collective-permute-done | bytes 65568 | tf_op jit(solution)/shard_map/ppermute | solution.py:462
  101.9 0.9 rows.1.refs_0_.refs_4_
  103.0 1.9 %collective-permute-start.32 = (bf16[128,768]{1,0:T(8,128)(2,1)S(1)}, bf16[128,768]{1,0:T(8,128)(2,1)S(1)}, u32[]{:S(2)}, u32[]{:S(2)}) collective-permute-start(bf16[128,768]{1,0:T(8,128)(2,1)S(1)} %rows.1.refs_0_.refs_4_), channel_id=1, source_target_pairs={{0,64},{4,68},{8,72},{12,76},{16,80},{20,84},{24,88},{28,92},{32,9... | collective-permute-start | bytes 589832 | tf_op jit(solution)/shard_map/ppermute | solution.py:452
  104.9 2.1 %spread.1 = (f32[128,512]{1,0:T(8,128)S(1)}, f32[8,128]{1,0:T(8,128)S(1)}, bf16[144,512]{1,0:T(8,128)(2,1)S(1)}, bf16[144,512]{1,0:T(8,128)(2,1)S(1)}, bf16[144,512]{1,0:T(8,128)(2,1)S(1)}) custom-call(s32[8]{0:T(128)S(1)} %copy-done.7, bf16[128,768]{1,0:T(8,128)(2,1)S(1)} %rows.1.refs_0_.refs_4_, bf16[2048,768]{1,0:T(8,128)(2,1)S(1)} %copy-done.1, ...), custom_call_target="tpu_custom_call" | custom-call | flops 1000 | bytes 1000 | tf_op jit(solution)/shard_map/spread/pallas_call | solution.py:46
  107.0 1.7 %context.1 = bf16[256,512]{1,0:T(8,128)(2,1)} custom-call(s32[8]{0:T(128)S(1)} %copy-done.7, bf16[128,512]{1,0:T(8,128)(2,1)S(1)} %get-tuple-element.49.o0, bf16[256,512]{1,0:T(8,128)(2,1)S(1)} %collective-permute-done.18.refs_4_.o1, bf16[256,512]{1,0:T(8,128)(2,1)S(1)} %collective-permute-done.19.refs_5_.o2, f32[8,512]{1,0:T(8,128)S(1)} %delta.1.refs_12_.s0, ...), custom_call_target="tpu_custom_call" | custom-call | flops 1000 | bytes 1000 | tf_op jit(solution)/shard_map/context/pallas_call | solution.py:46
  108.7 8.8 %all-to-all-start.1 = ((bf16[32,8,512]{2,1,0:T(8,128)(2,1)}), bf16[32,8,512]{2,1,0:T(8,128)(2,1)S(1)}, u32[]{:S(2)}, u32[]{:S(2)}) async-start(bf16[32,8,512]{2,1,0:T(8,128)(2,1)} %bitcast.3), calls=%async_computation.1 | async-start | bytes 524288 | tf_op jit(solution)/shard_map/all_to_all | solution.py:477
  117.5 2.0 %weight.1 = (bf16[8,32,768]{2,1,0:T(8,128)(2,1)S(1)}, bf16[8,32,768]{2,1,0:T(8,128)(2,1)S(1)}) custom-call(s32[8]{0:T(128)S(1)} %copy-done.7, bf16[128,512]{1,0:T(8,128)(2,1)S(1)} %get-tuple-element.76.refs_0_, bf16[128,512]{1,0:T(8,128)(2,1)S(1)} %collective-permute-done.25.refs_6_.refs_1_, bf16[128,512]{1,0:T(8,128)(2,1)S(1)} %collective-permute-done.26.refs_7_.refs_2_, ...), custom_call_target="tpu_custom_call" | custom-call | flops 1000 | bytes 1000 | tf_op jit(solution)/shard_map/weight/pallas_call | solution.py:46
  119.6 8.8 %all-to-all-done.1 = bf16[32,8,512]{2,1,0:T(8,128)(2,1)S(1)} async-done(((bf16[32,8,512]{2,1,0:T(8,128)(2,1)}), bf16[32,8,512]{2,1,0:T(8,128)(2,1)S(1)}, u32[]{:S(2)}, u32[]{:S(2)}) %all-to-all-start.1) | async-done | bytes 262176 | tf_op jit(solution)/shard_map/all_to_all | solution.py:477
  128.5 2.0 %collective-permute-start.37 = (bf16[2,32,768]{2,1,0:T(8,128)(2,1)S(1)}, bf16[2,32,768]{2,1,0:T(8,128)(2,1)S(1)}, u32[]{:S(2)}, u32[]{:S(2)}) collective-permute-start(bf16[2,32,768]{2,1,0:T(8,128)(2,1)S(1)} %get-tuple-element.81), channel_id=1, source_target_pairs={{0,8},{4,12},{8,16},{12,20},{16,24},{20,28},{24,32},{28,36},{32,40... | collective-permute-start | bytes 294920 | tf_op jit(solution)/shard_map/ppermute | solution.py:462
  130.5 1.4 collective-permute-start.36
  132.3 1.8 %collective-permute-start.30 = (bf16[144,512]{1,0:T(8,128)(2,1)S(1)}, bf16[144,512]{1,0:T(8,128)(2,1)S(1)}, u32[]{:S(2)}, u32[]{:S(2)}) collective-permute-start(bf16[144,512]{1,0:T(8,128)(2,1)S(1)} %get-tuple-element.73), channel_id=1, source_target_pairs={{0,2},{1,3},{2,0},{3,1},{4,6},{5,7},{6,4},{7,5},{8,10},{9,11},{10,... | collective-permute-start | bytes 442376 | tf_op jit(solution)/shard_map/ppermute | solution.py:471
  135.0 0.9 collective-permute-start.31
  136.5 1.3 collective-permute-start.38
  137.8 1.0 collective-permute-done.29.r1
  138.8 1.6 %collective-permute-start.39 = (bf16[32,768]{1,0:T(8,128)(2,1)S(1)}, bf16[32,768]{1,0:T(8,128)(2,1)S(1)}, u32[]{:S(2)}, u32[]{:S(2)}) collective-permute-start(bf16[32,768]{1,0:T(8,128)(2,1)S(1)} %get-tuple-element.84), channel_id=1, source_target_pairs={{0,24},{4,28},{8,32},{12,36},{16,40},{20,44},{24,48},{28,52},{32,5... | collective-permute-start | bytes 147464 | tf_op jit(solution)/shard_map/ppermute | solution.py:462
  140.6 1.8 %collective-permute-done.31.r3 = bf16[144,512]{1,0:T(8,128)(2,1)S(1)} collective-permute-done((bf16[144,512]{1,0:T(8,128)(2,1)S(1)}, bf16[144,512]{1,0:T(8,128)(2,1)S(1)}, u32[]{:S(2)}, u32[]{:S(2)}) %collective-permute-start.31) | collective-permute-done | bytes 147488 | tf_op jit(solution)/shard_map/ppermute | solution.py:471
  143.3 0.9 place.1
  144.2 2.2 %collective-permute-done.39.refs_2_ = bf16[32,768]{1,0:T(8,128)(2,1)S(1)} collective-permute-done((bf16[32,768]{1,0:T(8,128)(2,1)S(1)}, bf16[32,768]{1,0:T(8,128)(2,1)S(1)}, u32[]{:S(2)}, u32[]{:S(2)}) %collective-permute-start.39) | collective-permute-done | bytes 49184 | tf_op jit(solution)/shard_map/ppermute | solution.py:462
  (81 shorter events, 10.8 us)
Async XLA Ops:
  0.6 21.7 %collective-permute-start.2 = (bf16[128,512]{1,0:T(8,128)(2,1)}, bf16[128,512]{1,0:T(8,128)(2,1)S(1)}, u32[]{:S(2)}, u32[]{:S(2)}) collective-permute-start(bf16[128,512]{1,0:T(8,128)(2,1)} %hid.1), channel_id=1, source_target_pairs={{0,3},{1,0},{2,1},{3,2},{4,7},{5,4},{6,5},{7,6},{8,11},{9,8},{10,9... | collective-permute-start | bytes 393224 | tf_op jit(solution)/shard_map/ppermute | solution.py:471
  3.0 19.4 %collective-permute-start.1 = (bf16[128,512]{1,0:T(8,128)(2,1)}, bf16[128,512]{1,0:T(8,128)(2,1)S(1)}, u32[]{:S(2)}, u32[]{:S(2)}) collective-permute-start(bf16[128,512]{1,0:T(8,128)(2,1)} %hid.1), channel_id=1, source_target_pairs={{0,2},{1,3},{2,0},{3,1},{4,6},{5,7},{6,4},{7,5},{8,10},{9,11},{10,... | collective-permute-start | bytes 393224 | tf_op jit(solution)/shard_map/ppermute | solution.py:471
  3.7 18.7 %collective-permute-start = (bf16[128,512]{1,0:T(8,128)(2,1)}, bf16[128,512]{1,0:T(8,128)(2,1)S(1)}, u32[]{:S(2)}, u32[]{:S(2)}) collective-permute-start(bf16[128,512]{1,0:T(8,128)(2,1)} %hid.1), channel_id=1, source_target_pairs={{0,1},{1,2},{2,3},{3,0},{4,5},{5,6},{6,7},{7,4},{8,9},{9,10},{10,1... | collective-permute-start | bytes 393224 | tf_op jit(solution)/shard_map/ppermute | solution.py:471
  5.5 0.9 copy-start.4
  7.8 46.6 %copy-start.7 = (s32[8]{0:T(128)S(1)}, s32[8]{0:T(128)}, u32[]{:S(2)}) copy-start(s32[8]{0:T(128)} %lengths.15) | copy-start | bytes 100
  9.5 34.4 %all-to-all-start = ((bf16[32,8,512]{2,1,0:T(8,128)(2,1)}), bf16[32,8,512]{2,1,0:T(8,128)(2,1)S(1)}, u32[]{:S(2)}, u32[]{:S(2)}) async-start(bf16[32,8,512]{2,1,0:T(8,128)(2,1)} %bitcast.1), calls=%async_computation | async-start | bytes 524288 | tf_op jit(solution)/shard_map/all_to_all | solution.py:477
  22.4 1.9 %copy-start = (bf16[2048,768]{1,0:T(8,128)(2,1)S(1)}, bf16[2048,768]{1,0:T(8,128)(2,1)}, u32[]{:S(2)}) copy-start(bf16[2048,768]{1,0:T(8,128)(2,1)} %refs_1_.1) | copy-start | bytes 9437188
  28.0 15.8 %collective-permute-start.4 = (bf16[512,128]{1,0:T(8,128)(2,1)S(1)}, bf16[512,128]{1,0:T(8,128)(2,1)S(1)}, u32[]{:S(2)}, u32[]{:S(2)}) collective-permute-start(bf16[512,128]{1,0:T(8,128)(2,1)S(1)} %get-tuple-element.45.refs_0_), channel_id=1, source_target_pairs={{128,0},{132,4},{136,8},{140,12},{144,16},{148,20},{152,24},{156,2... | collective-permute-start | bytes 393224 | tf_op jit(solution)/shard_map/ppermute | solution.py:452
  29.3 14.5 %collective-permute-start.3 = (bf16[512,128]{1,0:T(8,128)(2,1)S(1)}, bf16[512,128]{1,0:T(8,128)(2,1)S(1)}, u32[]{:S(2)}, u32[]{:S(2)}) collective-permute-start(bf16[512,128]{1,0:T(8,128)(2,1)S(1)} %get-tuple-element.45.refs_0_), channel_id=1, source_target_pairs={{64,0},{68,4},{72,8},{76,12},{80,16},{84,20},{88,24},{92,28},{96,3... | collective-permute-start | bytes 393224 | tf_op jit(solution)/shard_map/ppermute | solution.py:452
  30.6 8.1 %collective-permute-start.6 = (bf16[256,128]{1,0:T(8,128)(2,1)S(1)}, bf16[256,128]{1,0:T(8,128)(2,1)S(1)}, u32[]{:S(2)}, u32[]{:S(2)}) collective-permute-start(bf16[256,128]{1,0:T(8,128)(2,1)S(1)} %get-tuple-element.46.b0), channel_id=1, source_target_pairs={{0,40},{4,44},{8,48},{12,52},{16,56},{20,60},{24,0},{28,4},{32,8},... | collective-permute-start | bytes 196616 | tf_op jit(solution)/shard_map/ppermute | solution.py:462
  35.5 8.3 %collective-permute-start.5 = (bf16[256,128]{1,0:T(8,128)(2,1)S(1)}, bf16[256,128]{1,0:T(8,128)(2,1)S(1)}, u32[]{:S(2)}, u32[]{:S(2)}) collective-permute-start(bf16[256,128]{1,0:T(8,128)(2,1)S(1)} %get-tuple-element.46.b0), channel_id=1, source_target_pairs={{0,24},{4,28},{8,32},{12,36},{16,40},{20,44},{24,48},{28,52},{32,5... | collective-permute-start | bytes 196616 | tf_op jit(solution)/shard_map/ppermute | solution.py:462
  43.8 7.0 %collective-permute-start.7 = (bf16[3,256,128]{2,1,0:T(8,128)(2,1)S(1)}, bf16[3,256,128]{2,1,0:T(8,128)(2,1)S(1)}, u32[]{:S(2)}, u32[]{:S(2)}) collective-permute-start(bf16[3,256,128]{2,1,0:T(8,128)(2,1)S(1)} %get-tuple-element.47.refs_3_.refs_6_), channel_id=1, source_target_pairs={{0,8},{4,12},{8,16},{12,20},{16,24},{20,28},{24,32},{28,36},{32,40... | collective-permute-start | bytes 589832 | tf_op jit(solution)/shard_map/ppermute | solution.py:462
  43.9 7.4 %collective-permute-start.12 = (bf16[256,512]{1,0:T(8,128)(2,1)S(1)}, bf16[256,512]{1,0:T(8,128)(2,1)S(1)}, u32[]{:S(2)}, u32[]{:S(2)}) collective-permute-start(bf16[256,512]{1,0:T(8,128)(2,1)S(1)} %bitcast.5), channel_id=1, source_target_pairs={{0,4},{4,0},{8,12},{12,8},{16,20},{20,16},{24,28},{28,24},{32,36},... | collective-permute-start | bytes 786440 | tf_op jit(solution)/shard_map/ppermute | solution.py:467
  44.0 6.8 %collective-permute-start.8 = (bf16[2,256,128]{2,1,0:T(8,128)(2,1)S(1)}, bf16[2,256,128]{2,1,0:T(8,128)(2,1)S(1)}, u32[]{:S(2)}, u32[]{:S(2)}) collective-permute-start(bf16[2,256,128]{2,1,0:T(8,128)(2,1)S(1)} %get-tuple-element.48), channel_id=1, source_target_pairs={{0,56},{4,60},{8,0},{12,4},{16,8},{20,12},{24,16},{28,20},{32,24},... | collective-permute-start | bytes 393224 | tf_op jit(solution)/shard_map/ppermute | solution.py:462
  47.2 7.2 %collective-permute-start.9 = (bf16[3,256,128]{2,1,0:T(8,128)(2,1)S(1)}, bf16[3,256,128]{2,1,0:T(8,128)(2,1)S(1)}, u32[]{:S(2)}, u32[]{:S(2)}) collective-permute-start(bf16[3,256,128]{2,1,0:T(8,128)(2,1)S(1)} %get-tuple-element.47.refs_3_.refs_6_), channel_id=1, source_target_pairs={{0,4},{4,0},{8,12},{12,8},{16,20},{20,16},{24,28},{28,24},{32,36},... | collective-permute-start | bytes 589832 | tf_op jit(solution)/shard_map/ppermute | solution.py:467
  50.8 3.6 %collective-permute-start.10 = (bf16[3,256,128]{2,1,0:T(8,128)(2,1)S(1)}, bf16[3,256,128]{2,1,0:T(8,128)(2,1)S(1)}, u32[]{:S(2)}, u32[]{:S(2)}) collective-permute-start(bf16[3,256,128]{2,1,0:T(8,128)(2,1)S(1)} %collective-permute-done.7.refs_4_.refs_7_), channel_id=1, source_target_pairs={{0,4},{4,0},{8,12},{12,8},{16,20},{20,16},{24,28},{28,24},{32,36},... | collective-permute-start | bytes 589832 | tf_op jit(solution)/shard_map/ppermute | solution.py:467
  50.8 3.6 %collective-permute-start.11 = (bf16[2,256,128]{2,1,0:T(8,128)(2,1)S(1)}, bf16[2,256,128]{2,1,0:T(8,128)(2,1)S(1)}, u32[]{:S(2)}, u32[]{:S(2)}) collective-permute-start(bf16[2,256,128]{2,1,0:T(8,128)(2,1)S(1)} %collective-permute-done.8.refs_5_.refs_8_), channel_id=1, source_target_pairs={{0,4},{4,0},{8,12},{12,8},{16,20},{20,16},{24,28},{28,24},{32,36},... | collective-permute-start | bytes 393224 | tf_op jit(solution)/shard_map/ppermute | solution.py:467
  51.6 9.3 %collective-permute-start.14 = (bf16[512,128]{1,0:T(8,128)(2,1)S(1)}, bf16[512,128]{1,0:T(8,128)(2,1)S(1)}, u32[]{:S(2)}, u32[]{:S(2)}) collective-permute-start(bf16[512,128]{1,0:T(8,128)(2,1)S(1)} %grad_home.1.d0.refs_3_), channel_id=1, source_target_pairs={{128,0},{132,4},{136,8},{140,12},{144,16},{148,20},{152,24},{156,2... | collective-permute-start | bytes 393224 | tf_op jit(solution)/shard_map/ppermute | solution.py:452
  52.9 8.0 %collective-permute-start.13 = (bf16[512,128]{1,0:T(8,128)(2,1)S(1)}, bf16[512,128]{1,0:T(8,128)(2,1)S(1)}, u32[]{:S(2)}, u32[]{:S(2)}) collective-permute-start(bf16[512,128]{1,0:T(8,128)(2,1)S(1)} %grad_home.1.d0.refs_3_), channel_id=1, source_target_pairs={{64,0},{68,4},{72,8},{76,12},{80,16},{84,20},{88,24},{92,28},{96,3... | collective-permute-start | bytes 393224 | tf_op jit(solution)/shard_map/ppermute | solution.py:452
  59.4 45.5 %copy-start.1 = (bf16[2048,768]{1,0:T(8,128)(2,1)S(1)}, bf16[2048,768]{1,0:T(8,128)(2,1)}, u32[]{:S(2)}) copy-start(bf16[2048,768]{1,0:T(8,128)(2,1)} %refs_1_.1) | copy-start | bytes 9437188
  59.4 45.5 %copy-start.3 = (bf16[128,512]{1,0:T(8,128)(2,1)S(1)}, bf16[128,512]{1,0:T(8,128)(2,1)}, u32[]{:S(2)}) copy-start(bf16[128,512]{1,0:T(8,128)(2,1)} %hid.1) | copy-start | bytes 393220
  61.1 8.0 %collective-permute-start.17 = (f32[8,512]{1,0:T(8,128)S(1)}, f32[8,512]{1,0:T(8,128)S(1)}, u32[]{:S(2)}, u32[]{:S(2)}) collective-permute-start(f32[8,512]{1,0:T(8,128)S(1)} %delta.1.refs_12_.s0), channel_id=1, source_target_pairs={{0,64},{4,68},{8,72},{12,76},{16,80},{20,84},{24,88},{28,92},{32,9... | collective-permute-start | bytes 49160 | tf_op jit(solution)/shard_map/ppermute | solution.py:452
  65.8 5.2 %collective-permute-start.16 = (f32[8,512]{1,0:T(8,128)S(1)}, f32[8,512]{1,0:T(8,128)S(1)}, u32[]{:S(2)}, u32[]{:S(2)}) collective-permute-start(f32[8,512]{1,0:T(8,128)S(1)} %delta.1.refs_12_.s0), channel_id=1, source_target_pairs={{0,128},{4,132},{8,136},{12,140},{16,144},{20,148},{24,152},{28,15... | collective-permute-start | bytes 49160 | tf_op jit(solution)/shard_map/ppermute | solution.py:452
  66.6 4.5 %collective-permute-start.15 = (f32[8,512]{1,0:T(8,128)S(1)}, f32[8,512]{1,0:T(8,128)S(1)}, u32[]{:S(2)}, u32[]{:S(2)}) collective-permute-start(f32[8,512]{1,0:T(8,128)S(1)} %delta.1.refs_12_.s0), channel_id=1, source_target_pairs={{0,192},{4,196},{8,200},{12,204},{16,208},{20,212},{24,216},{28,22... | collective-permute-start | bytes 49160 | tf_op jit(solution)/shard_map/ppermute | solution.py:452
  77.3 5.1 %collective-permute-start.20 = (bf16[8,256,128]{2,1,0:T(8,128)(2,1)S(1)}, bf16[8,256,128]{2,1,0:T(8,128)(2,1)S(1)}, u32[]{:S(2)}, u32[]{:S(2)}) collective-permute-start(bf16[8,256,128]{2,1,0:T(8,128)(2,1)S(1)} %get-tuple-element.59), channel_id=1, source_target_pairs={{0,4},{4,0},{8,12},{12,8},{16,20},{20,16},{24,28},{28,24},{32,36},... | collective-permute-start | bytes 1572872 | tf_op jit(solution)/shard_map/ppermute | solution.py:467
  77.4 19.7 %collective-permute-start.18 = (bf16[256,512]{1,0:T(8,128)(2,1)S(1)}, bf16[256,512]{1,0:T(8,128)(2,1)S(1)}, u32[]{:S(2)}, u32[]{:S(2)}) collective-permute-start(bf16[256,512]{1,0:T(8,128)(2,1)S(1)} %get-tuple-element.55), channel_id=1, source_target_pairs={{0,64},{4,68},{8,72},{12,76},{16,80},{20,84},{24,88},{28,92},{32,9... | collective-permute-start | bytes 786440 | tf_op jit(solution)/shard_map/ppermute | solution.py:452
  78.7 18.4 %collective-permute-start.19 = (bf16[256,512]{1,0:T(8,128)(2,1)S(1)}, bf16[256,512]{1,0:T(8,128)(2,1)S(1)}, u32[]{:S(2)}, u32[]{:S(2)}) collective-permute-start(bf16[256,512]{1,0:T(8,128)(2,1)S(1)} %get-tuple-element.56), channel_id=1, source_target_pairs={{0,128},{4,132},{8,136},{12,140},{16,144},{20,148},{24,152},{28,15... | collective-permute-start | bytes 786440 | tf_op jit(solution)/shard_map/ppermute | solution.py:452
  82.5 10.4 %collective-permute-start.21 = (bf16[3,256,128]{2,1,0:T(8,128)(2,1)S(1)}, bf16[3,256,128]{2,1,0:T(8,128)(2,1)S(1)}, u32[]{:S(2)}, u32[]{:S(2)}) collective-permute-start(bf16[3,256,128]{2,1,0:T(8,128)(2,1)S(1)} %get-tuple-element.61), channel_id=1, source_target_pairs={{0,56},{4,60},{8,0},{12,4},{16,8},{20,12},{24,16},{28,20},{32,24},... | collective-permute-start | bytes 589832 | tf_op jit(solution)/shard_map/ppermute | solution.py:462
  86.0 6.8 %collective-permute-start.22 = (bf16[2,256,128]{2,1,0:T(8,128)(2,1)S(1)}, bf16[2,256,128]{2,1,0:T(8,128)(2,1)S(1)}, u32[]{:S(2)}, u32[]{:S(2)}) collective-permute-start(bf16[2,256,128]{2,1,0:T(8,128)(2,1)S(1)} %get-tuple-element.62), channel_id=1, source_target_pairs={{0,8},{4,12},{8,16},{12,20},{16,24},{20,28},{24,32},{28,36},{32,40... | collective-permute-start | bytes 393224 | tf_op jit(solution)/shard_map/ppermute | solution.py:462
  86.0 16.9 %collective-permute-start.25 = (bf16[128,512]{1,0:T(8,128)(2,1)S(1)}, bf16[128,512]{1,0:T(8,128)(2,1)S(1)}, u32[]{:S(2)}, u32[]{:S(2)}) collective-permute-start(bf16[128,512]{1,0:T(8,128)(2,1)S(1)} %get-tuple-element.67), channel_id=1, source_target_pairs={{0,64},{4,68},{8,72},{12,76},{16,80},{20,84},{24,88},{28,92},{32,9... | collective-permute-start | bytes 393224 | tf_op jit(solution)/shard_map/ppermute | solution.py:452
  92.9 7.1 %collective-permute-start.23 = (bf16[256,128]{1,0:T(8,128)(2,1)S(1)}, bf16[256,128]{1,0:T(8,128)(2,1)S(1)}, u32[]{:S(2)}, u32[]{:S(2)}) collective-permute-start(bf16[256,128]{1,0:T(8,128)(2,1)S(1)} %get-tuple-element.64), channel_id=1, source_target_pairs={{0,40},{4,44},{8,48},{12,52},{16,56},{20,60},{24,0},{28,4},{32,8},... | collective-permute-start | bytes 196616 | tf_op jit(solution)/shard_map/ppermute | solution.py:462
  93.2 8.6 %collective-permute-start.24 = (bf16[256,128]{1,0:T(8,128)(2,1)S(1)}, bf16[256,128]{1,0:T(8,128)(2,1)S(1)}, u32[]{:S(2)}, u32[]{:S(2)}) collective-permute-start(bf16[256,128]{1,0:T(8,128)(2,1)S(1)} %get-tuple-element.65), channel_id=1, source_target_pairs={{0,24},{4,28},{8,32},{12,36},{16,40},{20,44},{24,48},{28,52},{32,5... | collective-permute-start | bytes 196616 | tf_op jit(solution)/shard_map/ppermute | solution.py:462
  97.0 7.8 %collective-permute-start.26 = (bf16[128,512]{1,0:T(8,128)(2,1)S(1)}, bf16[128,512]{1,0:T(8,128)(2,1)S(1)}, u32[]{:S(2)}, u32[]{:S(2)}) collective-permute-start(bf16[128,512]{1,0:T(8,128)(2,1)S(1)} %get-tuple-element.68), channel_id=1, source_target_pairs={{0,128},{4,132},{8,136},{12,140},{16,144},{20,148},{24,152},{28,15... | collective-permute-start | bytes 393224 | tf_op jit(solution)/shard_map/ppermute | solution.py:452
  97.1 7.8 %collective-permute-start.27 = (bf16[128,512]{1,0:T(8,128)(2,1)S(1)}, bf16[128,512]{1,0:T(8,128)(2,1)S(1)}, u32[]{:S(2)}, u32[]{:S(2)}) collective-permute-start(bf16[128,512]{1,0:T(8,128)(2,1)S(1)} %get-tuple-element.69), channel_id=1, source_target_pairs={{0,192},{4,196},{8,200},{12,204},{16,208},{20,212},{24,216},{28,22... | collective-permute-start | bytes 393224 | tf_op jit(solution)/shard_map/ppermute | solution.py:452
  102.8 14.7 %collective-permute-start.34 = (bf16[128,768]{1,0:T(8,128)(2,1)S(1)}, bf16[128,768]{1,0:T(8,128)(2,1)S(1)}, u32[]{:S(2)}, u32[]{:S(2)}) collective-permute-start(bf16[128,768]{1,0:T(8,128)(2,1)S(1)} %rows.1.refs_0_.refs_4_), channel_id=1, source_target_pairs={{0,192},{4,196},{8,200},{12,204},{16,208},{20,212},{24,216},{28,22... | collective-permute-start | bytes 589832 | tf_op jit(solution)/shard_map/ppermute | solution.py:452
  102.9 14.6 %collective-permute-start.33 = (bf16[128,768]{1,0:T(8,128)(2,1)S(1)}, bf16[128,768]{1,0:T(8,128)(2,1)S(1)}, u32[]{:S(2)}, u32[]{:S(2)}) collective-permute-start(bf16[128,768]{1,0:T(8,128)(2,1)S(1)} %rows.1.refs_0_.refs_4_), channel_id=1, source_target_pairs={{0,128},{4,132},{8,136},{12,140},{16,144},{20,148},{24,152},{28,15... | collective-permute-start | bytes 589832 | tf_op jit(solution)/shard_map/ppermute | solution.py:452
  103.0 14.5 %collective-permute-start.32 = (bf16[128,768]{1,0:T(8,128)(2,1)S(1)}, bf16[128,768]{1,0:T(8,128)(2,1)S(1)}, u32[]{:S(2)}, u32[]{:S(2)}) collective-permute-start(bf16[128,768]{1,0:T(8,128)(2,1)S(1)} %rows.1.refs_0_.refs_4_), channel_id=1, source_target_pairs={{0,64},{4,68},{8,72},{12,76},{16,80},{20,84},{24,88},{28,92},{32,9... | collective-permute-start | bytes 589832 | tf_op jit(solution)/shard_map/ppermute | solution.py:452
  107.0 1.7 %copy-start.9 = (bf16[144,512]{1,0:T(8,128)(2,1)}, bf16[144,512]{1,0:T(8,128)(2,1)S(1)}, u32[]{:S(2)}) copy-start(bf16[144,512]{1,0:T(8,128)(2,1)S(1)} %get-tuple-element.72) | copy-start | bytes 442372
  108.7 19.8 %all-to-all-start.1 = ((bf16[32,8,512]{2,1,0:T(8,128)(2,1)}), bf16[32,8,512]{2,1,0:T(8,128)(2,1)S(1)}, u32[]{:S(2)}, u32[]{:S(2)}) async-start(bf16[32,8,512]{2,1,0:T(8,128)(2,1)} %bitcast.3), calls=%async_computation.1 | async-start | bytes 524288 | tf_op jit(solution)/shard_map/all_to_all | solution.py:477
  119.5 8.9 %collective-permute-start.35 = (bf16[8,32,768]{2,1,0:T(8,128)(2,1)S(1)}, bf16[8,32,768]{2,1,0:T(8,128)(2,1)S(1)}, u32[]{:S(2)}, u32[]{:S(2)}) collective-permute-start(bf16[8,32,768]{2,1,0:T(8,128)(2,1)S(1)} %get-tuple-element.78), channel_id=1, source_target_pairs={{0,4},{4,0},{8,12},{12,8},{16,20},{20,16},{24,28},{28,24},{32,36},... | collective-permute-start | bytes 1179656 | tf_op jit(solution)/shard_map/ppermute | solution.py:467
  128.4 14.9 %collective-permute-start.28 = (bf16[256,512]{1,0:T(8,128)(2,1)S(1)}, bf16[256,512]{1,0:T(8,128)(2,1)S(1)}, u32[]{:S(2)}, u32[]{:S(2)}) collective-permute-start(bf16[256,512]{1,0:T(8,128)(2,1)S(1)} %bitcast.7), channel_id=1, source_target_pairs={{0,4},{4,0},{8,12},{12,8},{16,20},{20,16},{24,28},{28,24},{32,36},... | collective-permute-start | bytes 786440 | tf_op jit(solution)/shard_map/ppermute | solution.py:467
  128.5 6.5 %collective-permute-start.37 = (bf16[2,32,768]{2,1,0:T(8,128)(2,1)S(1)}, bf16[2,32,768]{2,1,0:T(8,128)(2,1)S(1)}, u32[]{:S(2)}, u32[]{:S(2)}) collective-permute-start(bf16[2,32,768]{2,1,0:T(8,128)(2,1)S(1)} %get-tuple-element.81), channel_id=1, source_target_pairs={{0,8},{4,12},{8,16},{12,20},{16,24},{20,28},{24,32},{28,36},{32,40... | collective-permute-start | bytes 294920 | tf_op jit(solution)/shard_map/ppermute | solution.py:462
  130.5 6.0 %collective-permute-start.36 = (bf16[3,32,768]{2,1,0:T(8,128)(2,1)S(1)}, bf16[3,32,768]{2,1,0:T(8,128)(2,1)S(1)}, u32[]{:S(2)}, u32[]{:S(2)}) collective-permute-start(bf16[3,32,768]{2,1,0:T(8,128)(2,1)S(1)} %get-tuple-element.80), channel_id=1, source_target_pairs={{0,56},{4,60},{8,0},{12,4},{16,8},{20,12},{24,16},{28,20},{32,24},... | collective-permute-start | bytes 442376 | tf_op jit(solution)/shard_map/ppermute | solution.py:462
  131.9 6.9 %collective-permute-start.29 = (bf16[144,512]{1,0:T(8,128)(2,1)}, bf16[144,512]{1,0:T(8,128)(2,1)S(1)}, u32[]{:S(2)}, u32[]{:S(2)}) collective-permute-start(bf16[144,512]{1,0:T(8,128)(2,1)} %copy-done.9), channel_id=1, source_target_pairs={{0,1},{1,2},{2,3},{3,0},{4,5},{5,6},{6,7},{7,4},{8,9},{9,10},{10,1... | collective-permute-start | bytes 442376 | tf_op jit(solution)/shard_map/ppermute | solution.py:471
  132.3 8.3 %collective-permute-start.30 = (bf16[144,512]{1,0:T(8,128)(2,1)S(1)}, bf16[144,512]{1,0:T(8,128)(2,1)S(1)}, u32[]{:S(2)}, u32[]{:S(2)}) collective-permute-start(bf16[144,512]{1,0:T(8,128)(2,1)S(1)} %get-tuple-element.73), channel_id=1, source_target_pairs={{0,2},{1,3},{2,0},{3,1},{4,6},{5,7},{6,4},{7,5},{8,10},{9,11},{10,... | collective-permute-start | bytes 442376 | tf_op jit(solution)/shard_map/ppermute | solution.py:471
  135.0 7.4 %collective-permute-start.31 = (bf16[144,512]{1,0:T(8,128)(2,1)S(1)}, bf16[144,512]{1,0:T(8,128)(2,1)S(1)}, u32[]{:S(2)}, u32[]{:S(2)}) collective-permute-start(bf16[144,512]{1,0:T(8,128)(2,1)S(1)} %get-tuple-element.74), channel_id=1, source_target_pairs={{0,3},{1,0},{2,1},{3,2},{4,7},{5,4},{6,5},{7,6},{8,11},{9,8},{10,9... | collective-permute-start | bytes 442376 | tf_op jit(solution)/shard_map/ppermute | solution.py:471
  136.5 7.7 %collective-permute-start.38 = (bf16[32,768]{1,0:T(8,128)(2,1)S(1)}, bf16[32,768]{1,0:T(8,128)(2,1)S(1)}, u32[]{:S(2)}, u32[]{:S(2)}) collective-permute-start(bf16[32,768]{1,0:T(8,128)(2,1)S(1)} %get-tuple-element.83), channel_id=1, source_target_pairs={{0,40},{4,44},{8,48},{12,52},{16,56},{20,60},{24,0},{28,4},{32,8},... | collective-permute-start | bytes 147464 | tf_op jit(solution)/shard_map/ppermute | solution.py:462
  138.8 7.6 %collective-permute-start.39 = (bf16[32,768]{1,0:T(8,128)(2,1)S(1)}, bf16[32,768]{1,0:T(8,128)(2,1)S(1)}, u32[]{:S(2)}, u32[]{:S(2)}) collective-permute-start(bf16[32,768]{1,0:T(8,128)(2,1)S(1)} %get-tuple-element.84), channel_id=1, source_target_pairs={{0,24},{4,28},{8,32},{12,36},{16,40},{20,44},{24,48},{28,52},{32,5... | collective-permute-start | bytes 147464 | tf_op jit(solution)/shard_map/ppermute | solution.py:462
  (4 other events, 3.0 us)
